TPU v7x, 512 devices: a whole 4x8x8 slice. The times are simulated.
512 devices in a mesh: patch: 64 (over z, y_hi, core), head: 8 (over y_lo, x).
Axes of the slice: x: 4, y: 8 (y_hi: 4, y_lo: 2; y = y_hi * 2 + y_lo), z: 8, core: 2. Of those that a mesh axis runs over, the one named last changes fastest.
Arguments:
- fresh_query: bfloat16 [6144, 4096], P(('patch', 'head')), may hold values from -128 to 128
- fresh_key: bfloat16 [6144, 4096], P(('patch', 'head')), may hold values from -6 to 6
- fresh_value: bfloat16 [6144, 4096], P(('patch', 'head')), may hold values from -6 to 6
- stale_key: bfloat16 [6144, 4096], P('patch', 'head'), may hold values from -4 to 4
- stale_value: bfloat16 [6144, 4096], P('patch', 'head'), may hold values from -6 to 6
- lengths: int32 [64], replicated, may hold values from 1 to 96, 4608 in all
- hidden: bfloat16 [6144, 3072], P(('patch', 'head')), may hold values from -4 to 4
- gate_scale: float32 [3072], replicated, may hold values from 0.1 to 1.9
- out_weight: bfloat16 [4096, 3072], P('head'), may hold values from -0.09375 to 0.09375
Outputs:
- mixed: bfloat16 [6144, 3072], P(('patch', 'head'))
Inputs may be any that keep to these rules, and one draw needn't show every extreme that they name: Slot j of patch p is live when j < lengths[p]; some patch is full in every draw; the lengths sum to 4608.
All inputs are finite; a program needn't handle non-finite values.
Results may differ from a plain program's by a relative error of at most 0.013.
Values may be sent and summed in bfloat16 or wider, within the bound.
No kernel may reach another device: no remote copies, remote signals or barrier semaphores. Data moves between devices by JAX's collectives and lax.ppermute only.
A program may use at most 64 MiB of HBM per device.

v0:
```python
import jax
import jax.numpy as jnp
from jax import lax
from jax.sharding import PartitionSpec as P

HD = 128


negative_big = -1e30


def absorb(carry, scores, live, values_here):
    run_max, denominator, accum = carry
    masked = jnp.where(live[None, None, :], scores, negative_big)
    new_max = jnp.maximum(run_max, jnp.max(masked, axis=-1))
    factor = jnp.exp(run_max - new_max)
    weights = jnp.where(live[None, None, :], jnp.exp(scores - new_max[:, :, None]), 0.0)
    denominator = denominator * factor + jnp.sum(weights, axis=-1)
    update = jnp.einsum(
        "hij,jhd->hid",
        weights.astype(jnp.bfloat16),
        values_here,
        preferred_element_type=jnp.float32,
    )
    accum = accum * factor[:, :, None] + update
    return (new_max, denominator, accum)


def local(
    fresh_query,
    fresh_key,
    fresh_value,
    stale_key,
    stale_value,
    lengths,
    hidden,
    gate_scale,
    out_weight,
):
    npatch = lax.axis_size("patch")
    own_patch = lax.axis_index("patch")
    own_head = lax.axis_index("head")
    queries, keys_now, values_now = (
        lax.all_to_all(fresh_query, "head", split_axis=1, concat_axis=0, tiled=True),
        lax.all_to_all(fresh_key, "head", split_axis=1, concat_axis=0, tiled=True),
        lax.all_to_all(fresh_value, "head", split_axis=1, concat_axis=0, tiled=True),
    )
    capacity = queries.shape[0]
    heads_here = queries.shape[1] // HD
    score_scale = HD ** (-0.5)
    query_three = queries.reshape(capacity, heads_here, HD)
    patch_ids = jnp.arange(npatch, dtype=jnp.int32)
    own_length = jnp.sum(jnp.where(patch_ids == own_patch, lengths, 0))
    slot_ids = jnp.arange(capacity, dtype=jnp.int32)
    empty = (
        jnp.full((heads_here, capacity), negative_big, jnp.float32),
        jnp.zeros((heads_here, capacity), jnp.float32),
        jnp.zeros((heads_here, capacity, HD), jnp.float32),
    )
    key_three = keys_now.reshape(capacity, heads_here, HD)
    value_three = values_now.reshape(capacity, heads_here, HD)
    scores = (
        jnp.einsum("ihd,jhd->hij", query_three, key_three, preferred_element_type=jnp.float32)
        * score_scale
    )
    carry = absorb(empty, scores, slot_ids < own_length, value_three)
    remote_carry = carry
    key_rows = lax.all_gather(stale_key, "patch", axis=0, tiled=True)
    value_rows = lax.all_gather(stale_value, "patch", axis=0, tiled=True)
    row_count = key_rows.shape[0]
    blocks = row_count // capacity
    group = max((width for width in range(1, 9) if blocks % width == 0))
    span = group * capacity
    steps_count = blocks // group
    key_blocks = key_rows.reshape(steps_count, span, heads_here, HD)
    value_blocks = value_rows.reshape(steps_count, span, heads_here, HD)
    block_starts = jnp.arange(steps_count, dtype=jnp.int32) * span

    def one_block(state, block_item):
        key_block, value_block, block_start = block_item
        row_ids = block_start + jnp.arange(span, dtype=jnp.int32)
        row_patch = row_ids // capacity
        row_slot = row_ids % capacity
        patch_length = jnp.sum(
            jnp.where(row_patch[:, None] == patch_ids[None, :], lengths[None, :], 0), axis=1
        )
        live = (row_slot < patch_length) & (row_patch != own_patch)
        scores = (
            jnp.einsum("ihd,jhd->hij", query_three, key_block, preferred_element_type=jnp.float32)
            * score_scale
        )
        return (absorb(state, scores, live, value_block), None)

    remote_carry, _ = lax.scan(one_block, remote_carry, (key_blocks, value_blocks, block_starts))
    carry = remote_carry
    run_max, denominator, accum = carry
    attended = jnp.transpose(accum / denominator[:, :, None], (1, 0, 2))
    attended = attended.reshape(capacity, heads_here * HD).astype(jnp.bfloat16)
    own_rows = hidden.shape[0]
    projected = lax.psum_scatter(
        jnp.dot(attended, out_weight, preferred_element_type=jnp.float32).astype(jnp.bfloat16),
        "head",
        scatter_dimension=0,
        tiled=True,
    ).astype(jnp.float32)
    my_slots = own_head * own_rows + jnp.arange(own_rows, dtype=jnp.int32)
    query_live = my_slots < own_length
    residual = hidden.astype(jnp.float32)
    mixed = jnp.where(query_live[:, None], residual + gate_scale[None, :] * projected, residual)
    return mixed.astype(jnp.bfloat16)


def solution(mesh):
    in_specs = (
        P(("patch", "head"), None),
        P(("patch", "head"), None),
        P(("patch", "head"), None),
        P("patch", "head"),
        P("patch", "head"),
        P(),
        P(("patch", "head"), None),
        P(),
        P("head", None),
    )
    out_specs = P(("patch", "head"), None)
    return jax.shard_map(local, mesh=mesh, in_specs=in_specs, out_specs=out_specs, check_vma=False)
```

profile of v0, /device:TPU:6, one launch (start us, length us, event | category | flops | bytes accessed | tf_op | source)
XLA Modules:
  0.0 305.5 jit_solution(14392446215041637386)
XLA Ops:
  6.5 0.7 all-gather.3.cloned.1.call-update
  8.0 0.9 copy.58
  9.7 9.1 %all-to-all-start = ((bf16[12,8,512]{2,0,1:T(8,128)(2,1)}), bf16[12,8,512]{2,0,1:T(8,128)(2,1)S(1)}, u32[]{:S(2)}, u32[]{:S(2)}) async-start(bf16[12,8,512]{2,0,1:T(8,128)(2,1)} %copy.37), calls=%async_computation | async-start | bytes 262144 | tf_op jit(solution)/shard_map/all_to_all | solution.py:44
  19.6 3.7 %all-to-all-done = bf16[12,8,512]{2,0,1:T(8,128)(2,1)S(1)} async-done(((bf16[12,8,512]{2,0,1:T(8,128)(2,1)}), bf16[12,8,512]{2,0,1:T(8,128)(2,1)S(1)}, u32[]{:S(2)}, u32[]{:S(2)}) %all-to-all-start) | async-done | bytes 98336 | tf_op jit(solution)/shard_map/all_to_all | solution.py:44
  23.3 5.4 %all-to-all-start.1 = ((bf16[12,8,512]{2,0,1:T(8,128)(2,1)}), bf16[12,8,512]{2,0,1:T(8,128)(2,1)S(1)}, u32[]{:S(2)}, u32[]{:S(2)}) async-start(bf16[12,8,512]{2,0,1:T(8,128)(2,1)} %copy.38), calls=%async_computation.1 | async-start | bytes 262144 | tf_op jit(solution)/shard_map/all_to_all | solution.py:45
  29.5 1.3 dynamic-slice.4
  32.1 1.1 all-to-all-done.1
  33.2 5.4 %all-to-all-start.2 = ((bf16[12,8,512]{2,0,1:T(8,128)(2,1)}), bf16[12,8,512]{2,0,1:T(8,128)(2,1)S(1)}, u32[]{:S(2)}, u32[]{:S(2)}) async-start(bf16[12,8,512]{2,0,1:T(8,128)(2,1)} %copy.41), calls=%async_computation.2 | async-start | bytes 262144 | tf_op jit(solution)/shard_map/all_to_all | solution.py:46
  40.0 1.5 copy.39
  41.6 1.5 all-to-all-done.2
  43.8 1.1 select_reduce_fusion.2
  45.0 1.2 convolution_add_fusion.1
  46.2 64.0 %all-gather.3.cloned.1.call-done = bf16[6144,512]{1,0:T(8,128)(2,1)} async-done(((bf16[96,512]{1,0:T(8,128)(2,1)}), bf16[6144,512]{1,0:T(8,128)(2,1)}) %all-gather.3.cloned.1.call-update) | async-done | bytes 6291472 | tf_op jit(solution)/shard_map/all_gather | solution.py:68
  110.2 9.7 %reshape.92 = bf16[8,768,4,128]{3,2,1,0:T(4,128)(2,1)} reshape(bf16[6144,512]{1,0:T(8,128)(2,1)} %all-gather.3.cloned.1.call-done) | data formatting | bytes 12582912 | tf_op jit(solution)/shard_map/reshape | solution.py:75
  119.9 84.6 %all-gather.5.cloned.1.call-done = bf16[6144,512]{1,0:T(8,128)(2,1)} async-done(((bf16[96,512]{1,0:T(8,128)(2,1)}), bf16[6144,512]{1,0:T(8,128)(2,1)}) %all-gather.5.cloned.1.call-update) | async-done | bytes 6291472 | tf_op jit(solution)/shard_map/all_gather | solution.py:69
  204.5 9.8 %reshape.93 = bf16[8,768,4,128]{3,2,1,0:T(4,128)(2,1)} reshape(bf16[6144,512]{1,0:T(8,128)(2,1)} %all-gather.5.cloned.1.call-done) | data formatting | bytes 12582912 | tf_op jit(solution)/shard_map/reshape | solution.py:76
  214.2 42.5 %while.17 = (s32[]{:T(128)}, f32[4,96]{1,0:T(4,128)S(1)}, f32[4,96]{1,0:T(4,128)S(1)}, f32[4,96,128]{2,1,0:T(8,128)S(1)}, s32[8]{0:T(128)S(1)}, /*index=5*/s32[6...) while((s32[]{:T(128)}, f32[4,96]{1,0:T(4,128)S(1)}, ...), condition=%wide.region_7.8_spmd.clone, body=%wide.region_3.7_spmd.clone.sunk | while | flops 153914112 | bytes 8789393 | solution.py:94
  216.3 1.9 constant_dynamic-slice_fusion.3
  221.6 1.9 constant_dynamic-slice_fusion.3
  226.9 1.9 constant_dynamic-slice_fusion.3
  232.2 1.9 constant_dynamic-slice_fusion.3
  237.5 1.9 constant_dynamic-slice_fusion.3
  242.8 1.9 constant_dynamic-slice_fusion.3
  248.1 1.9 constant_dynamic-slice_fusion.3
  253.4 1.9 constant_dynamic-slice_fusion.3
  256.7 1.5 convolution_convert_fusion
  258.2 20.8 %fusion.2 = bf16[16,3072]{1,0:T(8,128)(2,1)S(1)} fusion(bf16[96,3072]{1,0:T(8,128)(2,1)} %convolution_convert_fusion), kind=kCustom, calls=%all-reduce-scatter | all-reduce-scatter fusion | flops 393217 | bytes 690176
  279.0 6.4 %collective-permute-start = (bf16[16,3072]{1,0:T(8,128)(2,1)S(1)}, bf16[16,3072]{1,0:T(8,128)(2,1)}, u32[]{:S(2)}, u32[]{:S(2)}) collective-permute-start(bf16[16,3072]{1,0:T(8,128)(2,1)S(1)} %fusion.2), channel_id=1, source_target_pairs={{0,1},{1,2},{2,3},{3,4},{4,5},{5,6},{6,7},{8,9},{9,10},{10,11},{11... | collective-permute-start | bytes 294920
  285.5 1.9 collective-permute-start.1
  288.1 5.4 %collective-permute-done.1 = bf16[12,3072]{1,0:T(8,128)(2,1)S(1)} collective-permute-done((bf16[12,3072]{1,0:T(8,128)(2,1)S(1)}, bf16[12,3072]{1,0:T(8,128)(2,1)S(1)}, u32[]{:S(2)}, u32[]{:S(2)}) %collective-permute-start.1) | collective-permute-done | bytes 73760
  294.1 2.9 concatenate
  297.0 1.6 fusion.13
  (117 shorter events, 33.8 us)
Async XLA Ops:
  6.5 250.2 %copy-start = (bf16[512,3072]{1,0:T(8,128)(2,1)S(1)}, bf16[512,3072]{1,0:T(8,128)(2,1)}, u32[]{:S(2)}) copy-start(bf16[512,3072]{1,0:T(8,128)(2,1)} %param.19) | copy-start | bytes 9437188
  6.5 12.3 %copy-start.1 = (bf16[12,4096]{1,0:T(8,128)(2,1)S(1)}, bf16[12,4096]{1,0:T(8,128)(2,1)}, u32[]{:S(2)}) copy-start(bf16[12,4096]{1,0:T(8,128)(2,1)} %param.12) | copy-start | bytes 294916
  6.5 22.2 %copy-start.2 = (bf16[12,4096]{1,0:T(8,128)(2,1)S(1)}, bf16[12,4096]{1,0:T(8,128)(2,1)}, u32[]{:S(2)}) copy-start(bf16[12,4096]{1,0:T(8,128)(2,1)} %param.13) | copy-start | bytes 294916
  6.5 103.6 %all-gather.3.cloned.1.call-start = ((), (), s32[]{:S(2)}) async-start(), calls=%async_computation.3 | async-start | bytes 6389760 | tf_op jit(solution)/shard_map/all_gather | solution.py:68
  7.3 197.2 %all-gather.5.cloned.1.call-start = ((), (), s32[]{:S(2)}) async-start(), calls=%async_computation.4 | async-start | bytes 6389760 | tf_op jit(solution)/shard_map/all_gather | solution.py:69
  9.0 22.4 %copy-start.5 = (s32[64]{0:T(128)S(1)}, s32[64]{0:T(128)}, u32[]{:S(2)}) copy-start(s32[64]{0:T(128)} %param.16) | copy-start | bytes 772
  9.7 13.6 %all-to-all-start = ((bf16[12,8,512]{2,0,1:T(8,128)(2,1)}), bf16[12,8,512]{2,0,1:T(8,128)(2,1)S(1)}, u32[]{:S(2)}, u32[]{:S(2)}) async-start(bf16[12,8,512]{2,0,1:T(8,128)(2,1)} %copy.37), calls=%async_computation | async-start | bytes 262144 | tf_op jit(solution)/shard_map/all_to_all | solution.py:44
  23.3 9.9 %all-to-all-start.1 = ((bf16[12,8,512]{2,0,1:T(8,128)(2,1)}), bf16[12,8,512]{2,0,1:T(8,128)(2,1)S(1)}, u32[]{:S(2)}, u32[]{:S(2)}) async-start(bf16[12,8,512]{2,0,1:T(8,128)(2,1)} %copy.38), calls=%async_computation.1 | async-start | bytes 262144 | tf_op jit(solution)/shard_map/all_to_all | solution.py:45
  33.2 9.9 %all-to-all-start.2 = ((bf16[12,8,512]{2,0,1:T(8,128)(2,1)}), bf16[12,8,512]{2,0,1:T(8,128)(2,1)S(1)}, u32[]{:S(2)}, u32[]{:S(2)}) async-start(bf16[12,8,512]{2,0,1:T(8,128)(2,1)} %copy.41), calls=%async_computation.2 | async-start | bytes 262144 | tf_op jit(solution)/shard_map/all_to_all | solution.py:46
  119.9 94.4 %copy-start.4 = (bf16[96,4,128]{2,0,1:T(8,128)(2,1)S(1)}, bf16[96,4,128]{2,0,1:T(8,128)(2,1)}, u32[]{:S(2)}) copy-start(bf16[96,4,128]{2,0,1:T(8,128)(2,1)} %copy.39) | copy-start | bytes 294916
  258.2 38.8 %copy-start.6 = (f32[3072]{0:T(1024)S(1)}, f32[3072]{0:T(1024)}, u32[]{:S(2)}) copy-start(f32[3072]{0:T(1024)} %param.18) | copy-start | bytes 36868
  279.0 15.1 %collective-permute-start = (bf16[16,3072]{1,0:T(8,128)(2,1)S(1)}, bf16[16,3072]{1,0:T(8,128)(2,1)}, u32[]{:S(2)}, u32[]{:S(2)}) collective-permute-start(bf16[16,3072]{1,0:T(8,128)(2,1)S(1)} %fusion.2), channel_id=1, source_target_pairs={{0,1},{1,2},{2,3},{3,4},{4,5},{5,6},{6,7},{8,9},{9,10},{10,11},{11... | collective-permute-start | bytes 294920
  285.5 8.0 %collective-permute-start.1 = (bf16[12,3072]{1,0:T(8,128)(2,1)S(1)}, bf16[12,3072]{1,0:T(8,128)(2,1)S(1)}, u32[]{:S(2)}, u32[]{:S(2)}) collective-permute-start(bf16[12,3072]{1,0:T(8,128)(2,1)S(1)} %slice), channel_id=1, source_target_pairs={{0,2},{1,3},{2,4},{3,5},{4,6},{5,7},{8,10},{9,11},{10,12},{11,13},... | collective-permute-start | bytes 221192
  293.5 0.6 copy-start.3
Sparse Core Ops, SparseCore 0:
  10.7 99.4 all-gather.2
  113.5 90.9 all-gather.4
where the time goes:
time: 307 us; the launch traced here: 305 us
  waiting for transfers between devices  162 us (53%)
  local copies, waits for them, and re-layouts  50.4 us (16%)
  starting transfers between devices  28.3 us (9%)
  blocking collectives  20.8 us (7%)
  other arithmetic  18.2 us (6%)
  between operations  14.2 us (5%)
  matrix products  11.4 us (4%)
    all_gather x1, waiting for transfers between devices, local(): value_rows = lax.all_gather(stale_value, 'patch', axis=0, tiled=True)  84.6 us
    all_gather x1, waiting for transfers between devices, local(): key_rows = lax.all_gather(stale_key, 'patch', axis=0, tiled=True)  64 us
    unnamed x1, blocking collectives  20.8 us
    dynamic_slice x16, local copies, waits for them, and re-layouts, local(): lax.scan(one_block, remote_carry, (key_blocks, value_blocks, block_starts))  20 us
    reshape x1, local copies, waits for them, and re-layouts, local(): value_blocks = value_rows.reshape(steps_count, span, heads_here, HD)  9.75 us
    reshape x1, local copies, waits for them, and re-layouts, local(): key_blocks = key_rows.reshape(steps_count, span, heads_here, HD)  9.71 us
    all_to_all x1, starting transfers between devices, local(): lax.all_to_all(fresh_query, 'head', split_axis=1, concat_axis=0, tiled=True)  9.14 us
    unnamed x2, starting transfers between devices  8.32 us
  transfers between devices with their start and end apart: 7, of which 6 were waited for; matrix products, arithmetic and copies ran while one was open for 7% of the time, Pallas kernels for 0%

commit v1 on v0

v1 whole, which is shorter than its diff:
```python
import jax
import jax.numpy as jnp
import numpy as np
from jax import lax
from jax.experimental import pallas as pl
from jax.experimental.pallas import tpu as pltpu
from jax.sharding import Mesh, PartitionSpec as P

HD = 128
CAP = 96
NZ, NY, NC, NYL, NX = 8, 4, 2, 2, 4
NHEAD = NYL * NX
GROUP = 512
HEADS_HERE = GROUP // HD
OWN = 12
D = 3072
FAR = NZ * CAP
BIG = -1e30
EXP2_SCALE = float(np.log2(np.e) * HD ** (-0.5))
HEAD = ("yl", "x")
ALL = ("z", "yh", "c", "yl", "x")
f32 = jnp.float32
bf16 = jnp.bfloat16
PACKED = 3 * 768 // 2
OUT_PACKED = (D + D // 2) // 2


def params(mb):
    return pltpu.CompilerParams(vmem_limit_bytes=mb * 2**20)


def lower_half(shape):
    return lax.broadcasted_iota(jnp.int32, shape, 0) < 4


def pack_kernel(q_ref, k_ref, v_ref, out_ref):
    mask = lower_half((8, GROUP // 2))
    for h in range(NHEAD):
        tops, rests = [], []
        for ref in (q_ref, k_ref, v_ref):
            rows = ref[:, h * GROUP:(h + 1) * GROUP].astype(f32)
            tops.append(rows[0:8])
            tail = rows[4:12]
            first = pltpu.roll(tail[:, : GROUP // 2], 4, 0)
            rests.append(jnp.where(mask, first, tail[:, GROUP // 2:]))
        flat = jnp.concatenate(tops + rests, axis=1)
        both = jnp.concatenate([flat[:, :PACKED], flat[:, PACKED:]], axis=0)
        out_ref[h] = both.astype(bf16)


def pack(fq, fk, fv):
    return pl.pallas_call(
        pack_kernel,
        out_shape=jax.ShapeDtypeStruct((NHEAD, 16, PACKED), bf16),
        compiler_params=params(16),
    )(fq, fk, fv)


def row_tokens():
    top = [12 * s + r for s in range(8) for r in range(8)]
    rest = [12 * s + r for s in range(8) for r in range(8, 12)]
    return np.array(top + rest, np.int32)


def unpack_kernel(in_ref, q_ref, k_ref, v_ref):
    mask = lower_half((8, GROUP // 2))
    tops = [[], [], []]
    rests = [[], [], []]
    for s in range(NHEAD):
        both = in_ref[s].astype(f32)
        flat = jnp.concatenate([both[0:8], both[8:16]], axis=1)
        for i in range(3):
            tops[i].append(flat[:, i * GROUP:(i + 1) * GROUP])
            base = 3 * GROUP + i * (GROUP // 2)
            rests[i].append(flat[:, base:base + GROUP // 2])
    for i, ref in enumerate((q_ref, k_ref, v_ref)):
        tiles = list(tops[i])
        for k in range(NHEAD // 2):
            a, b = rests[i][2 * k], rests[i][2 * k + 1]
            left = jnp.where(mask, a, pltpu.roll(b, 4, 0))
            right = jnp.where(mask, pltpu.roll(a, 4, 0), b)
            tiles.append(jnp.concatenate([left, right], axis=1))
        ref[...] = jnp.concatenate(tiles, axis=0).astype(bf16)


def unpack(received):
    one = jax.ShapeDtypeStruct((CAP, GROUP), bf16)
    return pl.pallas_call(
        unpack_kernel, out_shape=(one, one, one), compiler_params=params(16)
    )(received)


def attention_kernel(q_ref, ka_ref, kb_ref, kf_ref, va_ref, vb_ref, vf_ref, bias_ref, out_ref):
    h = pl.program_id(0)
    lane = lax.broadcasted_iota(jnp.int32, (CAP, HD), 1)
    keys = (ka_ref[...], kb_ref[...], kf_ref[...])
    values = (va_ref[...], vb_ref[...], vf_ref[...])
    starts = (0, FAR, 2 * FAR)
    sizes = (FAR, FAR, CAP)
    for b in range(NY):
        query = q_ref[b]
        scores = []
        for key, start, size in zip(keys, starts, sizes):
            dot = lax.dot_general(query, key, (((1,), (1,)), ((), ())), preferred_element_type=f32)
            scores.append(dot + bias_ref[b, :, start:start + size])
        top = scores[0].max(axis=1, keepdims=True)
        for s in scores[1:]:
            top = jnp.maximum(top, s.max(axis=1, keepdims=True))
        total = jnp.zeros((CAP, 1), f32)
        accum = jnp.zeros((CAP, HD), f32)
        for s, value in zip(scores, values):
            weights = jnp.exp2((s - top) * EXP2_SCALE)
            total = total + weights.sum(axis=1, keepdims=True)
            accum = accum + jnp.dot(weights.astype(bf16), value, preferred_element_type=f32)
        out_ref[b, :, pl.ds(pl.multiple_of(h * HD, HD), HD)] = (accum / total).astype(bf16)
        level = top * EXP2_SCALE + jnp.log2(total)
        hi = level.astype(bf16).astype(f32)
        mid = (level - hi).astype(bf16).astype(f32)
        low = level - hi - mid
        stat = jnp.where(lane == 3 * h, hi, 0.0)
        stat = jnp.where(lane == 3 * h + 1, mid, stat)
        stat = jnp.where(lane == 3 * h + 2, low, stat).astype(bf16)

        @pl.when(h == 0)
        def _():
            out_ref[b, :, GROUP:] = stat

        @pl.when(h != 0)
        def _():
            out_ref[b, :, GROUP:] = out_ref[b, :, GROUP:] + stat


def attention(q, ka, kb, kf, va, vb, vf, bias):
    def column(rows):
        return pl.BlockSpec((rows, HD), lambda h: (0, h))

    return pl.pallas_call(
        attention_kernel,
        grid=(HEADS_HERE,),
        in_specs=[
            pl.BlockSpec((NY, CAP, HD), lambda h: (0, 0, h)),
            column(FAR), column(FAR), column(CAP), column(FAR), column(FAR), column(CAP),
            pl.BlockSpec((NY, 1, 2 * FAR + HD), lambda h: (0, 0, 0)),
        ],
        out_specs=pl.BlockSpec((NY, CAP, GROUP + HD), lambda h: (0, 0, 0)),
        out_shape=jax.ShapeDtypeStruct((NY, CAP, GROUP + HD), bf16),
        compiler_params=params(32),
        cost_estimate=pl.CostEstimate(
            flops=4 * NY * CAP * (2 * FAR + CAP) * GROUP,
            bytes_accessed=4 * 2 * FAR * GROUP * 2,
            transcendentals=NY * CAP * (2 * FAR + CAP) * HEADS_HERE,
        ),
    )(q, ka, kb, kf, va, vb, vf, bias)


def project_kernel(part_ref, w_ref, out_ref, w_vmem, sem):
    copy = pltpu.make_async_copy(w_ref, w_vmem, sem)
    copy.start()
    stats = [part_ref[b, :, GROUP:].astype(f32) for b in range(NY)]
    heads = []
    for h in range(HEADS_HERE):
        levels = [s[:, 3 * h:3 * h + 1] + s[:, 3 * h + 1:3 * h + 2] + s[:, 3 * h + 2:3 * h + 3] for s in stats]
        top = levels[0]
        for level in levels[1:]:
            top = jnp.maximum(top, level)
        total = jnp.zeros((CAP, 1), f32)
        accum = jnp.zeros((CAP, HD), f32)
        for b in range(NY):
            weight = jnp.exp2(levels[b] - top)
            total = total + weight
            accum = accum + weight * part_ref[b, :, h * HD:(h + 1) * HD].astype(f32)
        heads.append((accum / total).astype(bf16))
    attended = jnp.concatenate(heads, axis=1)
    copy.wait()
    half = D // 2
    step = 384
    mask = lower_half((8, step))
    for j in range(half // step):
        left = jnp.dot(attended, w_vmem[:, j * step:(j + 1) * step], preferred_element_type=f32)
        right = jnp.dot(attended, w_vmem[:, half + j * step:half + (j + 1) * step], preferred_element_type=f32)
        for s in range(NHEAD):
            k = s // 2
            a = left[64 + 8 * k:72 + 8 * k]
            b = right[64 + 8 * k:72 + 8 * k]
            if s % 2 == 0:
                rest = jnp.where(mask, a, pltpu.roll(b, 4, 0))
            else:
                rest = jnp.where(mask, pltpu.roll(a, 4, 0), b)
            pieces = (
                (j * step, left[8 * s:8 * s + 8]),
                (half + j * step, right[8 * s:8 * s + 8]),
                (D + j * step, rest),
            )
            for col, tile in pieces:
                row = 8 * (col // OUT_PACKED)
                col = col % OUT_PACKED
                assert col + step <= OUT_PACKED
                out_ref[s, row:row + 8, col:col + step] = tile.astype(bf16)


def project(parts, w):
    return pl.pallas_call(
        project_kernel,
        in_specs=[pl.BlockSpec(memory_space=pltpu.VMEM), pl.BlockSpec(memory_space=pl.ANY)],
        out_specs=pl.BlockSpec(memory_space=pltpu.VMEM),
        out_shape=jax.ShapeDtypeStruct((NHEAD, 16, OUT_PACKED), bf16),
        scratch_shapes=[pltpu.VMEM((GROUP, D), bf16), pltpu.SemaphoreType.DMA],
        compiler_params=params(24),
    )(parts, w)


def mix_kernel(limit_ref, in_ref, hidden_ref, gate_ref, out_ref):
    total = in_ref[0].astype(f32)
    for s in range(1, NHEAD):
        total = total + in_ref[s].astype(f32)
    flat = jnp.concatenate([total[0:8], total[8:16]], axis=1)
    half = D // 2
    rest = flat[:, D:]
    tail = jnp.concatenate([rest[0:4], rest[4:8]], axis=1)
    projected = jnp.concatenate([flat[:, :D], tail], axis=0)
    residual = hidden_ref[...].astype(f32)
    live = lax.broadcasted_iota(jnp.int32, (OWN, D), 0) < limit_ref[0]
    mixed = jnp.where(live, residual + gate_ref[...] * projected, residual)
    out_ref[...] = mixed.astype(bf16)


def mix(limit, received, hidden, gate):
    vmem = pl.BlockSpec(memory_space=pltpu.VMEM)
    return pl.pallas_call(
        mix_kernel,
        in_specs=[pl.BlockSpec(memory_space=pltpu.SMEM), vmem, vmem, vmem],
        out_specs=vmem,
        out_shape=jax.ShapeDtypeStruct((OWN, D), bf16),
        compiler_params=params(16),
    )(limit, received, hidden, gate)


def swap(x, axis):
    return lax.all_to_all(x, axis, split_axis=0, concat_axis=0, tiled=True)


def local(fq, fk, fv, sk, sv, lengths, hidden, gate, w):
    z, yh, c = (lax.axis_index(a) for a in ("z", "yh", "c"))
    own_head = lax.axis_index("yl") * NX + lax.axis_index("x")

    def spread(x):
        return swap(jnp.broadcast_to(x[None], (NZ, CAP, GROUP)), "z").reshape(FAR, GROUP)

    def other_core(x):
        return lax.ppermute(x, "c", [(0, 1), (1, 0)])

    ka, va = spread(sk), spread(sv)
    kb, vb = other_core(ka), other_core(va)
    query, kf, vf = unpack(swap(pack(fq, fk, fv), HEAD))
    queries = lax.all_gather(query, "yh", axis=0)

    table = lengths.reshape(NZ, NY, NC)
    mine = lax.dynamic_slice_in_dim(table, yh, 1, 1)[:, 0, :]
    own_core = jnp.where(c == 0, mine[:, 0], mine[:, 1])
    far_core = jnp.where(c == 0, mine[:, 1], mine[:, 0])
    own_length = jnp.sum(jnp.where(jnp.arange(NZ) == z, own_core, 0))
    slots = jnp.arange(CAP, dtype=jnp.int32)
    is_mine = (jnp.arange(NY) == yh)[:, None, None]
    stale_here = (jnp.arange(NZ) == z)[None, :, None]
    live_a = (slots[None, None, :] < own_core[None, :, None]) & ~(is_mine & stale_here)
    live_b = jnp.broadcast_to(slots[None, None, :] < far_core[None, :, None], (NY, NZ, CAP))
    live_f = (jnp.asarray(row_tokens())[None, :] < own_length) & is_mine[:, :, 0]
    live = jnp.concatenate([live_a.reshape(NY, FAR), live_b.reshape(NY, FAR), live_f, jnp.zeros((NY, HD - CAP), bool)], axis=1)
    bias = jnp.where(live, 0.0, BIG).astype(f32)[:, None, :]

    parts = attention(queries, ka, kb, kf, va, vb, vf, bias)
    packed = project(swap(parts, "yh"), w)
    limit = jnp.clip(own_length - own_head * OWN, 0, OWN)[None]
    return mix(limit, swap(packed, HEAD), hidden, gate[None, :])


def solution(mesh):
    grid = Mesh(mesh.devices.reshape(NZ, NY, NC, NYL, NX), ALL)
    rows = P(ALL, None)
    stale = P(("z", "yh", "c"), HEAD)
    in_specs = (rows, rows, rows, stale, stale, P(), rows, P(), P(HEAD, None))
    return jax.shard_map(local, mesh=grid, in_specs=in_specs, out_specs=rows, check_vma=False)
```

time: 307 us -> 137 us (0.45)
  the two profiles are of different devices: /device:TPU:6 before, /device:TPU:8 now
where the time goes in v1:
time: 137 us; the launch traced here: 136 us
  waiting for transfers between devices  52.9 us (39%)
  blocking collectives  33.3 us (24%)
  starting transfers between devices  28.4 us (21%)
  Pallas kernels  14.6 us (11%)
  local copies, waits for them, and re-layouts  4.62 us (3%)
  other arithmetic  1.51 us (1%)
    all_to_all x4, waiting for transfers between devices, swap(): return lax.all_to_all(x, axis, split_axis=0, concat_axis=0, tiled=True)  52.9 us
    all_to_all x4, starting transfers between devices, swap(): return lax.all_to_all(x, axis, split_axis=0, concat_axis=0, tiled=True)  24.6 us
    all_to_all x1, blocking collectives, swap(): return lax.all_to_all(x, axis, split_axis=0, concat_axis=0, tiled=True)  16.9 us
    all_gather x1, blocking collectives, local(): queries = lax.all_gather(query, 'yh', axis=0)  16.4 us
    pallas_call x1, Pallas kernels, attention(): pl.pallas_call(attention_kernel, grid=(HEADS_HERE,), in_specs=[pl.BlockSp...  10.9 us
    ppermute x2, starting transfers between devices, other_core(): return lax.ppermute(x, 'c', [(0, 1), (1, 0)])  3.83 us
    broadcast_in_dim x2, local copies, waits for them, and re-layouts, spread(): jnp.broadcast_to(x[None], (NZ, CAP, GROUP))  3.78 us
  transfers between devices with their start and end apart: 6, of which 4 were waited for; matrix products, arithmetic and copies ran while one was open for 2% of the time, Pallas kernels for 1%

profile of v1, /device:TPU:8, one launch (start us, length us, event | category | flops | bytes accessed | tf_op | source)
XLA Modules:
  0.0 136.1 jit_solution(6472333102996944419)
XLA Ops:
  0.0 1.9 %broadcast_in_dim.27 = bf16[8,96,512]{2,1,0:T(8,128)(2,1)} broadcast(bf16[96,512]{1,0:T(8,128)(2,1)} %param.14), dimensions={1,2} | broadcast | bytes 884736 | tf_op jit(solution)/shard_map/broadcast_in_dim | solution.py:247
  2.0 10.3 %all-to-all-start.2 = ((bf16[8,96,512]{2,1,0:T(8,128)(2,1)}), bf16[8,96,512]{2,1,0:T(8,128)(2,1)S(1)}, u32[]{:S(2)}, u32[]{:S(2)}) async-start(bf16[8,96,512]{2,1,0:T(8,128)(2,1)} %broadcast_in_dim.27), calls=%async_computation.2 | async-start | bytes 1572864 | tf_op jit(solution)/shard_map/all_to_all | solution.py:239
  12.3 23.1 %all-to-all-done.2 = bf16[8,96,512]{2,1,0:T(8,128)(2,1)S(1)} async-done(((bf16[8,96,512]{2,1,0:T(8,128)(2,1)}), bf16[8,96,512]{2,1,0:T(8,128)(2,1)S(1)}, u32[]{:S(2)}, u32[]{:S(2)}) %all-to-all-start.2) | async-done | bytes 786464 | tf_op jit(solution)/shard_map/all_to_all | solution.py:239
  35.4 1.9 %broadcast_in_dim.26 = bf16[8,96,512]{2,1,0:T(8,128)(2,1)} broadcast(bf16[96,512]{1,0:T(8,128)(2,1)} %param.13), dimensions={1,2} | broadcast | bytes 884736 | tf_op jit(solution)/shard_map/broadcast_in_dim | solution.py:247
  37.2 3.5 %all-to-all-start.1 = ((bf16[8,96,512]{2,1,0:T(8,128)(2,1)}), bf16[8,96,512]{2,1,0:T(8,128)(2,1)S(1)}, u32[]{:S(2)}, u32[]{:S(2)}) async-start(bf16[8,96,512]{2,1,0:T(8,128)(2,1)} %broadcast_in_dim.26), calls=%async_computation.1 | async-start | bytes 1572864 | tf_op jit(solution)/shard_map/all_to_all | solution.py:239
  40.8 0.1 and_not_fusion
  40.9 0.1 and.68
  40.9 0.1 and.69
  41.0 0.1 lt.56
  41.1 0.1 reshape.225
  41.3 0.1 copy.15
  41.3 0.6 select_reduce_fusion
  42.0 0.1 broadcast_reduce_fusion
  42.1 0.1 lt.61
  42.2 0.1 lt.58
  42.2 0.8 shard_map.100
  43.1 0.6 broadcast_compare_fusion
  43.8 1.9 %collective-permute-start.1 = (bf16[768,512]{1,0:T(8,128)(2,1)S(1)}, bf16[768,512]{1,0:T(8,128)(2,1)S(1)}, u32[]{:S(2)}, u32[]{:S(2)}) collective-permute-start(bf16[768,512]{1,0:T(8,128)(2,1)S(1)} %bitcast.15), channel_id=1, source_target_pairs={{0,8},{8,0},{1,9},{9,1},{2,10},{10,2},{3,11},{11,3},{4,12},{12,4},... | collective-permute-start | bytes 2359304 | tf_op jit(solution)/shard_map/ppermute | solution.py:250
  45.7 18.6 %all-to-all-done.1 = bf16[8,96,512]{2,1,0:T(8,128)(2,1)S(1)} async-done(((bf16[8,96,512]{2,1,0:T(8,128)(2,1)}), bf16[8,96,512]{2,1,0:T(8,128)(2,1)S(1)}, u32[]{:S(2)}, u32[]{:S(2)}) %all-to-all-start.1) | async-done | bytes 786464 | tf_op jit(solution)/shard_map/all_to_all | solution.py:239
  64.3 5.8 %all-to-all-start = ((bf16[8,16,1152]{2,1,0:T(8,128)(2,1)}), bf16[8,16,1152]{2,1,0:T(8,128)(2,1)S(1)}, u32[]{:S(2)}, u32[]{:S(2)}) async-start(bf16[8,16,1152]{2,1,0:T(8,128)(2,1)} %shard_map.100), calls=%async_computation | async-start | bytes 589824 | tf_op jit(solution)/shard_map/all_to_all | solution.py:239
  70.1 1.9 %collective-permute-start = (bf16[768,512]{1,0:T(8,128)(2,1)S(1)}, bf16[768,512]{1,0:T(8,128)(2,1)S(1)}, u32[]{:S(2)}, u32[]{:S(2)}) collective-permute-start(bf16[768,512]{1,0:T(8,128)(2,1)S(1)} %bitcast.17), channel_id=1, source_target_pairs={{0,8},{8,0},{1,9},{9,1},{2,10},{10,2},{3,11},{11,3},{4,12},{12,4},... | collective-permute-start | bytes 2359304 | tf_op jit(solution)/shard_map/ppermute | solution.py:250
  72.0 0.1 and_bitcast_fusion.1
  72.1 0.1 concatenate.16
  72.2 4.2 %all-to-all-done.in_ref = bf16[8,16,1152]{2,1,0:T(8,128)(2,1)S(1)} async-done(((bf16[8,16,1152]{2,1,0:T(8,128)(2,1)}), bf16[8,16,1152]{2,1,0:T(8,128)(2,1)S(1)}, u32[]{:S(2)}, u32[]{:S(2)}) %all-to-all-start) | async-done | bytes 294944 | tf_op jit(solution)/shard_map/all_to_all | solution.py:239
  76.5 0.0 copy-start
  76.5 16.4 %all-gather = bf16[384,512]{1,0:T(8,128)(2,1)S(1)} all-gather(bf16[96,512]{1,0:T(8,128)(2,1)S(1)} %get-tuple-element.8), channel_id=2, replica_groups=mesh['z'=8,'yh'=4,'c'=2,'yl'=2,'x'=4] {'yh'}, dimensions={0}, use_global_device_ids=true | all-gather | bytes 491520 | tf_op jit(solution)/shard_map/all_gather | solution.py:255
  92.8 10.9 %shard_map.102 = bf16[4,96,640]{2,1,0:T(8,128)(2,1)S(1)} custom-call(bf16[4,96,512]{2,1,0:T(8,128)(2,1)S(1)} %bitcast.19, bf16[768,512]{1,0:T(8,128)(2,1)S(1)} %bitcast.18, bf16[768,512]{1,0:T(8,128)(2,1)S(1)} %collective-permute-done.kb_ref, bf16[96,512]{1,0:T(8,128)(2,1)S(1)} %get-tuple-element.9.kf_ref, bf16[768,512]{1,0:T(8,128)(2,1)S(1)} %bitcast.16, ...), custom_call_target="tpu_custom_call" | custom-call | flops 1283457024 | bytes 6291456 | tf_op jit(solution)/shard_map/pallas_call | solution.py:137
  103.7 16.9 %all_to_all.25.part_ref = bf16[4,96,640]{2,1,0:T(8,128)(2,1)S(1)} all-to-all(bf16[4,96,640]{2,1,0:T(8,128)(2,1)S(1)} %shard_map.102), channel_id=1, replica_groups=mesh['z'=8,'yh'=4,'c'=2,'yl'=2,'x'=4] {'yh'}, dimensions={0} | all-to-all | bytes 983040 | tf_op jit(solution)/shard_map/all_to_all | solution.py:239
  120.7 2.1 %shard_map.103 = bf16[8,16,2304]{2,1,0:T(8,128)(2,1)} custom-call(bf16[4,96,640]{2,1,0:T(8,128)(2,1)S(1)} %all_to_all.25.part_ref, bf16[512,3072]{1,0:T(8,128)(2,1)S(1)} %copy-done), custom_call_target="tpu_custom_call" | custom-call | tf_op jit(solution)/shard_map/pallas_call | solution.py:202
  122.8 5.0 %all-to-all-start.4 = ((bf16[8,16,2304]{2,1,0:T(8,128)(2,1)}), bf16[8,16,2304]{2,1,0:T(8,128)(2,1)S(1)}, u32[]{:S(2)}, u32[]{:S(2)}) async-start(bf16[8,16,2304]{2,1,0:T(8,128)(2,1)} %shard_map.103), calls=%async_computation.4 | async-start | bytes 1179648 | tf_op jit(solution)/shard_map/all_to_all | solution.py:239
  128.4 6.9 %all-to-all-done.4.in_ref = bf16[8,16,2304]{2,1,0:T(8,128)(2,1)S(1)} async-done(((bf16[8,16,2304]{2,1,0:T(8,128)(2,1)}), bf16[8,16,2304]{2,1,0:T(8,128)(2,1)S(1)}, u32[]{:S(2)}, u32[]{:S(2)}) %all-to-all-start.4) | async-done | bytes 589856 | tf_op jit(solution)/shard_map/all_to_all | solution.py:239
  135.3 0.7 shard_map.104
  (28 shorter events, 0.2 us)
Async XLA Ops:
  0.0 43.1 %copy-start.7 = (s32[96]{0:T(128)S(1)}, s32[96]{0:T(128)}, u32[]{:S(2)}) copy-start(s32[96]{0:T(128)} %constant.35.clone) | copy-start | bytes 1156
  0.0 41.1 %copy-start.6 = (s32[64]{0:T(128)S(1)}, s32[64]{0:T(128)}, u32[]{:S(2)}) copy-start(s32[64]{0:T(128)} %param.15) | copy-start | bytes 772
  0.0 42.2 %copy-start.3 = (bf16[12,4096]{1,0:T(8,128)(2,1)S(1)}, bf16[12,4096]{1,0:T(8,128)(2,1)}, u32[]{:S(2)}) copy-start(bf16[12,4096]{1,0:T(8,128)(2,1)} %v_ref.1) | copy-start | bytes 294916
  0.0 42.2 %copy-start.2 = (bf16[12,4096]{1,0:T(8,128)(2,1)S(1)}, bf16[12,4096]{1,0:T(8,128)(2,1)}, u32[]{:S(2)}) copy-start(bf16[12,4096]{1,0:T(8,128)(2,1)} %k_ref.1) | copy-start | bytes 294916
  0.0 42.2 %copy-start.1 = (bf16[12,4096]{1,0:T(8,128)(2,1)S(1)}, bf16[12,4096]{1,0:T(8,128)(2,1)}, u32[]{:S(2)}) copy-start(bf16[12,4096]{1,0:T(8,128)(2,1)} %q_ref.1) | copy-start | bytes 294916
  2.0 33.4 %all-to-all-start.2 = ((bf16[8,96,512]{2,1,0:T(8,128)(2,1)}), bf16[8,96,512]{2,1,0:T(8,128)(2,1)S(1)}, u32[]{:S(2)}, u32[]{:S(2)}) async-start(bf16[8,96,512]{2,1,0:T(8,128)(2,1)} %broadcast_in_dim.27), calls=%async_computation.2 | async-start | bytes 1572864 | tf_op jit(solution)/shard_map/all_to_all | solution.py:239
  37.2 27.1 %all-to-all-start.1 = ((bf16[8,96,512]{2,1,0:T(8,128)(2,1)}), bf16[8,96,512]{2,1,0:T(8,128)(2,1)S(1)}, u32[]{:S(2)}, u32[]{:S(2)}) async-start(bf16[8,96,512]{2,1,0:T(8,128)(2,1)} %broadcast_in_dim.26), calls=%async_computation.1 | async-start | bytes 1572864 | tf_op jit(solution)/shard_map/all_to_all | solution.py:239
  43.8 49.1 %collective-permute-start.1 = (bf16[768,512]{1,0:T(8,128)(2,1)S(1)}, bf16[768,512]{1,0:T(8,128)(2,1)S(1)}, u32[]{:S(2)}, u32[]{:S(2)}) collective-permute-start(bf16[768,512]{1,0:T(8,128)(2,1)S(1)} %bitcast.15), channel_id=1, source_target_pairs={{0,8},{8,0},{1,9},{9,1},{2,10},{10,2},{3,11},{11,3},{4,12},{12,4},... | collective-permute-start | bytes 2359304 | tf_op jit(solution)/shard_map/ppermute | solution.py:250
  64.3 12.1 %all-to-all-start = ((bf16[8,16,1152]{2,1,0:T(8,128)(2,1)}), bf16[8,16,1152]{2,1,0:T(8,128)(2,1)S(1)}, u32[]{:S(2)}, u32[]{:S(2)}) async-start(bf16[8,16,1152]{2,1,0:T(8,128)(2,1)} %shard_map.100), calls=%async_computation | async-start | bytes 589824 | tf_op jit(solution)/shard_map/all_to_all | solution.py:239
  70.1 22.8 %collective-permute-start = (bf16[768,512]{1,0:T(8,128)(2,1)S(1)}, bf16[768,512]{1,0:T(8,128)(2,1)S(1)}, u32[]{:S(2)}, u32[]{:S(2)}) collective-permute-start(bf16[768,512]{1,0:T(8,128)(2,1)S(1)} %bitcast.17), channel_id=1, source_target_pairs={{0,8},{8,0},{1,9},{9,1},{2,10},{10,2},{3,11},{11,3},{4,12},{12,4},... | collective-permute-start | bytes 2359304 | tf_op jit(solution)/shard_map/ppermute | solution.py:250
  76.5 44.2 %copy-start = (bf16[512,3072]{1,0:T(8,128)(2,1)S(1)}, bf16[512,3072]{1,0:T(8,128)(2,1)}, u32[]{:S(2)}) copy-start(bf16[512,3072]{1,0:T(8,128)(2,1)} %w_ref.1) | copy-start | bytes 9437188
  103.7 31.6 %copy-start.4 = (bf16[12,3072]{1,0:T(8,128)(2,1)S(1)}, bf16[12,3072]{1,0:T(8,128)(2,1)}, u32[]{:S(2)}) copy-start(bf16[12,3072]{1,0:T(8,128)(2,1)} %hidden_ref.1) | copy-start | bytes 221188
  103.7 31.6 %copy-start.5 = (f32[3072]{0:T(1024)S(1)}, f32[3072]{0:T(1024)}, u32[]{:S(2)}) copy-start(f32[3072]{0:T(1024)} %param.17) | copy-start | bytes 36868
  122.8 12.5 %all-to-all-start.4 = ((bf16[8,16,2304]{2,1,0:T(8,128)(2,1)}), bf16[8,16,2304]{2,1,0:T(8,128)(2,1)S(1)}, u32[]{:S(2)}, u32[]{:S(2)}) async-start(bf16[8,16,2304]{2,1,0:T(8,128)(2,1)} %shard_map.103), calls=%async_computation.4 | async-start | bytes 1179648 | tf_op jit(solution)/shard_map/all_to_all | solution.py:239

commit v2 on v1

--- a/solution.py
+++ b/solution.py
@@ -14,7 +14,8 @@
 HEADS_HERE = GROUP // HD
 OWN = 12
 D = 3072
-FAR = NZ * CAP
+KEYS = NZ * NC * CAP
+QUERIES = NY * CAP
 BIG = -1e30
 EXP2_SCALE = float(np.log2(np.e) * HD ** (-0.5))
 HEAD = ("yl", "x")
@@ -56,13 +57,7 @@
     )(fq, fk, fv)
 
 
-def row_tokens():
-    top = [12 * s + r for s in range(8) for r in range(8)]
-    rest = [12 * s + r for s in range(8) for r in range(8, 12)]
-    return np.array(top + rest, np.int32)
-
-
-def unpack_kernel(in_ref, q_ref, k_ref, v_ref):
+def unpack_kernel(place_ref, lengths_ref, in_ref, q_ref, k_ref, v_ref, bias_ref):
     mask = lower_half((8, GROUP // 2))
     tops = [[], [], []]
     rests = [[], [], []]
@@ -82,75 +77,98 @@
             tiles.append(jnp.concatenate([left, right], axis=1))
         ref[...] = jnp.concatenate(tiles, axis=0).astype(bf16)
 
-
-def unpack(received):
+    z, yh, c = place_ref[0], place_ref[1], place_ref[2]
+    row = lax.broadcasted_iota(jnp.int32, (CAP, HD), 0)
+    mine = lax.broadcasted_iota(jnp.int32, (CAP, HD), 1) == yh
+    for j in range(NZ * NC):
+        length = lengths_ref[(j // NC) * NY * NC + yh * NC + j % NC]
+        hidden_length = jnp.where((j // NC == z) & (j % NC == c), 0, length)
+        seen = row < jnp.where(mine, hidden_length, length)
+        bias_ref[j * CAP:(j + 1) * CAP] = jnp.where(seen, 0.0, BIG).astype(bf16)
+    rest = row - 64
+    token = jnp.where(row < 64, 12 * (row >> 3) + (row & 7), 12 * (rest >> 2) + 8 + (rest & 3))
+    own_length = lengths_ref[z * NY * NC + yh * NC + c]
+    seen = token < jnp.where(mine, own_length, 0)
+    bias_ref[KEYS:] = jnp.where(seen, 0.0, BIG).astype(bf16)
+
+
+def unpack(place, lengths, received):
     one = jax.ShapeDtypeStruct((CAP, GROUP), bf16)
-    return pl.pallas_call(
-        unpack_kernel, out_shape=(one, one, one), compiler_params=params(16)
-    )(received)
-
-
-def attention_kernel(q_ref, ka_ref, kb_ref, kf_ref, va_ref, vb_ref, vf_ref, bias_ref, out_ref):
+    smem = pl.BlockSpec(memory_space=pltpu.SMEM)
+    vmem = pl.BlockSpec(memory_space=pltpu.VMEM)
+    return pl.pallas_call(
+        unpack_kernel,
+        in_specs=[smem, smem, vmem],
+        out_specs=(vmem,) * 4,
+        out_shape=(one, one, one, jax.ShapeDtypeStruct((KEYS + CAP, HD), bf16)),
+        compiler_params=params(16),
+    )(place, lengths, received)
+
+
+def attention_kernel(q_ref, k_ref, v_ref, kf_ref, vf_ref, hot_ref, bias_ref, out_ref):
     h = pl.program_id(0)
-    lane = lax.broadcasted_iota(jnp.int32, (CAP, HD), 1)
-    keys = (ka_ref[...], kb_ref[...], kf_ref[...])
-    values = (va_ref[...], vb_ref[...], vf_ref[...])
-    starts = (0, FAR, 2 * FAR)
-    sizes = (FAR, FAR, CAP)
-    for b in range(NY):
-        query = q_ref[b]
-        scores = []
-        for key, start, size in zip(keys, starts, sizes):
-            dot = lax.dot_general(query, key, (((1,), (1,)), ((), ())), preferred_element_type=f32)
-            scores.append(dot + bias_ref[b, :, start:start + size])
-        top = scores[0].max(axis=1, keepdims=True)
-        for s in scores[1:]:
-            top = jnp.maximum(top, s.max(axis=1, keepdims=True))
-        total = jnp.zeros((CAP, 1), f32)
-        accum = jnp.zeros((CAP, HD), f32)
-        for s, value in zip(scores, values):
-            weights = jnp.exp2((s - top) * EXP2_SCALE)
-            total = total + weights.sum(axis=1, keepdims=True)
-            accum = accum + jnp.dot(weights.astype(bf16), value, preferred_element_type=f32)
-        out_ref[b, :, pl.ds(pl.multiple_of(h * HD, HD), HD)] = (accum / total).astype(bf16)
-        level = top * EXP2_SCALE + jnp.log2(total)
-        hi = level.astype(bf16).astype(f32)
-        mid = (level - hi).astype(bf16).astype(f32)
-        low = level - hi - mid
-        stat = jnp.where(lane == 3 * h, hi, 0.0)
-        stat = jnp.where(lane == 3 * h + 1, mid, stat)
-        stat = jnp.where(lane == 3 * h + 2, low, stat).astype(bf16)
-
-        @pl.when(h == 0)
-        def _():
-            out_ref[b, :, GROUP:] = stat
-
-        @pl.when(h != 0)
-        def _():
-            out_ref[b, :, GROUP:] = out_ref[b, :, GROUP:] + stat
-
-
-def attention(q, ka, kb, kf, va, vb, vf, bias):
-    def column(rows):
-        return pl.BlockSpec((rows, HD), lambda h: (0, h))
+    lane = lax.broadcasted_iota(jnp.int32, (QUERIES, HD), 1)
+    query = jnp.concatenate([q_ref[...], hot_ref[...]], axis=1)
+    chunk = KEYS // 4
+    pieces = [(k_ref[i:i + chunk], v_ref[i:i + chunk], bias_ref[i:i + chunk]) for i in range(0, KEYS, chunk)]
+    pieces.append((kf_ref[...], vf_ref[...], bias_ref[KEYS:]))
+    scores = []
+    for key, _, bias in pieces:
+        key = jnp.concatenate([key, bias], axis=1)
+        scores.append(lax.dot_general(query, key, (((1,), (1,)), ((), ())), preferred_element_type=f32))
+    top = scores[0].max(axis=1, keepdims=True)
+    for s in scores[1:]:
+        top = jnp.maximum(top, s.max(axis=1, keepdims=True))
+    total = jnp.zeros((QUERIES, 1), f32)
+    accum = jnp.zeros((QUERIES, HD), f32)
+    for s, (_, value, _) in zip(scores, pieces):
+        weights = jnp.exp2((s - top) * EXP2_SCALE)
+        total = total + weights.sum(axis=1, keepdims=True)
+        accum = accum + jnp.dot(weights.astype(bf16), value, preferred_element_type=f32)
+    out_ref[:, pl.ds(pl.multiple_of(h * HD, HD), HD)] = (accum / total).astype(bf16)
+    level = top * EXP2_SCALE + jnp.log2(total)
+    hi = level.astype(bf16).astype(f32)
+    mid = (level - hi).astype(bf16).astype(f32)
+    low = level - hi - mid
+    stat = jnp.where(lane == 3 * h, hi, 0.0)
+    stat = jnp.where(lane == 3 * h + 1, mid, stat)
+    stat = jnp.where(lane == 3 * h + 2, low, stat).astype(bf16)
+
+    @pl.when(h == 0)
+    def _():
+        out_ref[:, GROUP:] = stat
+
+    @pl.when(h != 0)
+    def _():
+        out_ref[:, GROUP:] = out_ref[:, GROUP:] + stat
+
+
+def attention(q, kv, kf, vf, bias):
+    hot = np.zeros((QUERIES, HD), np.float32)
+    hot[np.arange(QUERIES), np.arange(QUERIES) // CAP] = 1
+
+    def column(rows, skip=0):
+        return pl.BlockSpec((rows, HD), lambda h: (0, h + skip))
+
+    def whole(rows, cols):
+        return pl.BlockSpec((rows, cols), lambda h: (0, 0))
 
     return pl.pallas_call(
         attention_kernel,
         grid=(HEADS_HERE,),
         in_specs=[
-            pl.BlockSpec((NY, CAP, HD), lambda h: (0, 0, h)),
-            column(FAR), column(FAR), column(CAP), column(FAR), column(FAR), column(CAP),
-            pl.BlockSpec((NY, 1, 2 * FAR + HD), lambda h: (0, 0, 0)),
+            column(QUERIES), column(KEYS), column(KEYS, HEADS_HERE), column(CAP), column(CAP),
+            whole(QUERIES, HD), whole(KEYS + CAP, HD),
         ],
-        out_specs=pl.BlockSpec((NY, CAP, GROUP + HD), lambda h: (0, 0, 0)),
-        out_shape=jax.ShapeDtypeStruct((NY, CAP, GROUP + HD), bf16),
-        compiler_params=params(32),
+        out_specs=whole(QUERIES, GROUP + HD),
+        out_shape=jax.ShapeDtypeStruct((QUERIES, GROUP + HD), bf16),
+        compiler_params=params(40),
         cost_estimate=pl.CostEstimate(
-            flops=4 * NY * CAP * (2 * FAR + CAP) * GROUP,
-            bytes_accessed=4 * 2 * FAR * GROUP * 2,
-            transcendentals=NY * CAP * (2 * FAR + CAP) * HEADS_HERE,
+            flops=4 * QUERIES * (KEYS + CAP) * GROUP,
+            bytes_accessed=4 * KEYS * GROUP,
+            transcendentals=QUERIES * (KEYS + CAP) * HEADS_HERE,
         ),
-    )(q, ka, kb, kf, va, vb, vf, bias)
+    )(q, kv, kv, kf, vf, jnp.asarray(hot, bf16), bias)
 
 
 def project_kernel(part_ref, w_ref, out_ref, w_vmem, sem):
@@ -243,33 +261,14 @@
     z, yh, c = (lax.axis_index(a) for a in ("z", "yh", "c"))
     own_head = lax.axis_index("yl") * NX + lax.axis_index("x")
 
-    def spread(x):
-        return swap(jnp.broadcast_to(x[None], (NZ, CAP, GROUP)), "z").reshape(FAR, GROUP)
-
-    def other_core(x):
-        return lax.ppermute(x, "c", [(0, 1), (1, 0)])
-
-    ka, va = spread(sk), spread(sv)
-    kb, vb = other_core(ka), other_core(va)
-    query, kf, vf = unpack(swap(pack(fq, fk, fv), HEAD))
-    queries = lax.all_gather(query, "yh", axis=0)
-
-    table = lengths.reshape(NZ, NY, NC)
-    mine = lax.dynamic_slice_in_dim(table, yh, 1, 1)[:, 0, :]
-    own_core = jnp.where(c == 0, mine[:, 0], mine[:, 1])
-    far_core = jnp.where(c == 0, mine[:, 1], mine[:, 0])
-    own_length = jnp.sum(jnp.where(jnp.arange(NZ) == z, own_core, 0))
-    slots = jnp.arange(CAP, dtype=jnp.int32)
-    is_mine = (jnp.arange(NY) == yh)[:, None, None]
-    stale_here = (jnp.arange(NZ) == z)[None, :, None]
-    live_a = (slots[None, None, :] < own_core[None, :, None]) & ~(is_mine & stale_here)
-    live_b = jnp.broadcast_to(slots[None, None, :] < far_core[None, :, None], (NY, NZ, CAP))
-    live_f = (jnp.asarray(row_tokens())[None, :] < own_length) & is_mine[:, :, 0]
-    live = jnp.concatenate([live_a.reshape(NY, FAR), live_b.reshape(NY, FAR), live_f, jnp.zeros((NY, HD - CAP), bool)], axis=1)
-    bias = jnp.where(live, 0.0, BIG).astype(f32)[:, None, :]
-
-    parts = attention(queries, ka, kb, kf, va, vb, vf, bias)
-    packed = project(swap(parts, "yh"), w)
+    place = jnp.stack([z, yh, c]).astype(jnp.int32)
+    kv = lax.all_gather(jnp.concatenate([sk, sv], axis=1), ("z", "c"), axis=0, tiled=True)
+    query, kf, vf, bias = unpack(place, lengths, swap(pack(fq, fk, fv), HEAD))
+    queries = lax.all_gather(query, "yh", axis=0, tiled=True)
+    parts = attention(queries, kv, kf, vf, bias)
+    parts = swap(parts.reshape(NY, CAP, GROUP + HD), "yh")
+    packed = project(parts, w)
+    own_length = lax.dynamic_index_in_dim(lengths, (z * NY + yh) * NC + c, 0, keepdims=False)
     limit = jnp.clip(own_length - own_head * OWN, 0, OWN)[None]
     return mix(limit, swap(packed, HEAD), hidden, gate[None, :])
 

time: 137 us -> 114 us (0.83)
  the two profiles are of different devices: /device:TPU:8 before, /device:TPU:16 now
where the time goes in v2:
time: 114 us
  blocking collectives  37.6 us (33%)
  waiting for transfers between devices  33.1 us (29%)
  between operations  14.1 us (12%)
  Pallas kernels  10.9 us (10%)
  starting transfers between devices  9.77 us (9%)
  local copies, waits for them, and re-layouts  6.75 us (6%)
  other arithmetic  1.71 us (2%)
    all_to_all x1, blocking collectives, swap(): return lax.all_to_all(x, axis, split_axis=0, concat_axis=0, tiled=True)  21.8 us
    all_gather x1, waiting for transfers between devices, local(): lax.all_gather(jnp.concatenate([sk, sv], axis=1), ('z', 'c'), axis=0, til...  16.9 us
    all_to_all x2, waiting for transfers between devices, swap(): return lax.all_to_all(x, axis, split_axis=0, concat_axis=0, tiled=True)  16.2 us
    all_gather x1, blocking collectives, local(): queries = lax.all_gather(query, 'yh', axis=0, tiled=True)  15.7 us
    all_to_all x2, starting transfers between devices, swap(): return lax.all_to_all(x, axis, split_axis=0, concat_axis=0, tiled=True)  9.77 us
    pallas_call x1, Pallas kernels, attention(): pl.pallas_call(attention_kernel, grid=(HEADS_HERE,), in_specs=[column(QUE...  6.55 us
    unnamed x20, local copies, waits for them, and re-layouts  6.17 us
  transfers between devices with their start and end apart: 3, of which 3 were waited for; matrix products, arithmetic and copies ran while one was open for 1% of the time, Pallas kernels for 1%

profile of v2, /device:TPU:16, one launch (start us, length us, event | category | flops | bytes accessed | tf_op | source)
XLA Modules:
  0.0 113.9 jit_solution(12942555325009512010)
XLA Ops:
  6.5 0.0 all-gather.2.cloned.1.call-start
  6.5 1.6 %pad_maximum_fusion = bf16[96,1024]{1,0:T(8,128)(2,1)} fusion(bf16[96,512]{1,0:T(8,128)(2,1)} %param.14, bf16[96,512]{1,0:T(8,128)(2,1)} %param.13), kind=kLoop, calls=%fused_computation | loop fusion | flops 393216 | bytes 393216 | tf_op jit(solution)/shard_map/concatenate | solution.py:265
  8.2 0.0 all-gather.2.cloned.1.call-update
  8.2 0.0 copy-start.2
  8.2 0.9 copy-done.2
  9.1 0.0 copy-start.3
  9.1 0.9 copy-done.3
  10.0 0.9 copy-done.4
  10.9 0.8 shard_map.100
  11.7 5.3 %all-to-all-start = ((bf16[8,16,1152]{2,1,0:T(8,128)(2,1)}), bf16[8,16,1152]{2,1,0:T(8,128)(2,1)S(1)}, u32[]{:S(2)}, u32[]{:S(2)}) async-start(bf16[8,16,1152]{2,1,0:T(8,128)(2,1)} %shard_map.100), calls=%async_computation | async-start | bytes 589824 | tf_op jit(solution)/shard_map/all_to_all | solution.py:257
  17.0 0.1 pad_add_fusion.place_ref
  17.1 7.4 %all-to-all-done.in_ref = bf16[8,16,1152]{2,1,0:T(8,128)(2,1)S(1)} async-done(((bf16[8,16,1152]{2,1,0:T(8,128)(2,1)}), bf16[8,16,1152]{2,1,0:T(8,128)(2,1)S(1)}, u32[]{:S(2)}, u32[]{:S(2)}) %all-to-all-start) | async-done | bytes 294944 | tf_op jit(solution)/shard_map/all_to_all | solution.py:257
  24.6 0.7 copy-done.8
  25.2 0.7 shard_map.101
  25.9 15.7 %all_gather.6.q_ref = bf16[384,512]{1,0:T(8,128)(2,1)S(1)} all-gather(bf16[96,512]{1,0:T(8,128)(2,1)S(1)} %get-tuple-element.9), channel_id=1, replica_groups=mesh['z'=8,'yh'=4,'c'=2,'yl'=2,'x'=4] {'yh'}, dimensions={0}, use_global_device_ids=true | all-gather | bytes 491520 | tf_op jit(solution)/shard_map/all_gather | solution.py:267
  41.6 16.9 %all-gather.2.cloned.1.call-done.k_ref.v_ref = bf16[1536,1024]{1,0:T(8,128)(2,1)} async-done(((bf16[96,1024]{1,0:T(8,128)(2,1)}), bf16[1536,1024]{1,0:T(8,128)(2,1)}) %all-gather.2.cloned.1.call-update) | async-done | bytes 3145744 | tf_op jit(solution)/shard_map/all_gather | solution.py:265
  58.5 1.9 %copy-done = bf16[1536,1024]{1,0:T(8,128)(2,1)S(1)} copy-done((bf16[1536,1024]{1,0:T(8,128)(2,1)S(1)}, bf16[1536,1024]{1,0:T(8,128)(2,1)}, u32[]{:S(2)}) %copy-start) | copy-done | bytes 3145752
  60.4 0.9 copy-done.5
  61.3 6.6 %shard_map.102 = bf16[384,640]{1,0:T(8,128)(2,1)S(1)} custom-call(bf16[384,512]{1,0:T(8,128)(2,1)S(1)} %all_gather.6.q_ref, bf16[1536,1024]{1,0:T(8,128)(2,1)S(1)} %copy-done, bf16[1536,1024]{1,0:T(8,128)(2,1)S(1)} %copy-done, bf16[96,512]{1,0:T(8,128)(2,1)S(1)} %get-tuple-element.10.kf_ref, bf16[96,512]{1,0:T(8,128)(2,1)S(1)} %get-tuple-element.11.vf_ref, ...), custom_call_target="tpu_custom_call" | custom-call | flops 1283457024 | bytes 3145728 | tf_op jit(solution)/shard_map/pallas_call | solution.py:156
  67.8 0.0 copy-start.9
  67.8 0.0 copy-start.6
  67.8 0.0 copy-start.7
  67.9 21.8 %all_to_all.15.part_ref = bf16[4,96,640]{2,1,0:T(8,128)(2,1)S(1)} all-to-all(bf16[4,96,640]{2,1,0:T(8,128)(2,1)S(1)} %bitcast.7), channel_id=1, replica_groups=mesh['z'=8,'yh'=4,'c'=2,'yl'=2,'x'=4] {'yh'}, dimensions={0} | all-to-all | bytes 983040 | tf_op jit(solution)/shard_map/all_to_all | solution.py:257
  89.7 0.0 copy-done.1
  89.7 2.1 %shard_map.103 = bf16[8,16,2304]{2,1,0:T(8,128)(2,1)} custom-call(bf16[4,96,640]{2,1,0:T(8,128)(2,1)S(1)} %all_to_all.15.part_ref, bf16[512,3072]{1,0:T(8,128)(2,1)S(1)} %copy-done.1), custom_call_target="tpu_custom_call" | custom-call | tf_op jit(solution)/shard_map/pallas_call | solution.py:220
  91.8 4.5 %all-to-all-start.2 = ((bf16[8,16,2304]{2,1,0:T(8,128)(2,1)}), bf16[8,16,2304]{2,1,0:T(8,128)(2,1)S(1)}, u32[]{:S(2)}, u32[]{:S(2)}) async-start(bf16[8,16,2304]{2,1,0:T(8,128)(2,1)} %shard_map.103), calls=%async_computation.2 | async-start | bytes 1179648 | tf_op jit(solution)/shard_map/all_to_all | solution.py:257
  96.3 0.0 copy-done.9
  96.3 0.6 dynamic_slice.4
  97.5 8.8 %all-to-all-done.2.in_ref = bf16[8,16,2304]{2,1,0:T(8,128)(2,1)S(1)} async-done(((bf16[8,16,2304]{2,1,0:T(8,128)(2,1)}), bf16[8,16,2304]{2,1,0:T(8,128)(2,1)S(1)}, u32[]{:S(2)}, u32[]{:S(2)}) %all-to-all-start.2) | async-done | bytes 589856 | tf_op jit(solution)/shard_map/all_to_all | solution.py:257
  106.3 0.0 copy-done.6
  106.3 0.0 copy-done.7
  106.3 0.7 shard_map.104
  (5 shorter events, 0.0 us)
Async XLA Ops:
  6.5 51.9 %all-gather.2.cloned.1.call-start = ((), (), s32[]{:S(2)}) async-start(), calls=%async_computation.3 | async-start | bytes 3342336 | tf_op jit(solution)/shard_map/all_gather | solution.py:265
  8.2 0.9 copy-start.2
  9.1 0.9 copy-start.3
  10.0 0.9 copy-start.4
  11.7 12.8 %all-to-all-start = ((bf16[8,16,1152]{2,1,0:T(8,128)(2,1)}), bf16[8,16,1152]{2,1,0:T(8,128)(2,1)S(1)}, u32[]{:S(2)}, u32[]{:S(2)}) async-start(bf16[8,16,1152]{2,1,0:T(8,128)(2,1)} %shard_map.100), calls=%async_computation | async-start | bytes 589824 | tf_op jit(solution)/shard_map/all_to_all | solution.py:257
  24.6 0.7 copy-start.8
  58.5 1.9 %copy-start = (bf16[1536,1024]{1,0:T(8,128)(2,1)S(1)}, bf16[1536,1024]{1,0:T(8,128)(2,1)}, u32[]{:S(2)}) copy-start(bf16[1536,1024]{1,0:T(8,128)(2,1)} %all-gather.2.cloned.1.call-done.k_ref.v_ref) | copy-start | bytes 9437188
  60.4 0.9 copy-start.5
  61.3 28.4 %copy-start.1 = (bf16[512,3072]{1,0:T(8,128)(2,1)S(1)}, bf16[512,3072]{1,0:T(8,128)(2,1)}, u32[]{:S(2)}) copy-start(bf16[512,3072]{1,0:T(8,128)(2,1)} %w_ref.1) | copy-start | bytes 9437188
  67.8 28.5 %copy-start.9 = (s32[64]{0:T(128)S(1)}, s32[64]{0:T(128)}, u32[]{:S(2)}) copy-start(s32[64]{0:T(128)} %lengths_ref.1) | copy-start | bytes 772
  67.8 38.5 %copy-start.6 = (bf16[12,3072]{1,0:T(8,128)(2,1)S(1)}, bf16[12,3072]{1,0:T(8,128)(2,1)}, u32[]{:S(2)}) copy-start(bf16[12,3072]{1,0:T(8,128)(2,1)} %hidden_ref.1) | copy-start | bytes 221188
  67.8 38.5 %copy-start.7 = (f32[3072]{0:T(1024)S(1)}, f32[3072]{0:T(1024)}, u32[]{:S(2)}) copy-start(f32[3072]{0:T(1024)} %param.17) | copy-start | bytes 36868
  91.8 14.5 %all-to-all-start.2 = ((bf16[8,16,2304]{2,1,0:T(8,128)(2,1)}), bf16[8,16,2304]{2,1,0:T(8,128)(2,1)S(1)}, u32[]{:S(2)}, u32[]{:S(2)}) async-start(bf16[8,16,2304]{2,1,0:T(8,128)(2,1)} %shard_map.103), calls=%async_computation.2 | async-start | bytes 1179648 | tf_op jit(solution)/shard_map/all_to_all | solution.py:257
Sparse Core Ops, SparseCore 0:
  9.5 48.9 all-gather.1

commit v3 on v2

--- a/solution.py
+++ b/solution.py
@@ -17,6 +17,7 @@
 KEYS = NZ * NC * CAP
 QUERIES = NY * CAP
 BIG = -1e30
+TOGETHER = 2
 EXP2_SCALE = float(np.log2(np.e) * HD ** (-0.5))
 HEAD = ("yl", "x")
 ALL = ("z", "yh", "c", "yl", "x")
@@ -53,7 +54,7 @@
     return pl.pallas_call(
         pack_kernel,
         out_shape=jax.ShapeDtypeStruct((NHEAD, 16, PACKED), bf16),
-        compiler_params=params(16),
+        compiler_params=params(60),
     )(fq, fk, fv)
 
 
@@ -106,39 +107,47 @@
 
 
 def attention_kernel(q_ref, k_ref, v_ref, kf_ref, vf_ref, hot_ref, bias_ref, out_ref):
-    h = pl.program_id(0)
+    g = pl.program_id(0)
     lane = lax.broadcasted_iota(jnp.int32, (QUERIES, HD), 1)
-    query = jnp.concatenate([q_ref[...], hot_ref[...]], axis=1)
+    stat = jnp.zeros((QUERIES, HD), f32)
     chunk = KEYS // 4
-    pieces = [(k_ref[i:i + chunk], v_ref[i:i + chunk], bias_ref[i:i + chunk]) for i in range(0, KEYS, chunk)]
-    pieces.append((kf_ref[...], vf_ref[...], bias_ref[KEYS:]))
-    scores = []
-    for key, _, bias in pieces:
-        key = jnp.concatenate([key, bias], axis=1)
-        scores.append(lax.dot_general(query, key, (((1,), (1,)), ((), ())), preferred_element_type=f32))
-    top = scores[0].max(axis=1, keepdims=True)
-    for s in scores[1:]:
-        top = jnp.maximum(top, s.max(axis=1, keepdims=True))
-    total = jnp.zeros((QUERIES, 1), f32)
-    accum = jnp.zeros((QUERIES, HD), f32)
-    for s, (_, value, _) in zip(scores, pieces):
-        weights = jnp.exp2((s - top) * EXP2_SCALE)
-        total = total + weights.sum(axis=1, keepdims=True)
-        accum = accum + jnp.dot(weights.astype(bf16), value, preferred_element_type=f32)
-    out_ref[:, pl.ds(pl.multiple_of(h * HD, HD), HD)] = (accum / total).astype(bf16)
-    level = top * EXP2_SCALE + jnp.log2(total)
-    hi = level.astype(bf16).astype(f32)
-    mid = (level - hi).astype(bf16).astype(f32)
-    low = level - hi - mid
-    stat = jnp.where(lane == 3 * h, hi, 0.0)
-    stat = jnp.where(lane == 3 * h + 1, mid, stat)
-    stat = jnp.where(lane == 3 * h + 2, low, stat).astype(bf16)
-
-    @pl.when(h == 0)
+    for i in range(TOGETHER):
+        cols = slice(i * HD, (i + 1) * HD)
+        query = jnp.concatenate([q_ref[:, cols], hot_ref[...]], axis=1)
+        pieces = [
+            (k_ref[j:j + chunk, cols], v_ref[j:j + chunk, cols], bias_ref[j:j + chunk])
+            for j in range(0, KEYS, chunk)
+        ]
+        pieces.append((kf_ref[:, cols], vf_ref[:, cols], bias_ref[KEYS:]))
+        scores = []
+        for key, _, bias in pieces:
+            key = jnp.concatenate([key, bias], axis=1)
+            scores.append(lax.dot_general(query, key, (((1,), (1,)), ((), ())), preferred_element_type=f32))
+        top = scores[0].max(axis=1, keepdims=True)
+        for s in scores[1:]:
+            top = jnp.maximum(top, s.max(axis=1, keepdims=True))
+        total = jnp.zeros((QUERIES, 1), f32)
+        accum = jnp.zeros((QUERIES, HD), f32)
+        for s, (_, value, _) in zip(scores, pieces):
+            weights = jnp.exp2((s - top) * EXP2_SCALE)
+            total = total + weights.sum(axis=1, keepdims=True)
+            accum = accum + jnp.dot(weights.astype(bf16), value, preferred_element_type=f32)
+        h = g * TOGETHER + i
+        out_ref[:, pl.ds(pl.multiple_of(h * HD, HD), HD)] = (accum / total).astype(bf16)
+        level = top * EXP2_SCALE + jnp.log2(total)
+        hi = level.astype(bf16).astype(f32)
+        mid = (level - hi).astype(bf16).astype(f32)
+        low = level - hi - mid
+        stat = jnp.where(lane == 3 * h, hi, stat)
+        stat = jnp.where(lane == 3 * h + 1, mid, stat)
+        stat = jnp.where(lane == 3 * h + 2, low, stat)
+    stat = stat.astype(bf16)
+
+    @pl.when(g == 0)
     def _():
         out_ref[:, GROUP:] = stat
 
-    @pl.when(h != 0)
+    @pl.when(g != 0)
     def _():
         out_ref[:, GROUP:] = out_ref[:, GROUP:] + stat
 
@@ -146,23 +155,24 @@
 def attention(q, kv, kf, vf, bias):
     hot = np.zeros((QUERIES, HD), np.float32)
     hot[np.arange(QUERIES), np.arange(QUERIES) // CAP] = 1
+    steps = HEADS_HERE // TOGETHER
 
     def column(rows, skip=0):
-        return pl.BlockSpec((rows, HD), lambda h: (0, h + skip))
+        return pl.BlockSpec((rows, TOGETHER * HD), lambda g: (0, g + skip))
 
     def whole(rows, cols):
-        return pl.BlockSpec((rows, cols), lambda h: (0, 0))
+        return pl.BlockSpec((rows, cols), lambda g: (0, 0))
 
     return pl.pallas_call(
         attention_kernel,
-        grid=(HEADS_HERE,),
+        grid=(steps,),
         in_specs=[
-            column(QUERIES), column(KEYS), column(KEYS, HEADS_HERE), column(CAP), column(CAP),
+            column(QUERIES), column(KEYS), column(KEYS, steps), column(CAP), column(CAP),
             whole(QUERIES, HD), whole(KEYS + CAP, HD),
         ],
         out_specs=whole(QUERIES, GROUP + HD),
         out_shape=jax.ShapeDtypeStruct((QUERIES, GROUP + HD), bf16),
-        compiler_params=params(40),
+        compiler_params=params(60),
         cost_estimate=pl.CostEstimate(
             flops=4 * QUERIES * (KEYS + CAP) * GROUP,
             bytes_accessed=4 * KEYS * GROUP,
@@ -171,9 +181,7 @@
     )(q, kv, kv, kf, vf, jnp.asarray(hot, bf16), bias)
 
 
-def project_kernel(part_ref, w_ref, out_ref, w_vmem, sem):
-    copy = pltpu.make_async_copy(w_ref, w_vmem, sem)
-    copy.start()
+def project_kernel(part_ref, w_ref, out_ref):
     stats = [part_ref[b, :, GROUP:].astype(f32) for b in range(NY)]
     heads = []
     for h in range(HEADS_HERE):
@@ -189,13 +197,12 @@
             accum = accum + weight * part_ref[b, :, h * HD:(h + 1) * HD].astype(f32)
         heads.append((accum / total).astype(bf16))
     attended = jnp.concatenate(heads, axis=1)
-    copy.wait()
     half = D // 2
     step = 384
     mask = lower_half((8, step))
     for j in range(half // step):
-        left = jnp.dot(attended, w_vmem[:, j * step:(j + 1) * step], preferred_element_type=f32)
-        right = jnp.dot(attended, w_vmem[:, half + j * step:half + (j + 1) * step], preferred_element_type=f32)
+        left = jnp.dot(attended, w_ref[:, j * step:(j + 1) * step], preferred_element_type=f32)
+        right = jnp.dot(attended, w_ref[:, half + j * step:half + (j + 1) * step], preferred_element_type=f32)
         for s in range(NHEAD):
             k = s // 2
             a = left[64 + 8 * k:72 + 8 * k]
@@ -219,10 +226,9 @@
 def project(parts, w):
     return pl.pallas_call(
         project_kernel,
-        in_specs=[pl.BlockSpec(memory_space=pltpu.VMEM), pl.BlockSpec(memory_space=pl.ANY)],
+        in_specs=[pl.BlockSpec(memory_space=pltpu.VMEM)] * 2,
         out_specs=pl.BlockSpec(memory_space=pltpu.VMEM),
         out_shape=jax.ShapeDtypeStruct((NHEAD, 16, OUT_PACKED), bf16),
-        scratch_shapes=[pltpu.VMEM((GROUP, D), bf16), pltpu.SemaphoreType.DMA],
         compiler_params=params(24),
     )(parts, w)
 

time: 114 us -> 113 us (level)
  the two profiles are of different devices: /device:TPU:16 before, /device:TPU:8 now
where the time goes in v3:
time: 113 us
  blocking collectives  37.4 us (33%)
  waiting for transfers between devices  26.9 us (24%)
  starting transfers between devices  16.3 us (14%)
  between operations  14.1 us (12%)
  Pallas kernels  13.2 us (12%)
  local copies, waits for them, and re-layouts  3.27 us (3%)
  other arithmetic  1.7 us (2%)
    all_to_all x1, blocking collectives, swap(): return lax.all_to_all(x, axis, split_axis=0, concat_axis=0, tiled=True)  21 us
    all_gather x1, blocking collectives, local(): queries = lax.all_gather(query, 'yh', axis=0, tiled=True)  16.4 us
    all_to_all x2, starting transfers between devices, swap(): return lax.all_to_all(x, axis, split_axis=0, concat_axis=0, tiled=True)  16.3 us
    all_gather x1, waiting for transfers between devices, local(): lax.all_gather(jnp.concatenate([sk, sv], axis=1), ('z', 'c'), axis=0, til...  13.6 us
    all_to_all x2, waiting for transfers between devices, swap(): return lax.all_to_all(x, axis, split_axis=0, concat_axis=0, tiled=True)  13.2 us
    pallas_call x1, Pallas kernels, attention(): pl.pallas_call(attention_kernel, grid=(steps,), in_specs=[column(QUERIES)...  7.98 us
    unnamed x16, local copies, waits for them, and re-layouts  2.69 us
  transfers between devices with their start and end apart: 3, of which 3 were waited for; matrix products, arithmetic and copies ran while one was open for 1% of the time, Pallas kernels for 2%

profile of v3, /device:TPU:8, one launch (start us, length us, event | category | flops | bytes accessed | tf_op | source)
XLA Modules:
  0.0 112.8 jit_solution(2231357030318069322)
XLA Ops:
  6.5 0.0 all-gather.2.cloned.1.call-start
  6.5 1.6 %pad_maximum_fusion = bf16[96,1024]{1,0:T(8,128)(2,1)} fusion(bf16[96,512]{1,0:T(8,128)(2,1)} %param.14, bf16[96,512]{1,0:T(8,128)(2,1)} %param.13), kind=kLoop, calls=%fused_computation | loop fusion | flops 393216 | bytes 393216 | tf_op jit(solution)/shard_map/concatenate | solution.py:271
  8.2 0.0 all-gather.2.cloned.1.call-update
  8.2 1.8 %shard_map.100 = bf16[8,16,1152]{2,1,0:T(8,128)(2,1)} custom-call(bf16[12,4096]{1,0:T(8,128)(2,1)} %q_ref.1, bf16[12,4096]{1,0:T(8,128)(2,1)} %k_ref.1, bf16[12,4096]{1,0:T(8,128)(2,1)} %v_ref.1), custom_call_target="tpu_custom_call" | custom-call | tf_op jit(solution)/shard_map/pallas_call | solution.py:54
  10.0 9.2 %all-to-all-start = ((bf16[8,16,1152]{2,1,0:T(8,128)(2,1)}), bf16[8,16,1152]{2,1,0:T(8,128)(2,1)S(1)}, u32[]{:S(2)}, u32[]{:S(2)}) async-start(bf16[8,16,1152]{2,1,0:T(8,128)(2,1)} %shard_map.100), calls=%async_computation | async-start | bytes 589824 | tf_op jit(solution)/shard_map/all_to_all | solution.py:263
  19.2 0.1 pad_add_fusion.place_ref
  19.3 5.9 %all-to-all-done.in_ref = bf16[8,16,1152]{2,1,0:T(8,128)(2,1)S(1)} async-done(((bf16[8,16,1152]{2,1,0:T(8,128)(2,1)}), bf16[8,16,1152]{2,1,0:T(8,128)(2,1)S(1)}, u32[]{:S(2)}, u32[]{:S(2)}) %all-to-all-start) | async-done | bytes 294944 | tf_op jit(solution)/shard_map/all_to_all | solution.py:263
  25.2 0.0 copy-start.6
  25.2 0.7 copy-done.6
  25.9 0.7 shard_map.101
  26.5 0.0 copy-start.1
  26.5 0.7 copy-done.1
  27.3 0.0 copy-start.2
  27.3 0.6 copy-done.2
  27.9 0.0 copy-start.3
  27.9 0.6 copy-done.3
  28.6 16.4 %all_gather.6.q_ref = bf16[384,512]{1,0:T(8,128)(2,1)} all-gather(bf16[96,512]{1,0:T(8,128)(2,1)S(1)} %get-tuple-element.9), channel_id=1, replica_groups=mesh['z'=8,'yh'=4,'c'=2,'yl'=2,'x'=4] {'yh'}, dimensions={0}, use_global_device_ids=true | all-gather | bytes 491520 | tf_op jit(solution)/shard_map/all_gather | solution.py:273
  45.0 13.6 %all-gather.2.cloned.1.call-done.k_ref.v_ref = bf16[1536,1024]{1,0:T(8,128)(2,1)} async-done(((bf16[96,1024]{1,0:T(8,128)(2,1)}), bf16[1536,1024]{1,0:T(8,128)(2,1)}) %all-gather.2.cloned.1.call-update) | async-done | bytes 3145744 | tf_op jit(solution)/shard_map/all_gather | solution.py:271
  58.6 0.0 copy-start
  58.6 8.0 %shard_map.102 = bf16[384,640]{1,0:T(8,128)(2,1)} custom-call(bf16[384,512]{1,0:T(8,128)(2,1)} %all_gather.6.q_ref, bf16[1536,1024]{1,0:T(8,128)(2,1)} %all-gather.2.cloned.1.call-done.k_ref.v_ref, bf16[1536,1024]{1,0:T(8,128)(2,1)} %all-gather.2.cloned.1.call-done.k_ref.v_ref, bf16[96,512]{1,0:T(8,128)(2,1)} %copy-done.2, bf16[96,512]{1,0:T(8,128)(2,1)} %copy-done.3, ...), custom_call_target="tpu_custom_call" | custom-call | flops 1283457024 | bytes 3145728 | tf_op jit(solution)/shard_map/pallas_call | solution.py:166
  66.6 0.0 copy-start.7
  66.6 0.0 copy-start.5
  66.6 21.0 %all_to_all.15.part_ref = bf16[4,96,640]{2,1,0:T(8,128)(2,1)S(1)} all-to-all(bf16[4,96,640]{2,1,0:T(8,128)(2,1)} %bitcast.8), channel_id=1, replica_groups=mesh['z'=8,'yh'=4,'c'=2,'yl'=2,'x'=4] {'yh'}, dimensions={0} | all-to-all | bytes 983040 | tf_op jit(solution)/shard_map/all_to_all | solution.py:263
  87.5 0.0 copy-done
  87.5 1.9 %shard_map.103 = bf16[8,16,2304]{2,1,0:T(8,128)(2,1)} custom-call(bf16[4,96,640]{2,1,0:T(8,128)(2,1)S(1)} %all_to_all.15.part_ref, bf16[512,3072]{1,0:T(8,128)(2,1)S(1)} %copy-done), custom_call_target="tpu_custom_call" | custom-call | tf_op jit(solution)/shard_map/pallas_call | solution.py:227
  89.5 7.1 %all-to-all-start.2 = ((bf16[8,16,2304]{2,1,0:T(8,128)(2,1)}), bf16[8,16,2304]{2,1,0:T(8,128)(2,1)S(1)}, u32[]{:S(2)}, u32[]{:S(2)}) async-start(bf16[8,16,2304]{2,1,0:T(8,128)(2,1)} %shard_map.103), calls=%async_computation.2 | async-start | bytes 1179648 | tf_op jit(solution)/shard_map/all_to_all | solution.py:263
  96.6 0.0 copy-done.7
  96.6 0.6 dynamic_slice.4
  97.9 7.3 %all-to-all-done.2.in_ref = bf16[8,16,2304]{2,1,0:T(8,128)(2,1)S(1)} async-done(((bf16[8,16,2304]{2,1,0:T(8,128)(2,1)}), bf16[8,16,2304]{2,1,0:T(8,128)(2,1)S(1)}, u32[]{:S(2)}, u32[]{:S(2)}) %all-to-all-start.2) | async-done | bytes 589856 | tf_op jit(solution)/shard_map/all_to_all | solution.py:263
  105.2 0.0 copy-done.4
  105.2 0.0 copy-done.5
  105.2 0.7 shard_map.104
  (1 shorter events, 0.0 us)
Async XLA Ops:
  6.5 52.1 %all-gather.2.cloned.1.call-start = ((), (), s32[]{:S(2)}) async-start(), calls=%async_computation.3 | async-start | bytes 3342336 | tf_op jit(solution)/shard_map/all_gather | solution.py:271
  10.0 15.2 %all-to-all-start = ((bf16[8,16,1152]{2,1,0:T(8,128)(2,1)}), bf16[8,16,1152]{2,1,0:T(8,128)(2,1)S(1)}, u32[]{:S(2)}, u32[]{:S(2)}) async-start(bf16[8,16,1152]{2,1,0:T(8,128)(2,1)} %shard_map.100), calls=%async_computation | async-start | bytes 589824 | tf_op jit(solution)/shard_map/all_to_all | solution.py:263
  25.2 0.7 copy-start.6
  26.5 0.8 copy-start.1
  27.3 0.6 copy-start.2
  27.9 0.6 copy-start.3
  58.6 29.0 %copy-start = (bf16[512,3072]{1,0:T(8,128)(2,1)S(1)}, bf16[512,3072]{1,0:T(8,128)(2,1)}, u32[]{:S(2)}) copy-start(bf16[512,3072]{1,0:T(8,128)(2,1)} %w_ref.1) | copy-start | bytes 9437188
  66.6 30.1 %copy-start.7 = (s32[64]{0:T(128)S(1)}, s32[64]{0:T(128)}, u32[]{:S(2)}) copy-start(s32[64]{0:T(128)} %lengths_ref.1) | copy-start | bytes 772
  66.6 38.6 %copy-start.4 = (bf16[12,3072]{1,0:T(8,128)(2,1)S(1)}, bf16[12,3072]{1,0:T(8,128)(2,1)}, u32[]{:S(2)}) copy-start(bf16[12,3072]{1,0:T(8,128)(2,1)} %hidden_ref.1) | copy-start | bytes 221188
  66.6 38.6 %copy-start.5 = (f32[3072]{0:T(1024)S(1)}, f32[3072]{0:T(1024)}, u32[]{:S(2)}) copy-start(f32[3072]{0:T(1024)} %param.17) | copy-start | bytes 36868
  89.5 15.7 %all-to-all-start.2 = ((bf16[8,16,2304]{2,1,0:T(8,128)(2,1)}), bf16[8,16,2304]{2,1,0:T(8,128)(2,1)S(1)}, u32[]{:S(2)}, u32[]{:S(2)}) async-start(bf16[8,16,2304]{2,1,0:T(8,128)(2,1)} %shard_map.103), calls=%async_computation.2 | async-start | bytes 1179648 | tf_op jit(solution)/shard_map/all_to_all | solution.py:263
Sparse Core Ops, SparseCore 0:
  9.5 49.0 all-gather.1

commit v4 on v3

--- a/solution.py
+++ b/solution.py
@@ -18,6 +18,8 @@
 QUERIES = NY * CAP
 BIG = -1e30
 TOGETHER = 2
+STAT_ROWS = 16
+RETURNED = HEADS_HERE * CAP + STAT_ROWS
 EXP2_SCALE = float(np.log2(np.e) * HD ** (-0.5))
 HEAD = ("yl", "x")
 ALL = ("z", "yh", "c", "yl", "x")
@@ -106,7 +108,7 @@
     )(place, lengths, received)
 
 
-def attention_kernel(q_ref, k_ref, v_ref, kf_ref, vf_ref, hot_ref, bias_ref, out_ref):
+def attention_kernel(q_ref, k_ref, v_ref, kf_ref, vf_ref, hot_ref, bias_ref, out_ref, stat_ref):
     g = pl.program_id(0)
     lane = lax.broadcasted_iota(jnp.int32, (QUERIES, HD), 1)
     stat = jnp.zeros((QUERIES, HD), f32)
@@ -133,7 +135,9 @@
             total = total + weights.sum(axis=1, keepdims=True)
             accum = accum + jnp.dot(weights.astype(bf16), value, preferred_element_type=f32)
         h = g * TOGETHER + i
-        out_ref[:, pl.ds(pl.multiple_of(h * HD, HD), HD)] = (accum / total).astype(bf16)
+        result = (accum / total).astype(bf16)
+        for b in range(NY):
+            out_ref[b, pl.ds(pl.multiple_of(h * CAP, 32), CAP), :] = result[b * CAP:(b + 1) * CAP]
         level = top * EXP2_SCALE + jnp.log2(total)
         hi = level.astype(bf16).astype(f32)
         mid = (level - hi).astype(bf16).astype(f32)
@@ -141,15 +145,21 @@
         stat = jnp.where(lane == 3 * h, hi, stat)
         stat = jnp.where(lane == 3 * h + 1, mid, stat)
         stat = jnp.where(lane == 3 * h + 2, low, stat)
-    stat = stat.astype(bf16)
 
     @pl.when(g == 0)
     def _():
-        out_ref[:, GROUP:] = stat
+        stat_ref[...] = stat
 
     @pl.when(g != 0)
     def _():
-        out_ref[:, GROUP:] = out_ref[:, GROUP:] + stat
+        stat_ref[...] = stat_ref[...] + stat
+
+    @pl.when(g == pl.num_programs(0) - 1)
+    def _():
+        for b in range(NY):
+            rows = stat_ref[b * CAP:(b + 1) * CAP]
+            square = jnp.concatenate([rows, jnp.zeros((HD - CAP, HD), f32)], axis=0)
+            out_ref[b, HEADS_HERE * CAP:, :] = square.T[:STAT_ROWS].astype(bf16)
 
 
 def attention(q, kv, kf, vf, bias):
@@ -170,8 +180,9 @@
             column(QUERIES), column(KEYS), column(KEYS, steps), column(CAP), column(CAP),
             whole(QUERIES, HD), whole(KEYS + CAP, HD),
         ],
-        out_specs=whole(QUERIES, GROUP + HD),
-        out_shape=jax.ShapeDtypeStruct((QUERIES, GROUP + HD), bf16),
+        out_specs=pl.BlockSpec((NY, RETURNED, HD), lambda g: (0, 0, 0)),
+        out_shape=jax.ShapeDtypeStruct((NY, RETURNED, HD), bf16),
+        scratch_shapes=[pltpu.VMEM((QUERIES, HD), f32)],
         compiler_params=params(60),
         cost_estimate=pl.CostEstimate(
             flops=4 * QUERIES * (KEYS + CAP) * GROUP,
@@ -182,20 +193,26 @@
 
 
 def project_kernel(part_ref, w_ref, out_ref):
-    stats = [part_ref[b, :, GROUP:].astype(f32) for b in range(NY)]
-    heads = []
+    stats = [part_ref[b, HEADS_HERE * CAP:, :].astype(f32) for b in range(NY)]
+    shares = []
     for h in range(HEADS_HERE):
-        levels = [s[:, 3 * h:3 * h + 1] + s[:, 3 * h + 1:3 * h + 2] + s[:, 3 * h + 2:3 * h + 3] for s in stats]
+        levels = [s[3 * h:3 * h + 1] + s[3 * h + 1:3 * h + 2] + s[3 * h + 2:3 * h + 3] for s in stats]
         top = levels[0]
         for level in levels[1:]:
             top = jnp.maximum(top, level)
-        total = jnp.zeros((CAP, 1), f32)
+        weights = [jnp.exp2(level - top) for level in levels]
+        total = weights[0]
+        for weight in weights[1:]:
+            total = total + weight
+        shares += [weight / total for weight in weights]
+    shares = jnp.concatenate(shares + [jnp.zeros((HD - len(shares), HD), f32)], axis=0).T
+    heads = []
+    for h in range(HEADS_HERE):
         accum = jnp.zeros((CAP, HD), f32)
         for b in range(NY):
-            weight = jnp.exp2(levels[b] - top)
-            total = total + weight
-            accum = accum + weight * part_ref[b, :, h * HD:(h + 1) * HD].astype(f32)
-        heads.append((accum / total).astype(bf16))
+            share = shares[:CAP, h * NY + b:h * NY + b + 1]
+            accum = accum + share * part_ref[b, h * CAP:(h + 1) * CAP, :].astype(f32)
+        heads.append(accum.astype(bf16))
     attended = jnp.concatenate(heads, axis=1)
     half = D // 2
     step = 384
@@ -272,8 +289,7 @@
     query, kf, vf, bias = unpack(place, lengths, swap(pack(fq, fk, fv), HEAD))
     queries = lax.all_gather(query, "yh", axis=0, tiled=True)
     parts = attention(queries, kv, kf, vf, bias)
-    parts = swap(parts.reshape(NY, CAP, GROUP + HD), "yh")
-    packed = project(parts, w)
+    packed = project(swap(parts, "yh"), w)
     own_length = lax.dynamic_index_in_dim(lengths, (z * NY + yh) * NC + c, 0, keepdims=False)
     limit = jnp.clip(own_length - own_head * OWN, 0, OWN)[None]
     return mix(limit, swap(packed, HEAD), hidden, gate[None, :])

time: 113 us -> 111 us (0.982)
  starting transfers between devices: 16.3 us -> 14.6 us
    all_to_all x2, starting transfers between devices: 16.3 us -> 14.6 us  [swap(): return lax.all_to_all(x, axis, split_axis=0, concat_axis=0, tiled=True)]
where the time goes in v4:
time: 111 us
  blocking collectives  37.7 us (34%)
  waiting for transfers between devices  26.2 us (24%)
  starting transfers between devices  14.6 us (13%)
  between operations  14.1 us (13%)
  Pallas kernels  13.2 us (12%)
  local copies, waits for them, and re-layouts  3.29 us (3%)
  other arithmetic  1.69 us (2%)
    all_to_all x1, blocking collectives, swap(): return lax.all_to_all(x, axis, split_axis=0, concat_axis=0, tiled=True)  21.3 us
    all_gather x1, blocking collectives, local(): queries = lax.all_gather(query, 'yh', axis=0, tiled=True)  16.4 us
    all_to_all x2, starting transfers between devices, swap(): return lax.all_to_all(x, axis, split_axis=0, concat_axis=0, tiled=True)  14.6 us
    all_gather x1, waiting for transfers between devices, local(): lax.all_gather(jnp.concatenate([sk, sv], axis=1), ('z', 'c'), axis=0, til...  13.6 us
    all_to_all x2, waiting for transfers between devices, swap(): return lax.all_to_all(x, axis, split_axis=0, concat_axis=0, tiled=True)  12.6 us
    pallas_call x1, Pallas kernels, attention(): pl.pallas_call(attention_kernel, grid=(steps,), in_specs=[column(QUERIES)...  8 us
    unnamed x16, local copies, waits for them, and re-layouts  2.71 us
  transfers between devices with their start and end apart: 3, of which 3 were waited for; matrix products, arithmetic and copies ran while one was open for 1% of the time, Pallas kernels for 2%

profile of v4, /device:TPU:8, one launch (start us, length us, event | category | flops | bytes accessed | tf_op | source)
XLA Modules:
  0.0 110.8 jit_solution(14461004841379194188)
XLA Ops:
  6.5 0.0 all-gather.2.cloned.1.call-start
  6.5 1.6 %pad_maximum_fusion = bf16[96,1024]{1,0:T(8,128)(2,1)} fusion(bf16[96,512]{1,0:T(8,128)(2,1)} %param.14, bf16[96,512]{1,0:T(8,128)(2,1)} %param.13), kind=kLoop, calls=%fused_computation | loop fusion | flops 393216 | bytes 393216 | tf_op jit(solution)/shard_map/concatenate | solution.py:288
  8.2 0.0 all-gather.2.cloned.1.call-update
  8.2 1.8 %shard_map.100 = bf16[8,16,1152]{2,1,0:T(8,128)(2,1)} custom-call(bf16[12,4096]{1,0:T(8,128)(2,1)} %q_ref.1, bf16[12,4096]{1,0:T(8,128)(2,1)} %k_ref.1, bf16[12,4096]{1,0:T(8,128)(2,1)} %v_ref.1), custom_call_target="tpu_custom_call" | custom-call | tf_op jit(solution)/shard_map/pallas_call | solution.py:56
  10.0 9.2 %all-to-all-start = ((bf16[8,16,1152]{2,1,0:T(8,128)(2,1)}), bf16[8,16,1152]{2,1,0:T(8,128)(2,1)S(1)}, u32[]{:S(2)}, u32[]{:S(2)}) async-start(bf16[8,16,1152]{2,1,0:T(8,128)(2,1)} %shard_map.100), calls=%async_computation | async-start | bytes 589824 | tf_op jit(solution)/shard_map/all_to_all | solution.py:280
  19.2 0.1 pad_add_fusion.place_ref
  19.3 5.9 %all-to-all-done.in_ref = bf16[8,16,1152]{2,1,0:T(8,128)(2,1)S(1)} async-done(((bf16[8,16,1152]{2,1,0:T(8,128)(2,1)}), bf16[8,16,1152]{2,1,0:T(8,128)(2,1)S(1)}, u32[]{:S(2)}, u32[]{:S(2)}) %all-to-all-start) | async-done | bytes 294944 | tf_op jit(solution)/shard_map/all_to_all | solution.py:280
  25.2 0.0 copy-start.6
  25.2 0.7 copy-done.6
  25.9 0.7 shard_map.101
  26.5 0.0 copy-start.1
  26.5 0.8 copy-done.1
  27.3 0.0 copy-start.2
  27.3 0.6 copy-done.2
  27.9 0.0 copy-start.3
  27.9 0.6 copy-done.3
  28.6 16.4 %all_gather.6.q_ref = bf16[384,512]{1,0:T(8,128)(2,1)} all-gather(bf16[96,512]{1,0:T(8,128)(2,1)S(1)} %get-tuple-element.9), channel_id=1, replica_groups=mesh['z'=8,'yh'=4,'c'=2,'yl'=2,'x'=4] {'yh'}, dimensions={0}, use_global_device_ids=true | all-gather | bytes 491520 | tf_op jit(solution)/shard_map/all_gather | solution.py:290
  45.0 13.6 %all-gather.2.cloned.1.call-done.k_ref.v_ref = bf16[1536,1024]{1,0:T(8,128)(2,1)} async-done(((bf16[96,1024]{1,0:T(8,128)(2,1)}), bf16[1536,1024]{1,0:T(8,128)(2,1)}) %all-gather.2.cloned.1.call-update) | async-done | bytes 3145744 | tf_op jit(solution)/shard_map/all_gather | solution.py:288
  58.6 0.0 copy-start
  58.6 8.0 %shard_map.102 = bf16[4,400,128]{2,1,0:T(8,128)(2,1)} custom-call(bf16[384,512]{1,0:T(8,128)(2,1)} %all_gather.6.q_ref, bf16[1536,1024]{1,0:T(8,128)(2,1)} %all-gather.2.cloned.1.call-done.k_ref.v_ref, bf16[1536,1024]{1,0:T(8,128)(2,1)} %all-gather.2.cloned.1.call-done.k_ref.v_ref, bf16[96,512]{1,0:T(8,128)(2,1)} %copy-done.2, bf16[96,512]{1,0:T(8,128)(2,1)} %copy-done.3, ...), custom_call_target="tpu_custom_call" | custom-call | flops 1283457024 | bytes 3145728 | tf_op jit(solution)/shard_map/pallas_call | solution.py:176
  66.6 0.0 copy-start.7
  66.6 0.0 copy-start.5
  66.6 21.3 %all_to_all.15.part_ref = bf16[4,400,128]{2,1,0:T(8,128)(2,1)S(1)} all-to-all(bf16[4,400,128]{2,1,0:T(8,128)(2,1)} %shard_map.102), channel_id=1, replica_groups=mesh['z'=8,'yh'=4,'c'=2,'yl'=2,'x'=4] {'yh'}, dimensions={0} | all-to-all | bytes 819200 | tf_op jit(solution)/shard_map/all_to_all | solution.py:280
  87.9 0.0 copy-done
  87.9 1.9 %shard_map.103 = bf16[8,16,2304]{2,1,0:T(8,128)(2,1)} custom-call(bf16[4,400,128]{2,1,0:T(8,128)(2,1)S(1)} %all_to_all.15.part_ref, bf16[512,3072]{1,0:T(8,128)(2,1)S(1)} %copy-done), custom_call_target="tpu_custom_call" | custom-call | tf_op jit(solution)/shard_map/pallas_call | solution.py:244
  89.9 5.4 %all-to-all-start.2 = ((bf16[8,16,2304]{2,1,0:T(8,128)(2,1)}), bf16[8,16,2304]{2,1,0:T(8,128)(2,1)S(1)}, u32[]{:S(2)}, u32[]{:S(2)}) async-start(bf16[8,16,2304]{2,1,0:T(8,128)(2,1)} %shard_map.103), calls=%async_computation.2 | async-start | bytes 1179648 | tf_op jit(solution)/shard_map/all_to_all | solution.py:280
  95.3 0.0 copy-done.7
  95.3 0.6 dynamic_slice.4
  96.5 6.7 %all-to-all-done.2.in_ref = bf16[8,16,2304]{2,1,0:T(8,128)(2,1)S(1)} async-done(((bf16[8,16,2304]{2,1,0:T(8,128)(2,1)}), bf16[8,16,2304]{2,1,0:T(8,128)(2,1)S(1)}, u32[]{:S(2)}, u32[]{:S(2)}) %all-to-all-start.2) | async-done | bytes 589856 | tf_op jit(solution)/shard_map/all_to_all | solution.py:280
  103.2 0.0 copy-done.4
  103.2 0.0 copy-done.5
  103.2 0.7 shard_map.104
  (1 shorter events, 0.0 us)
Async XLA Ops:
  6.5 52.1 %all-gather.2.cloned.1.call-start = ((), (), s32[]{:S(2)}) async-start(), calls=%async_computation.3 | async-start | bytes 3342336 | tf_op jit(solution)/shard_map/all_gather | solution.py:288
  10.0 15.2 %all-to-all-start = ((bf16[8,16,1152]{2,1,0:T(8,128)(2,1)}), bf16[8,16,1152]{2,1,0:T(8,128)(2,1)S(1)}, u32[]{:S(2)}, u32[]{:S(2)}) async-start(bf16[8,16,1152]{2,1,0:T(8,128)(2,1)} %shard_map.100), calls=%async_computation | async-start | bytes 589824 | tf_op jit(solution)/shard_map/all_to_all | solution.py:280
  25.2 0.7 copy-start.6
  26.5 0.8 copy-start.1
  27.3 0.6 copy-start.2
  27.9 0.6 copy-start.3
  58.6 29.4 %copy-start = (bf16[512,3072]{1,0:T(8,128)(2,1)S(1)}, bf16[512,3072]{1,0:T(8,128)(2,1)}, u32[]{:S(2)}) copy-start(bf16[512,3072]{1,0:T(8,128)(2,1)} %w_ref.1) | copy-start | bytes 9437188
  66.6 28.7 %copy-start.7 = (s32[64]{0:T(128)S(1)}, s32[64]{0:T(128)}, u32[]{:S(2)}) copy-start(s32[64]{0:T(128)} %lengths_ref.1) | copy-start | bytes 772
  66.6 36.6 %copy-start.4 = (bf16[12,3072]{1,0:T(8,128)(2,1)S(1)}, bf16[12,3072]{1,0:T(8,128)(2,1)}, u32[]{:S(2)}) copy-start(bf16[12,3072]{1,0:T(8,128)(2,1)} %hidden_ref.1) | copy-start | bytes 221188
  66.6 36.6 %copy-start.5 = (f32[3072]{0:T(1024)S(1)}, f32[3072]{0:T(1024)}, u32[]{:S(2)}) copy-start(f32[3072]{0:T(1024)} %param.17) | copy-start | bytes 36868
  89.9 13.4 %all-to-all-start.2 = ((bf16[8,16,2304]{2,1,0:T(8,128)(2,1)}), bf16[8,16,2304]{2,1,0:T(8,128)(2,1)S(1)}, u32[]{:S(2)}, u32[]{:S(2)}) async-start(bf16[8,16,2304]{2,1,0:T(8,128)(2,1)} %shard_map.103), calls=%async_computation.2 | async-start | bytes 1179648 | tf_op jit(solution)/shard_map/all_to_all | solution.py:280
Sparse Core Ops, SparseCore 0:
  9.5 49.0 all-gather.1

commit v5 on v4

--- a/solution.py
+++ b/solution.py
@@ -82,7 +82,7 @@
 
     z, yh, c = place_ref[0], place_ref[1], place_ref[2]
     row = lax.broadcasted_iota(jnp.int32, (CAP, HD), 0)
-    mine = lax.broadcasted_iota(jnp.int32, (CAP, HD), 1) == yh
+    mine = lax.broadcasted_iota(jnp.int32, (CAP, HD), 1) == 1
     for j in range(NZ * NC):
         length = lengths_ref[(j // NC) * NY * NC + yh * NC + j % NC]
         hidden_length = jnp.where((j // NC == z) & (j % NC == c), 0, length)
@@ -108,43 +108,51 @@
     )(place, lengths, received)
 
 
-def attention_kernel(q_ref, k_ref, v_ref, kf_ref, vf_ref, hot_ref, bias_ref, out_ref, stat_ref):
+def attend(load_query, keys, hot_lane, count):
+    rows = count * CAP
+    hot = (lax.broadcasted_iota(jnp.int32, (rows, HD), 1) == hot_lane).astype(f32).astype(bf16)
+    query = jnp.concatenate([load_query, hot], axis=1)
+    scores = []
+    for key, _, bias in keys:
+        key = jnp.concatenate([key, bias], axis=1)
+        scores.append(lax.dot_general(query, key, (((1,), (1,)), ((), ())), preferred_element_type=f32))
+    top = scores[0].max(axis=1, keepdims=True)
+    for s in scores[1:]:
+        top = jnp.maximum(top, s.max(axis=1, keepdims=True))
+    total = jnp.zeros((rows, 1), f32)
+    accum = jnp.zeros((rows, HD), f32)
+    for s, (_, value, _) in zip(scores, keys):
+        weights = jnp.exp2((s - top) * EXP2_SCALE)
+        total = total + weights.sum(axis=1, keepdims=True)
+        accum = accum + jnp.dot(weights.astype(bf16), value, preferred_element_type=f32)
+    return (accum / total).astype(bf16), top * EXP2_SCALE + jnp.log2(total)
+
+
+def add_stat(stat, level, h):
+    lane = lax.broadcasted_iota(jnp.int32, stat.shape, 1)
+    hi = level.astype(bf16).astype(f32)
+    mid = (level - hi).astype(bf16).astype(f32)
+    low = level - hi - mid
+    stat = jnp.where(lane == 3 * h, hi, stat)
+    stat = jnp.where(lane == 3 * h + 1, mid, stat)
+    return jnp.where(lane == 3 * h + 2, low, stat)
+
+
+def stale_pieces(k_ref, v_ref, bias_ref, cols):
+    chunk = KEYS // 4
+    return [
+        (k_ref[j:j + chunk, cols], v_ref[j:j + chunk, cols], bias_ref[j:j + chunk])
+        for j in range(0, KEYS, chunk)
+    ]
+
+
+def stat_rows(stat):
+    square = jnp.concatenate([stat, jnp.zeros((HD - CAP, HD), f32)], axis=0)
+    return square.T[:STAT_ROWS].astype(bf16)
+
+
+def collect(stat_ref, stat, finish):
     g = pl.program_id(0)
-    lane = lax.broadcasted_iota(jnp.int32, (QUERIES, HD), 1)
-    stat = jnp.zeros((QUERIES, HD), f32)
-    chunk = KEYS // 4
-    for i in range(TOGETHER):
-        cols = slice(i * HD, (i + 1) * HD)
-        query = jnp.concatenate([q_ref[:, cols], hot_ref[...]], axis=1)
-        pieces = [
-            (k_ref[j:j + chunk, cols], v_ref[j:j + chunk, cols], bias_ref[j:j + chunk])
-            for j in range(0, KEYS, chunk)
-        ]
-        pieces.append((kf_ref[:, cols], vf_ref[:, cols], bias_ref[KEYS:]))
-        scores = []
-        for key, _, bias in pieces:
-            key = jnp.concatenate([key, bias], axis=1)
-            scores.append(lax.dot_general(query, key, (((1,), (1,)), ((), ())), preferred_element_type=f32))
-        top = scores[0].max(axis=1, keepdims=True)
-        for s in scores[1:]:
-            top = jnp.maximum(top, s.max(axis=1, keepdims=True))
-        total = jnp.zeros((QUERIES, 1), f32)
-        accum = jnp.zeros((QUERIES, HD), f32)
-        for s, (_, value, _) in zip(scores, pieces):
-            weights = jnp.exp2((s - top) * EXP2_SCALE)
-            total = total + weights.sum(axis=1, keepdims=True)
-            accum = accum + jnp.dot(weights.astype(bf16), value, preferred_element_type=f32)
-        h = g * TOGETHER + i
-        result = (accum / total).astype(bf16)
-        for b in range(NY):
-            out_ref[b, pl.ds(pl.multiple_of(h * CAP, 32), CAP), :] = result[b * CAP:(b + 1) * CAP]
-        level = top * EXP2_SCALE + jnp.log2(total)
-        hi = level.astype(bf16).astype(f32)
-        mid = (level - hi).astype(bf16).astype(f32)
-        low = level - hi - mid
-        stat = jnp.where(lane == 3 * h, hi, stat)
-        stat = jnp.where(lane == 3 * h + 1, mid, stat)
-        stat = jnp.where(lane == 3 * h + 2, low, stat)
 
     @pl.when(g == 0)
     def _():
@@ -154,46 +162,111 @@
     def _():
         stat_ref[...] = stat_ref[...] + stat
 
-    @pl.when(g == pl.num_programs(0) - 1)
+    pl.when(g == pl.num_programs(0) - 1)(finish)
+
+
+def others_kernel(place_ref, q_ref, k_ref, v_ref, bias_ref, out_ref, stat_ref):
+    g = pl.program_id(0)
+    yh = place_ref[1]
+    count = NY - 1
+    slots = [lax.rem(yh + k, NY) for k in range(1, NY)]
+    stat = jnp.zeros((count * CAP, HD), f32)
+
+    @pl.when(g == 0)
     def _():
-        for b in range(NY):
-            rows = stat_ref[b * CAP:(b + 1) * CAP]
-            square = jnp.concatenate([rows, jnp.zeros((HD - CAP, HD), f32)], axis=0)
-            out_ref[b, HEADS_HERE * CAP:, :] = square.T[:STAT_ROWS].astype(bf16)
-
-
-def attention(q, kv, kf, vf, bias):
-    hot = np.zeros((QUERIES, HD), np.float32)
-    hot[np.arange(QUERIES), np.arange(QUERIES) // CAP] = 1
-    steps = HEADS_HERE // TOGETHER
-
-    def column(rows, skip=0):
-        return pl.BlockSpec((rows, TOGETHER * HD), lambda g: (0, g + skip))
-
-    def whole(rows, cols):
-        return pl.BlockSpec((rows, cols), lambda g: (0, 0))
-
-    return pl.pallas_call(
-        attention_kernel,
-        grid=(steps,),
+        out_ref[yh] = jnp.zeros((RETURNED, HD), bf16)
+
+    for i in range(TOGETHER):
+        cols = slice(i * HD, (i + 1) * HD)
+        query = jnp.concatenate([q_ref[slot, :, cols] for slot in slots], axis=0)
+        result, level = attend(query, stale_pieces(k_ref, v_ref, bias_ref, cols), 0, count)
+        h = g * TOGETHER + i
+        for n, slot in enumerate(slots):
+            out_ref[slot, pl.ds(pl.multiple_of(h * CAP, 32), CAP), :] = result[n * CAP:(n + 1) * CAP]
+        stat = add_stat(stat, level, h)
+
+    def finish():
+        for n, slot in enumerate(slots):
+            out_ref[slot, HEADS_HERE * CAP:, :] = stat_rows(stat_ref[n * CAP:(n + 1) * CAP])
+
+    collect(stat_ref, stat, finish)
+
+
+def own_kernel(q_ref, k_ref, v_ref, kf_ref, vf_ref, bias_ref, out_ref, stat_ref):
+    g = pl.program_id(0)
+    stat = jnp.zeros((CAP, HD), f32)
+    for i in range(TOGETHER):
+        cols = slice(i * HD, (i + 1) * HD)
+        pieces = stale_pieces(k_ref, v_ref, bias_ref, cols)
+        pieces.append((kf_ref[:, cols], vf_ref[:, cols], bias_ref[KEYS:]))
+        result, level = attend(q_ref[:, cols], pieces, 1, 1)
+        h = g * TOGETHER + i
+        out_ref[pl.ds(pl.multiple_of(h * CAP, 32), CAP), :] = result
+        stat = add_stat(stat, level, h)
+
+    def finish():
+        out_ref[HEADS_HERE * CAP:, :] = stat_rows(stat_ref[...])
+
+    collect(stat_ref, stat, finish)
+
+
+STEPS = HEADS_HERE // TOGETHER
+
+
+def column(rows, skip=0):
+    return pl.BlockSpec((rows, TOGETHER * HD), lambda g: (0, g + skip))
+
+
+def whole(*shape):
+    return pl.BlockSpec(shape, lambda g: (0,) * len(shape))
+
+
+def cost(rows, keys):
+    return pl.CostEstimate(
+        flops=4 * rows * keys * GROUP,
+        bytes_accessed=4 * keys * GROUP,
+        transcendentals=rows * keys * HEADS_HERE,
+    )
+
+
+def attend_others(place, q, kv, bias):
+    rows = (NY - 1) * CAP
+    return pl.pallas_call(
+        others_kernel,
+        grid=(STEPS,),
         in_specs=[
-            column(QUERIES), column(KEYS), column(KEYS, steps), column(CAP), column(CAP),
-            whole(QUERIES, HD), whole(KEYS + CAP, HD),
+            pl.BlockSpec(memory_space=pltpu.SMEM),
+            pl.BlockSpec((NY, CAP, TOGETHER * HD), lambda g: (0, 0, g)),
+            column(KEYS), column(KEYS, STEPS), whole(KEYS + CAP, HD),
         ],
-        out_specs=pl.BlockSpec((NY, RETURNED, HD), lambda g: (0, 0, 0)),
+        out_specs=whole(NY, RETURNED, HD),
         out_shape=jax.ShapeDtypeStruct((NY, RETURNED, HD), bf16),
-        scratch_shapes=[pltpu.VMEM((QUERIES, HD), f32)],
+        scratch_shapes=[pltpu.VMEM((rows, HD), f32)],
         compiler_params=params(60),
-        cost_estimate=pl.CostEstimate(
-            flops=4 * QUERIES * (KEYS + CAP) * GROUP,
-            bytes_accessed=4 * KEYS * GROUP,
-            transcendentals=QUERIES * (KEYS + CAP) * HEADS_HERE,
-        ),
-    )(q, kv, kv, kf, vf, jnp.asarray(hot, bf16), bias)
-
-
-def project_kernel(part_ref, w_ref, out_ref):
-    stats = [part_ref[b, HEADS_HERE * CAP:, :].astype(f32) for b in range(NY)]
+        cost_estimate=cost(rows, KEYS),
+    )(place, q, kv, kv, bias)
+
+
+def attend_own(q, kv, kf, vf, bias):
+    return pl.pallas_call(
+        own_kernel,
+        grid=(STEPS,),
+        in_specs=[
+            column(CAP), column(KEYS), column(KEYS, STEPS), column(CAP), column(CAP), whole(KEYS + CAP, HD),
+        ],
+        out_specs=whole(RETURNED, HD),
+        out_shape=jax.ShapeDtypeStruct((RETURNED, HD), bf16),
+        scratch_shapes=[pltpu.VMEM((CAP, HD), f32)],
+        compiler_params=params(40),
+        cost_estimate=cost(CAP, KEYS + CAP),
+    )(q, kv, kv, kf, vf, bias)
+
+
+def project_kernel(place_ref, part_ref, own_ref, w_ref, out_ref):
+    def part(b, rows):
+        return jnp.where(place_ref[1] == b, own_ref[rows, :].astype(f32), part_ref[b, rows, :].astype(f32))
+
+    stats = [part(b, slice(HEADS_HERE * CAP, RETURNED)) for b in range(NY)]
     shares = []
     for h in range(HEADS_HERE):
         levels = [s[3 * h:3 * h + 1] + s[3 * h + 1:3 * h + 2] + s[3 * h + 2:3 * h + 3] for s in stats]
@@ -211,7 +284,7 @@
         accum = jnp.zeros((CAP, HD), f32)
         for b in range(NY):
             share = shares[:CAP, h * NY + b:h * NY + b + 1]
-            accum = accum + share * part_ref[b, h * CAP:(h + 1) * CAP, :].astype(f32)
+            accum = accum + share * part(b, slice(h * CAP, (h + 1) * CAP))
         heads.append(accum.astype(bf16))
     attended = jnp.concatenate(heads, axis=1)
     half = D // 2
@@ -240,14 +313,14 @@
                 out_ref[s, row:row + 8, col:col + step] = tile.astype(bf16)
 
 
-def project(parts, w):
+def project(place, parts, own, w):
     return pl.pallas_call(
         project_kernel,
-        in_specs=[pl.BlockSpec(memory_space=pltpu.VMEM)] * 2,
+        in_specs=[pl.BlockSpec(memory_space=pltpu.SMEM)] + [pl.BlockSpec(memory_space=pltpu.VMEM)] * 3,
         out_specs=pl.BlockSpec(memory_space=pltpu.VMEM),
         out_shape=jax.ShapeDtypeStruct((NHEAD, 16, OUT_PACKED), bf16),
         compiler_params=params(24),
-    )(parts, w)
+    )(place, parts, own, w)
 
 
 def mix_kernel(limit_ref, in_ref, hidden_ref, gate_ref, out_ref):
@@ -287,9 +360,10 @@
     place = jnp.stack([z, yh, c]).astype(jnp.int32)
     kv = lax.all_gather(jnp.concatenate([sk, sv], axis=1), ("z", "c"), axis=0, tiled=True)
     query, kf, vf, bias = unpack(place, lengths, swap(pack(fq, fk, fv), HEAD))
-    queries = lax.all_gather(query, "yh", axis=0, tiled=True)
-    parts = attention(queries, kv, kf, vf, bias)
-    packed = project(swap(parts, "yh"), w)
+    queries = lax.all_gather(query, "yh", axis=0)
+    returned = swap(attend_others(place, queries, kv, bias), "yh")
+    own = attend_own(query, kv, kf, vf, bias)
+    packed = project(place, returned, own, w)
     own_length = lax.dynamic_index_in_dim(lengths, (z * NY + yh) * NC + c, 0, keepdims=False)
     limit = jnp.clip(own_length - own_head * OWN, 0, OWN)[None]
     return mix(limit, swap(packed, HEAD), hidden, gate[None, :])

time: 111 us -> 114 us (1.027)
  blocking collectives: 37.7 us -> 16.4 us
  local copies, waits for them, and re-layouts: 3.29 us -> 11.7 us
  starting transfers between devices: 14.6 us -> 21.8 us
  waiting for transfers between devices: 26.2 us -> 32.3 us
  Pallas kernels: 13.2 us -> 15.4 us
    all_to_all x1 -> x0, blocking collectives: 21.3 us -> none  [swap(): return lax.all_to_all(x, axis, split_axis=0, concat_axis=0, tiled=True)]
    unnamed x16 -> x36, local copies, waits for them, and re-layouts: 2.71 us -> 11.1 us
    all_to_all x2 -> x3, starting transfers between devices: 14.6 us -> 21.8 us  [swap(): return lax.all_to_all(x, axis, split_axis=0, concat_axis=0, tiled=True)]
    all_to_all x2 -> x3, waiting for transfers between devices: 12.6 us -> 19.3 us  [swap(): return lax.all_to_all(x, axis, split_axis=0, concat_axis=0, tiled=True)]
    pallas_call x1 -> x2, Pallas kernels: 8 us -> 9.65 us  [the longest x1 6.63 us: attend_others(): pl.pallas_call(others_kernel, grid=(STEPS,), in_specs=[pl.BlockSpec(memor...]
  transfers between devices with their start and end apart: 3 -> 4, of which waited for: 3 -> 4; matrix products, arithmetic and copies ran while one was open for 1% -> 1% of each run, Pallas kernels for 2% -> 5%
where the time goes in v5:
time: 114 us; the launch traced here: 113 us
  waiting for transfers between devices  32.3 us (28%)
  starting transfers between devices  21.8 us (19%)
  blocking collectives  16.4 us (14%)
  Pallas kernels  15.4 us (14%)
  between operations  14.1 us (12%)
  local copies, waits for them, and re-layouts  11.7 us (10%)
  other arithmetic  1.71 us (2%)
    all_to_all x3, starting transfers between devices, swap(): return lax.all_to_all(x, axis, split_axis=0, concat_axis=0, tiled=True)  21.8 us
    all_to_all x3, waiting for transfers between devices, swap(): return lax.all_to_all(x, axis, split_axis=0, concat_axis=0, tiled=True)  19.3 us
    all_gather x1, blocking collectives, local(): queries = lax.all_gather(query, 'yh', axis=0)  16.4 us
    all_gather x1, waiting for transfers between devices, local(): lax.all_gather(jnp.concatenate([sk, sv], axis=1), ('z', 'c'), axis=0, til...  13 us
    unnamed x36, local copies, waits for them, and re-layouts  11.1 us
    pallas_call x1, Pallas kernels, attend_others(): pl.pallas_call(others_kernel, grid=(STEPS,), in_specs=[pl.BlockSpec(memor...  6.63 us
    pallas_call x1, Pallas kernels, attend_own(): pl.pallas_call(own_kernel, grid=(STEPS,), in_specs=[column(CAP), column(K...  3.03 us
    pallas_call x1, Pallas kernels, project(): pl.pallas_call(project_kernel, in_specs=[pl.BlockSpec(memory_space=pltpu....  2.5 us
  transfers between devices with their start and end apart: 4, of which 4 were waited for; matrix products, arithmetic and copies ran while one was open for 1% of the time, Pallas kernels for 5%

profile of v5, /device:TPU:8, one launch (start us, length us, event | category | flops | bytes accessed | tf_op | source)
XLA Modules:
  0.0 113.3 jit_solution(10644598817933320559)
XLA Ops:
  6.5 1.6 %pad_maximum_fusion = bf16[96,1024]{1,0:T(8,128)(2,1)} fusion(bf16[96,512]{1,0:T(8,128)(2,1)} %param.13, bf16[96,512]{1,0:T(8,128)(2,1)} %param.12), kind=kLoop, calls=%fused_computation | loop fusion | flops 393216 | bytes 393216 | tf_op jit(solution)/shard_map/concatenate | solution.py:361
  8.2 0.0 all-gather.3.cloned.1.call-update
  8.2 1.8 %shard_map.91 = bf16[8,16,1152]{2,1,0:T(8,128)(2,1)} custom-call(bf16[12,4096]{1,0:T(8,128)(2,1)} %q_ref.1, bf16[12,4096]{1,0:T(8,128)(2,1)} %k_ref.1, bf16[12,4096]{1,0:T(8,128)(2,1)} %v_ref.1), custom_call_target="tpu_custom_call" | custom-call | tf_op jit(solution)/shard_map/pallas_call | solution.py:56
  10.0 9.2 %all-to-all-start = ((bf16[8,16,1152]{2,1,0:T(8,128)(2,1)}), bf16[8,16,1152]{2,1,0:T(8,128)(2,1)S(1)}, u32[]{:S(2)}, u32[]{:S(2)}) async-start(bf16[8,16,1152]{2,1,0:T(8,128)(2,1)} %shard_map.91), calls=%async_computation | async-start | bytes 589824 | tf_op jit(solution)/shard_map/all_to_all | solution.py:353
  19.2 0.1 pad_add_fusion.place_ref
  19.3 5.9 %all-to-all-done.in_ref = bf16[8,16,1152]{2,1,0:T(8,128)(2,1)S(1)} async-done(((bf16[8,16,1152]{2,1,0:T(8,128)(2,1)}), bf16[8,16,1152]{2,1,0:T(8,128)(2,1)S(1)}, u32[]{:S(2)}, u32[]{:S(2)}) %all-to-all-start) | async-done | bytes 294944 | tf_op jit(solution)/shard_map/all_to_all | solution.py:353
  25.2 0.7 copy-done.16
  25.9 0.7 shard_map.92
  26.6 0.7 copy-done.2
  27.3 0.6 copy-done.9
  27.9 0.6 copy-done.11
  28.6 16.4 %all-gather = bf16[384,512]{1,0:T(8,128)(2,1)} all-gather(bf16[96,512]{1,0:T(8,128)(2,1)S(1)} %get-tuple-element.9.q_ref), channel_id=2, replica_groups=mesh['z'=8,'yh'=4,'c'=2,'yl'=2,'x'=4] {'yh'}, dimensions={0}, use_global_device_ids=true | all-gather | bytes 491520 | tf_op jit(solution)/shard_map/all_gather | solution.py:363
  45.0 0.6 copy-done.6
  45.6 13.0 %all-gather.3.cloned.1.call-done.k_ref.v_ref = bf16[1536,1024]{1,0:T(8,128)(2,1)} async-done(((bf16[96,1024]{1,0:T(8,128)(2,1)}), bf16[1536,1024]{1,0:T(8,128)(2,1)}) %all-gather.3.cloned.1.call-update) | async-done | bytes 3145744 | tf_op jit(solution)/shard_map/all_gather | solution.py:361
  58.6 6.6 %shard_map.93 = bf16[4,400,128]{2,1,0:T(8,128)(2,1)} custom-call(s32[3]{0:T(128)} %copy-done.14, bf16[4,96,512]{2,1,0:T(8,128)(2,1)} %bitcast.8, bf16[1536,1024]{1,0:T(8,128)(2,1)} %all-gather.3.cloned.1.call-done.k_ref.v_ref, bf16[1536,1024]{1,0:T(8,128)(2,1)} %all-gather.3.cloned.1.call-done.k_ref.v_ref, bf16[1632,128]{1,0:T(8,128)(2,1)} %copy-done.2), custom_call_target="tpu_custom_call" | custom-call | flops 905969664 | bytes 3145728 | tf_op jit(solution)/shard_map/pallas_call | solution.py:234
  65.2 5.8 %all-to-all-start.1 = ((bf16[4,400,128]{2,1,0:T(8,128)(2,1)}), bf16[4,400,128]{2,1,0:T(8,128)(2,1)S(1)}, u32[]{:S(2)}, u32[]{:S(2)}) async-start(bf16[4,400,128]{2,1,0:T(8,128)(2,1)} %shard_map.93), calls=%async_computation.1 | async-start | bytes 819200 | tf_op jit(solution)/shard_map/all_to_all | solution.py:353
  71.1 1.0 copy-done.3
  72.1 0.9 copy-done.7
  73.0 0.9 copy-done.10
  73.8 0.9 copy-done.12
  74.7 3.0 %shard_map.94.own_ref = bf16[400,128]{1,0:T(8,128)(2,1)S(1)} custom-call(bf16[96,512]{1,0:T(8,128)(2,1)S(1)} %copy-done.7, bf16[1536,1024]{1,0:T(8,128)(2,1)S(1)} %copy-done, bf16[1536,1024]{1,0:T(8,128)(2,1)S(1)} %copy-done, bf16[96,512]{1,0:T(8,128)(2,1)S(1)} %copy-done.10, bf16[96,512]{1,0:T(8,128)(2,1)S(1)} %copy-done.12, bf16[1632,128]{1,0:T(8,128)(2,1)S(1)} %copy-done.3), custom_call_target="tpu_custom_call" | custom-call | flops 320864256 | bytes 3342336 | tf_op jit(solution)/shard_map/pallas_call | solution.py:251
  77.8 0.7 copy-done.4
  78.4 6.2 %all-to-all-done.1.part_ref = bf16[4,400,128]{2,1,0:T(8,128)(2,1)S(1)} async-done(((bf16[4,400,128]{2,1,0:T(8,128)(2,1)}), bf16[4,400,128]{2,1,0:T(8,128)(2,1)S(1)}, u32[]{:S(2)}, u32[]{:S(2)}) %all-to-all-start.1) | async-done | bytes 409632 | tf_op jit(solution)/shard_map/all_to_all | solution.py:353
  84.7 1.9 %copy-done.1 = bf16[512,3072]{1,0:T(8,128)(2,1)S(1)} copy-done((bf16[512,3072]{1,0:T(8,128)(2,1)S(1)}, bf16[512,3072]{1,0:T(8,128)(2,1)}, u32[]{:S(2)}) %copy-start.1) | copy-done | bytes 3145752
  86.5 0.9 copy-done.5
  87.4 0.7 copy-done.15
  88.1 2.5 %shard_map.95 = bf16[8,16,2304]{2,1,0:T(8,128)(2,1)} custom-call(s32[3]{0:T(128)S(1)} %copy-done.15, bf16[4,400,128]{2,1,0:T(8,128)(2,1)S(1)} %all-to-all-done.1.part_ref, bf16[400,128]{1,0:T(8,128)(2,1)S(1)} %copy-done.5, bf16[512,3072]{1,0:T(8,128)(2,1)S(1)} %copy-done.1), custom_call_target="tpu_custom_call" | custom-call | tf_op jit(solution)/shard_map/pallas_call | solution.py:317
  90.6 6.8 %all-to-all-start.2 = ((bf16[8,16,2304]{2,1,0:T(8,128)(2,1)}), bf16[8,16,2304]{2,1,0:T(8,128)(2,1)S(1)}, u32[]{:S(2)}, u32[]{:S(2)}) async-start(bf16[8,16,2304]{2,1,0:T(8,128)(2,1)} %shard_map.95), calls=%async_computation.2 | async-start | bytes 1179648 | tf_op jit(solution)/shard_map/all_to_all | solution.py:353
  97.4 0.0 copy-done.17
  97.4 0.6 dynamic_slice.4
  98.6 7.1 %all-to-all-done.2.in_ref = bf16[8,16,2304]{2,1,0:T(8,128)(2,1)S(1)} async-done(((bf16[8,16,2304]{2,1,0:T(8,128)(2,1)}), bf16[8,16,2304]{2,1,0:T(8,128)(2,1)S(1)}, u32[]{:S(2)}, u32[]{:S(2)}) %all-to-all-start.2) | async-done | bytes 589856 | tf_op jit(solution)/shard_map/all_to_all | solution.py:353
  105.7 0.7 shard_map.96
  (23 shorter events, 0.0 us)
Async XLA Ops:
  6.5 52.1 %all-gather.3.cloned.1.call-start = ((), (), s32[]{:S(2)}) async-start(), calls=%async_computation.3 | async-start | bytes 3342336 | tf_op jit(solution)/shard_map/all_gather | solution.py:361
  10.0 15.2 %all-to-all-start = ((bf16[8,16,1152]{2,1,0:T(8,128)(2,1)}), bf16[8,16,1152]{2,1,0:T(8,128)(2,1)S(1)}, u32[]{:S(2)}, u32[]{:S(2)}) async-start(bf16[8,16,1152]{2,1,0:T(8,128)(2,1)} %shard_map.91), calls=%async_computation | async-start | bytes 589824 | tf_op jit(solution)/shard_map/all_to_all | solution.py:353
  19.3 39.3 %copy-start.14 = (s32[3]{0:T(128)}, s32[3]{0:T(128)S(1)}, u32[]{:S(2)}) copy-start(s32[3]{0:T(128)S(1)} %pad_add_fusion.place_ref) | copy-start | bytes 40
  25.2 0.7 copy-start.16
  26.5 0.7 copy-start.2
  27.3 0.6 copy-start.9
  27.9 0.6 copy-start.11
  45.0 0.6 copy-start.6
  58.6 12.5 %copy-start = (bf16[1536,1024]{1,0:T(8,128)(2,1)S(1)}, bf16[1536,1024]{1,0:T(8,128)(2,1)}, u32[]{:S(2)}) copy-start(bf16[1536,1024]{1,0:T(8,128)(2,1)} %all-gather.3.cloned.1.call-done.k_ref.v_ref) | copy-start | bytes 9437188
  65.2 19.4 %all-to-all-start.1 = ((bf16[4,400,128]{2,1,0:T(8,128)(2,1)}), bf16[4,400,128]{2,1,0:T(8,128)(2,1)S(1)}, u32[]{:S(2)}, u32[]{:S(2)}) async-start(bf16[4,400,128]{2,1,0:T(8,128)(2,1)} %shard_map.93), calls=%async_computation.1 | async-start | bytes 819200 | tf_op jit(solution)/shard_map/all_to_all | solution.py:353
  71.1 1.0 copy-start.3
  72.1 0.9 copy-start.7
  72.9 0.9 copy-start.10
  73.8 0.9 copy-start.12
  77.8 0.7 copy-start.4
  84.7 1.9 %copy-start.1 = (bf16[512,3072]{1,0:T(8,128)(2,1)S(1)}, bf16[512,3072]{1,0:T(8,128)(2,1)}, u32[]{:S(2)}) copy-start(bf16[512,3072]{1,0:T(8,128)(2,1)} %w_ref.1) | copy-start | bytes 9437188
  86.5 0.9 copy-start.5
  87.4 0.7 copy-start.15
  88.1 9.3 %copy-start.17 = (s32[64]{0:T(128)S(1)}, s32[64]{0:T(128)}, u32[]{:S(2)}) copy-start(s32[64]{0:T(128)} %lengths_ref.1) | copy-start | bytes 772
  88.1 17.6 %copy-start.8 = (bf16[12,3072]{1,0:T(8,128)(2,1)S(1)}, bf16[12,3072]{1,0:T(8,128)(2,1)}, u32[]{:S(2)}) copy-start(bf16[12,3072]{1,0:T(8,128)(2,1)} %hidden_ref.1) | copy-start | bytes 221188
  88.1 17.6 %copy-start.13 = (f32[3072]{0:T(1024)S(1)}, f32[3072]{0:T(1024)}, u32[]{:S(2)}) copy-start(f32[3072]{0:T(1024)} %param.16) | copy-start | bytes 36868
  90.6 15.1 %all-to-all-start.2 = ((bf16[8,16,2304]{2,1,0:T(8,128)(2,1)}), bf16[8,16,2304]{2,1,0:T(8,128)(2,1)S(1)}, u32[]{:S(2)}, u32[]{:S(2)}) async-start(bf16[8,16,2304]{2,1,0:T(8,128)(2,1)} %shard_map.95), calls=%async_computation.2 | async-start | bytes 1179648 | tf_op jit(solution)/shard_map/all_to_all | solution.py:353
Sparse Core Ops, SparseCore 0:
  9.5 49.0 all-gather.2

commit v6 on v5

--- a/solution.py
+++ b/solution.py
@@ -60,7 +60,7 @@
     )(fq, fk, fv)
 
 
-def unpack_kernel(place_ref, lengths_ref, in_ref, q_ref, k_ref, v_ref, bias_ref):
+def unpack_kernel(lengths_ref, in_ref, q_ref, k_ref, v_ref, bias_ref):
     mask = lower_half((8, GROUP // 2))
     tops = [[], [], []]
     rests = [[], [], []]
@@ -80,7 +80,7 @@
             tiles.append(jnp.concatenate([left, right], axis=1))
         ref[...] = jnp.concatenate(tiles, axis=0).astype(bf16)
 
-    z, yh, c = place_ref[0], place_ref[1], place_ref[2]
+    z, yh, c = (lax.axis_index(a) for a in ("z", "yh", "c"))
     row = lax.broadcasted_iota(jnp.int32, (CAP, HD), 0)
     mine = lax.broadcasted_iota(jnp.int32, (CAP, HD), 1) == 1
     for j in range(NZ * NC):
@@ -95,17 +95,17 @@
     bias_ref[KEYS:] = jnp.where(seen, 0.0, BIG).astype(bf16)
 
 
-def unpack(place, lengths, received):
+def unpack(lengths, received):
     one = jax.ShapeDtypeStruct((CAP, GROUP), bf16)
     smem = pl.BlockSpec(memory_space=pltpu.SMEM)
     vmem = pl.BlockSpec(memory_space=pltpu.VMEM)
     return pl.pallas_call(
         unpack_kernel,
-        in_specs=[smem, smem, vmem],
+        in_specs=[smem, vmem],
         out_specs=(vmem,) * 4,
         out_shape=(one, one, one, jax.ShapeDtypeStruct((KEYS + CAP, HD), bf16)),
         compiler_params=params(16),
-    )(place, lengths, received)
+    )(lengths, received)
 
 
 def attend(load_query, keys, hot_lane, count):
@@ -165,9 +165,9 @@
     pl.when(g == pl.num_programs(0) - 1)(finish)
 
 
-def others_kernel(place_ref, q_ref, k_ref, v_ref, bias_ref, out_ref, stat_ref):
+def others_kernel(q_ref, k_ref, v_ref, bias_ref, out_ref, stat_ref):
     g = pl.program_id(0)
-    yh = place_ref[1]
+    yh = lax.axis_index("yh")
     count = NY - 1
     slots = [lax.rem(yh + k, NY) for k in range(1, NY)]
     stat = jnp.zeros((count * CAP, HD), f32)
@@ -229,13 +229,12 @@
     )
 
 
-def attend_others(place, q, kv, bias):
+def attend_others(q, kv, bias):
     rows = (NY - 1) * CAP
     return pl.pallas_call(
         others_kernel,
         grid=(STEPS,),
         in_specs=[
-            pl.BlockSpec(memory_space=pltpu.SMEM),
             pl.BlockSpec((NY, CAP, TOGETHER * HD), lambda g: (0, 0, g)),
             column(KEYS), column(KEYS, STEPS), whole(KEYS + CAP, HD),
         ],
@@ -244,7 +243,7 @@
         scratch_shapes=[pltpu.VMEM((rows, HD), f32)],
         compiler_params=params(60),
         cost_estimate=cost(rows, KEYS),
-    )(place, q, kv, kv, bias)
+    )(q, kv, kv, bias)
 
 
 def attend_own(q, kv, kf, vf, bias):
@@ -257,14 +256,18 @@
         out_specs=whole(RETURNED, HD),
         out_shape=jax.ShapeDtypeStruct((RETURNED, HD), bf16),
         scratch_shapes=[pltpu.VMEM((CAP, HD), f32)],
-        compiler_params=params(40),
+        compiler_params=params(60),
         cost_estimate=cost(CAP, KEYS + CAP),
     )(q, kv, kv, kf, vf, bias)
 
 
-def project_kernel(place_ref, part_ref, own_ref, w_ref, out_ref):
+def project_kernel(part_ref, own_ref, w_hbm, out_ref, w_ref, sem):
+    copy = pltpu.make_async_copy(w_hbm, w_ref, sem)
+    copy.start()
+    yh = lax.axis_index("yh")
+
     def part(b, rows):
-        return jnp.where(place_ref[1] == b, own_ref[rows, :].astype(f32), part_ref[b, rows, :].astype(f32))
+        return jnp.where(yh == b, own_ref[rows, :].astype(f32), part_ref[b, rows, :].astype(f32))
 
     stats = [part(b, slice(HEADS_HERE * CAP, RETURNED)) for b in range(NY)]
     shares = []
@@ -287,6 +290,7 @@
             accum = accum + share * part(b, slice(h * CAP, (h + 1) * CAP))
         heads.append(accum.astype(bf16))
     attended = jnp.concatenate(heads, axis=1)
+    copy.wait()
     half = D // 2
     step = 384
     mask = lower_half((8, step))
@@ -313,17 +317,18 @@
                 out_ref[s, row:row + 8, col:col + step] = tile.astype(bf16)
 
 
-def project(place, parts, own, w):
+def project(parts, own, w):
     return pl.pallas_call(
         project_kernel,
-        in_specs=[pl.BlockSpec(memory_space=pltpu.SMEM)] + [pl.BlockSpec(memory_space=pltpu.VMEM)] * 3,
+        in_specs=[pl.BlockSpec(memory_space=pltpu.VMEM)] * 2 + [pl.BlockSpec(memory_space=pl.ANY)],
         out_specs=pl.BlockSpec(memory_space=pltpu.VMEM),
         out_shape=jax.ShapeDtypeStruct((NHEAD, 16, OUT_PACKED), bf16),
-        compiler_params=params(24),
-    )(place, parts, own, w)
-
-
-def mix_kernel(limit_ref, in_ref, hidden_ref, gate_ref, out_ref):
+        scratch_shapes=[pltpu.VMEM((GROUP, D), bf16), pltpu.SemaphoreType.DMA],
+        compiler_params=params(60),
+    )(parts, own, w)
+
+
+def mix_kernel(lengths_ref, in_ref, hidden_ref, gate_ref, out_ref):
     total = in_ref[0].astype(f32)
     for s in range(1, NHEAD):
         total = total + in_ref[s].astype(f32)
@@ -333,12 +338,14 @@
     tail = jnp.concatenate([rest[0:4], rest[4:8]], axis=1)
     projected = jnp.concatenate([flat[:, :D], tail], axis=0)
     residual = hidden_ref[...].astype(f32)
-    live = lax.broadcasted_iota(jnp.int32, (OWN, D), 0) < limit_ref[0]
+    patch = (lax.axis_index("z") * NY + lax.axis_index("yh")) * NC + lax.axis_index("c")
+    limit = lengths_ref[patch] - (lax.axis_index("yl") * NX + lax.axis_index("x")) * OWN
+    live = lax.broadcasted_iota(jnp.int32, (OWN, D), 0) < limit
     mixed = jnp.where(live, residual + gate_ref[...] * projected, residual)
     out_ref[...] = mixed.astype(bf16)
 
 
-def mix(limit, received, hidden, gate):
+def mix(lengths, received, hidden, gate):
     vmem = pl.BlockSpec(memory_space=pltpu.VMEM)
     return pl.pallas_call(
         mix_kernel,
@@ -346,7 +353,7 @@
         out_specs=vmem,
         out_shape=jax.ShapeDtypeStruct((OWN, D), bf16),
         compiler_params=params(16),
-    )(limit, received, hidden, gate)
+    )(lengths, received, hidden, gate)
 
 
 def swap(x, axis):
@@ -354,19 +361,13 @@
 
 
 def local(fq, fk, fv, sk, sv, lengths, hidden, gate, w):
-    z, yh, c = (lax.axis_index(a) for a in ("z", "yh", "c"))
-    own_head = lax.axis_index("yl") * NX + lax.axis_index("x")
-
-    place = jnp.stack([z, yh, c]).astype(jnp.int32)
     kv = lax.all_gather(jnp.concatenate([sk, sv], axis=1), ("z", "c"), axis=0, tiled=True)
-    query, kf, vf, bias = unpack(place, lengths, swap(pack(fq, fk, fv), HEAD))
+    query, kf, vf, bias = unpack(lengths, swap(pack(fq, fk, fv), HEAD))
     queries = lax.all_gather(query, "yh", axis=0)
-    returned = swap(attend_others(place, queries, kv, bias), "yh")
+    returned = swap(attend_others(queries, kv, bias), "yh")
     own = attend_own(query, kv, kf, vf, bias)
-    packed = project(place, returned, own, w)
-    own_length = lax.dynamic_index_in_dim(lengths, (z * NY + yh) * NC + c, 0, keepdims=False)
-    limit = jnp.clip(own_length - own_head * OWN, 0, OWN)[None]
-    return mix(limit, swap(packed, HEAD), hidden, gate[None, :])
+    packed = project(returned, own, w)
+    return mix(lengths, swap(packed, HEAD), hidden, gate[None, :])
 
 
 def solution(mesh):

time: 114 us -> 114 us (level)
  the two profiles are of different devices: /device:TPU:8 before, /device:TPU:16 now
where the time goes in v6:
time: 114 us
  blocking collectives  44.8 us (39%)
  waiting for transfers between devices  23.6 us (21%)
  Pallas kernels  19.7 us (17%)
  between operations  13.4 us (12%)
  starting transfers between devices  7.22 us (6%)
  local copies, waits for them, and re-layouts  3.43 us (3%)
  other arithmetic  1.62 us (1%)
    all_to_all x2, blocking collectives, swap(): return lax.all_to_all(x, axis, split_axis=0, concat_axis=0, tiled=True)  28.4 us
    all_gather x1, blocking collectives, local(): queries = lax.all_gather(query, 'yh', axis=0)  16.4 us
    all_gather x1, waiting for transfers between devices, local(): lax.all_gather(jnp.concatenate([sk, sv], axis=1), ('z', 'c'), axis=0, til...  15.6 us
    all_to_all x1, waiting for transfers between devices, swap(): return lax.all_to_all(x, axis, split_axis=0, concat_axis=0, tiled=True)  7.96 us
    all_to_all x1, starting transfers between devices, swap(): return lax.all_to_all(x, axis, split_axis=0, concat_axis=0, tiled=True)  7.22 us
    pallas_call x1, Pallas kernels, attend_others(): pl.pallas_call(others_kernel, grid=(STEPS,), in_specs=[pl.BlockSpec((NY,...  6.46 us
    pallas_call x1, Pallas kernels, attend_own(): pl.pallas_call(own_kernel, grid=(STEPS,), in_specs=[column(CAP), column(K...  5.08 us
    pallas_call x1, Pallas kernels, project(): pl.pallas_call(project_kernel, in_specs=[pl.BlockSpec(memory_space=pltpu....  4.37 us
  transfers between devices with their start and end apart: 2, of which 2 were waited for; matrix products, arithmetic and copies ran while one was open for 0% of the time, Pallas kernels for 7%

profile of v6, /device:TPU:16, one launch (start us, length us, event | category | flops | bytes accessed | tf_op | source)
XLA Modules:
  0.0 113.8 jit_solution(13423772413912073471)
XLA Ops:
  6.5 0.0 all-gather.3.cloned.1.call-start
  6.5 1.6 %pad_maximum_fusion = bf16[96,1024]{1,0:T(8,128)(2,1)} fusion(bf16[96,512]{1,0:T(8,128)(2,1)} %param.13, bf16[96,512]{1,0:T(8,128)(2,1)} %param.12), kind=kLoop, calls=%fused_computation | loop fusion | flops 393216 | bytes 393216 | tf_op jit(solution)/shard_map/concatenate | solution.py:364
  8.2 0.0 all-gather.3.cloned.1.call-update
  8.2 1.8 %shard_map.91 = bf16[8,16,1152]{2,1,0:T(8,128)(2,1)} custom-call(bf16[12,4096]{1,0:T(8,128)(2,1)} %q_ref.1, bf16[12,4096]{1,0:T(8,128)(2,1)} %k_ref.1, bf16[12,4096]{1,0:T(8,128)(2,1)} %v_ref.1), custom_call_target="tpu_custom_call" | custom-call | tf_op jit(solution)/shard_map/pallas_call | solution.py:56
  10.0 13.1 %all_to_all.15.in_ref = bf16[8,16,1152]{2,1,0:T(8,128)(2,1)S(1)} all-to-all(bf16[8,16,1152]{2,1,0:T(8,128)(2,1)} %shard_map.91), channel_id=1, replica_groups=mesh['z'=8,'yh'=4,'c'=2,'yl'=2,'x'=4] {'yl','x'}, dimensions={0} | all-to-all | bytes 589824 | tf_op jit(solution)/shard_map/all_to_all | solution.py:360
  23.2 0.0 copy-start.6
  23.2 0.7 copy-done.6
  23.8 0.7 shard_map.92
  24.5 0.0 copy-start
  24.5 0.7 copy-done
  25.2 0.0 copy-start.3
  25.2 0.6 copy-done.3
  25.9 0.0 copy-start.4
  25.9 0.6 copy-done.4
  26.5 0.0 copy-start.1
  26.5 16.4 %all-gather = bf16[384,512]{1,0:T(8,128)(2,1)} all-gather(bf16[96,512]{1,0:T(8,128)(2,1)S(1)} %get-tuple-element.9.q_ref), channel_id=2, replica_groups=mesh['z'=8,'yh'=4,'c'=2,'yl'=2,'x'=4] {'yh'}, dimensions={0}, use_global_device_ids=true | all-gather | bytes 491520 | tf_op jit(solution)/shard_map/all_gather | solution.py:366
  42.9 15.6 %all-gather.3.cloned.1.call-done.k_ref.v_ref = bf16[1536,1024]{1,0:T(8,128)(2,1)} async-done(((bf16[96,1024]{1,0:T(8,128)(2,1)}), bf16[1536,1024]{1,0:T(8,128)(2,1)}) %all-gather.3.cloned.1.call-update) | async-done | bytes 3145744 | tf_op jit(solution)/shard_map/all_gather | solution.py:364
  58.5 6.5 %shard_map.93 = bf16[4,400,128]{2,1,0:T(8,128)(2,1)} custom-call(bf16[4,96,512]{2,1,0:T(8,128)(2,1)} %bitcast.3, bf16[1536,1024]{1,0:T(8,128)(2,1)} %all-gather.3.cloned.1.call-done.k_ref.v_ref, bf16[1536,1024]{1,0:T(8,128)(2,1)} %all-gather.3.cloned.1.call-done.k_ref.v_ref, bf16[1632,128]{1,0:T(8,128)(2,1)} %copy-done), custom_call_target="tpu_custom_call" | custom-call | flops 905969664 | bytes 3145728 | tf_op jit(solution)/shard_map/pallas_call | solution.py:234
  65.0 0.0 copy-done.1
  65.0 7.2 %all-to-all-start.1 = ((bf16[4,400,128]{2,1,0:T(8,128)(2,1)}), bf16[4,400,128]{2,1,0:T(8,128)(2,1)S(1)}, u32[]{:S(2)}, u32[]{:S(2)}) async-start(bf16[4,400,128]{2,1,0:T(8,128)(2,1)} %shard_map.93), calls=%async_computation.1 | async-start | bytes 819200 | tf_op jit(solution)/shard_map/all_to_all | solution.py:360
  72.2 5.1 %shard_map.94.own_ref = bf16[400,128]{1,0:T(8,128)(2,1)} custom-call(bf16[96,512]{1,0:T(8,128)(2,1)} %copy-done.1, bf16[1536,1024]{1,0:T(8,128)(2,1)} %all-gather.3.cloned.1.call-done.k_ref.v_ref, bf16[1536,1024]{1,0:T(8,128)(2,1)} %all-gather.3.cloned.1.call-done.k_ref.v_ref, bf16[96,512]{1,0:T(8,128)(2,1)} %copy-done.3, bf16[96,512]{1,0:T(8,128)(2,1)} %copy-done.4, ...), custom_call_target="tpu_custom_call" | custom-call | flops 320864256 | bytes 3342336 | tf_op jit(solution)/shard_map/pallas_call | solution.py:250
  77.3 0.0 copy-start.2
  77.3 0.0 copy-start.5
  77.3 0.0 copy-start.7
  77.3 8.0 %all-to-all-done.1.part_ref = bf16[4,400,128]{2,1,0:T(8,128)(2,1)S(1)} async-done(((bf16[4,400,128]{2,1,0:T(8,128)(2,1)}), bf16[4,400,128]{2,1,0:T(8,128)(2,1)S(1)}, u32[]{:S(2)}, u32[]{:S(2)}) %all-to-all-start.1) | async-done | bytes 409632 | tf_op jit(solution)/shard_map/all_to_all | solution.py:360
  85.2 0.7 copy-done.8
  86.0 4.4 %shard_map.95 = bf16[8,16,2304]{2,1,0:T(8,128)(2,1)} custom-call(bf16[4,400,128]{2,1,0:T(8,128)(2,1)} %copy-done.8, bf16[400,128]{1,0:T(8,128)(2,1)} %shard_map.94.own_ref, bf16[512,3072]{1,0:T(8,128)(2,1)} %w_hbm.1), custom_call_target="tpu_custom_call" | custom-call | tf_op jit(solution)/shard_map/pallas_call | solution.py:321
  90.4 15.3 %all_to_all.16.in_ref = bf16[8,16,2304]{2,1,0:T(8,128)(2,1)S(1)} all-to-all(bf16[8,16,2304]{2,1,0:T(8,128)(2,1)} %shard_map.95), channel_id=1, replica_groups=mesh['z'=8,'yh'=4,'c'=2,'yl'=2,'x'=4] {'yl','x'}, dimensions={0} | all-to-all | bytes 1179648 | tf_op jit(solution)/shard_map/all_to_all | solution.py:360
  105.7 0.0 copy-done.2
  105.7 0.0 copy-done.5
  105.7 0.0 copy-done.7
  105.7 1.3 %shard_map.96 = bf16[12,3072]{1,0:T(8,128)(2,1)} custom-call(s32[64]{0:T(128)S(1)} %copy-done.7, bf16[8,16,2304]{2,1,0:T(8,128)(2,1)S(1)} %all_to_all.16.in_ref, bf16[12,3072]{1,0:T(8,128)(2,1)S(1)} %copy-done.2, f32[1,3072]{1,0:T(1,128)S(1)} %bitcast.2), custom_call_target="tpu_custom_call" | custom-call | tf_op jit(solution)/shard_map/pallas_call | solution.py:350
  (1 shorter events, 0.0 us)
Async XLA Ops:
  6.5 52.0 %all-gather.3.cloned.1.call-start = ((), (), s32[]{:S(2)}) async-start(), calls=%async_computation.3 | async-start | bytes 3342336 | tf_op jit(solution)/shard_map/all_gather | solution.py:364
  23.2 0.7 copy-start.6
  24.5 0.8 copy-start
  25.2 0.6 copy-start.3
  25.9 0.6 copy-start.4
  26.5 38.5 %copy-start.1 = (bf16[96,512]{1,0:T(8,128)(2,1)}, bf16[96,512]{1,0:T(8,128)(2,1)S(1)}, u32[]{:S(2)}) copy-start(bf16[96,512]{1,0:T(8,128)(2,1)S(1)} %get-tuple-element.9.q_ref) | copy-start | bytes 294916
  65.0 20.3 %all-to-all-start.1 = ((bf16[4,400,128]{2,1,0:T(8,128)(2,1)}), bf16[4,400,128]{2,1,0:T(8,128)(2,1)S(1)}, u32[]{:S(2)}, u32[]{:S(2)}) async-start(bf16[4,400,128]{2,1,0:T(8,128)(2,1)} %shard_map.93), calls=%async_computation.1 | async-start | bytes 819200 | tf_op jit(solution)/shard_map/all_to_all | solution.py:360
  77.3 28.4 %copy-start.2 = (bf16[12,3072]{1,0:T(8,128)(2,1)S(1)}, bf16[12,3072]{1,0:T(8,128)(2,1)}, u32[]{:S(2)}) copy-start(bf16[12,3072]{1,0:T(8,128)(2,1)} %hidden_ref.1) | copy-start | bytes 221188
  77.3 28.4 %copy-start.5 = (f32[3072]{0:T(1024)S(1)}, f32[3072]{0:T(1024)}, u32[]{:S(2)}) copy-start(f32[3072]{0:T(1024)} %param.16) | copy-start | bytes 36868
  77.3 28.4 %copy-start.7 = (s32[64]{0:T(128)S(1)}, s32[64]{0:T(128)}, u32[]{:S(2)}) copy-start(s32[64]{0:T(128)} %lengths_ref.3) | copy-start | bytes 772
  85.2 0.7 copy-start.8
Sparse Core Ops, SparseCore 0:
  9.5 48.9 all-gather.2

commit v7 on v6

--- a/solution.py
+++ b/solution.py
@@ -60,7 +60,7 @@
     )(fq, fk, fv)
 
 
-def unpack_kernel(lengths_ref, in_ref, q_ref, k_ref, v_ref, bias_ref):
+def unpack_kernel(lengths_ref, in_ref, q_ref, k_ref, v_ref, bias_ref, live_ref):
     mask = lower_half((8, GROUP // 2))
     tops = [[], [], []]
     rests = [[], [], []]
@@ -93,6 +93,9 @@
     own_length = lengths_ref[z * NY * NC + yh * NC + c]
     seen = token < jnp.where(mine, own_length, 0)
     bias_ref[KEYS:] = jnp.where(seen, 0.0, BIG).astype(bf16)
+    first = (lax.axis_index("yl") * NX + lax.axis_index("x")) * OWN
+    slot = first + lax.broadcasted_iota(jnp.int32, (16, HD), 0)
+    live_ref[...] = jnp.where(slot < own_length, 1.0, 0.0)
 
 
 def unpack(lengths, received):
@@ -102,8 +105,11 @@
     return pl.pallas_call(
         unpack_kernel,
         in_specs=[smem, vmem],
-        out_specs=(vmem,) * 4,
-        out_shape=(one, one, one, jax.ShapeDtypeStruct((KEYS + CAP, HD), bf16)),
+        out_specs=(vmem,) * 5,
+        out_shape=(
+            one, one, one,
+            jax.ShapeDtypeStruct((KEYS + CAP, HD), bf16), jax.ShapeDtypeStruct((16, HD), f32),
+        ),
         compiler_params=params(16),
     )(lengths, received)
 
@@ -192,8 +198,14 @@
     collect(stat_ref, stat, finish)
 
 
-def own_kernel(q_ref, k_ref, v_ref, kf_ref, vf_ref, bias_ref, out_ref, stat_ref):
+def own_kernel(q_ref, k_ref, v_ref, kf_ref, vf_ref, bias_ref, w_ref, out_ref, staged_ref, stat_ref, sem):
     g = pl.program_id(0)
+    copy = pltpu.make_async_copy(w_ref, staged_ref, sem)
+
+    @pl.when(g == 0)
+    def _():
+        copy.start()
+
     stat = jnp.zeros((CAP, HD), f32)
     for i in range(TOGETHER):
         cols = slice(i * HD, (i + 1) * HD)
@@ -206,6 +218,7 @@
 
     def finish():
         out_ref[HEADS_HERE * CAP:, :] = stat_rows(stat_ref[...])
+        copy.wait()
 
     collect(stat_ref, stat, finish)
 
@@ -246,24 +259,23 @@
     )(q, kv, kv, bias)
 
 
-def attend_own(q, kv, kf, vf, bias):
+def attend_own(q, kv, kf, vf, bias, w):
     return pl.pallas_call(
         own_kernel,
         grid=(STEPS,),
         in_specs=[
             column(CAP), column(KEYS), column(KEYS, STEPS), column(CAP), column(CAP), whole(KEYS + CAP, HD),
+            pl.BlockSpec(memory_space=pltpu.HBM),
         ],
-        out_specs=whole(RETURNED, HD),
-        out_shape=jax.ShapeDtypeStruct((RETURNED, HD), bf16),
-        scratch_shapes=[pltpu.VMEM((CAP, HD), f32)],
-        compiler_params=params(60),
+        out_specs=(whole(RETURNED, HD), pl.BlockSpec(memory_space=pl.ANY)),
+        out_shape=(pltpu.VMEM((RETURNED, HD), bf16), pltpu.VMEM((GROUP, D), bf16)),
+        scratch_shapes=[pltpu.VMEM((CAP, HD), f32), pltpu.SemaphoreType.DMA],
+        compiler_params=params(56),
         cost_estimate=cost(CAP, KEYS + CAP),
-    )(q, kv, kv, kf, vf, bias)
-
-
-def project_kernel(part_ref, own_ref, w_hbm, out_ref, w_ref, sem):
-    copy = pltpu.make_async_copy(w_hbm, w_ref, sem)
-    copy.start()
+    )(q, kv, kv, kf, vf, bias, w)
+
+
+def project_kernel(part_ref, own_ref, w_ref, out_ref):
     yh = lax.axis_index("yh")
 
     def part(b, rows):
@@ -290,7 +302,6 @@
             accum = accum + share * part(b, slice(h * CAP, (h + 1) * CAP))
         heads.append(accum.astype(bf16))
     attended = jnp.concatenate(heads, axis=1)
-    copy.wait()
     half = D // 2
     step = 384
     mask = lower_half((8, step))
@@ -320,15 +331,14 @@
 def project(parts, own, w):
     return pl.pallas_call(
         project_kernel,
-        in_specs=[pl.BlockSpec(memory_space=pltpu.VMEM)] * 2 + [pl.BlockSpec(memory_space=pl.ANY)],
+        in_specs=[pl.BlockSpec(memory_space=pltpu.VMEM)] * 3,
         out_specs=pl.BlockSpec(memory_space=pltpu.VMEM),
         out_shape=jax.ShapeDtypeStruct((NHEAD, 16, OUT_PACKED), bf16),
-        scratch_shapes=[pltpu.VMEM((GROUP, D), bf16), pltpu.SemaphoreType.DMA],
-        compiler_params=params(60),
+        compiler_params=params(24),
     )(parts, own, w)
 
 
-def mix_kernel(lengths_ref, in_ref, hidden_ref, gate_ref, out_ref):
+def mix_kernel(live_ref, in_ref, hidden_ref, gate_ref, out_ref):
     total = in_ref[0].astype(f32)
     for s in range(1, NHEAD):
         total = total + in_ref[s].astype(f32)
@@ -338,22 +348,20 @@
     tail = jnp.concatenate([rest[0:4], rest[4:8]], axis=1)
     projected = jnp.concatenate([flat[:, :D], tail], axis=0)
     residual = hidden_ref[...].astype(f32)
-    patch = (lax.axis_index("z") * NY + lax.axis_index("yh")) * NC + lax.axis_index("c")
-    limit = lengths_ref[patch] - (lax.axis_index("yl") * NX + lax.axis_index("x")) * OWN
-    live = lax.broadcasted_iota(jnp.int32, (OWN, D), 0) < limit
+    live = live_ref[:OWN, :1] > 0.5
     mixed = jnp.where(live, residual + gate_ref[...] * projected, residual)
     out_ref[...] = mixed.astype(bf16)
 
 
-def mix(lengths, received, hidden, gate):
+def mix(live, received, hidden, gate):
     vmem = pl.BlockSpec(memory_space=pltpu.VMEM)
     return pl.pallas_call(
         mix_kernel,
-        in_specs=[pl.BlockSpec(memory_space=pltpu.SMEM), vmem, vmem, vmem],
+        in_specs=[vmem] * 4,
         out_specs=vmem,
         out_shape=jax.ShapeDtypeStruct((OWN, D), bf16),
         compiler_params=params(16),
-    )(lengths, received, hidden, gate)
+    )(live, received, hidden, gate)
 
 
 def swap(x, axis):
@@ -362,12 +370,12 @@
 
 def local(fq, fk, fv, sk, sv, lengths, hidden, gate, w):
     kv = lax.all_gather(jnp.concatenate([sk, sv], axis=1), ("z", "c"), axis=0, tiled=True)
-    query, kf, vf, bias = unpack(lengths, swap(pack(fq, fk, fv), HEAD))
+    query, kf, vf, bias, live = unpack(lengths, swap(pack(fq, fk, fv), HEAD))
     queries = lax.all_gather(query, "yh", axis=0)
     returned = swap(attend_others(queries, kv, bias), "yh")
-    own = attend_own(query, kv, kf, vf, bias)
-    packed = project(returned, own, w)
-    return mix(lengths, swap(packed, HEAD), hidden, gate[None, :])
+    own, staged = attend_own(query, kv, kf, vf, bias, w)
+    packed = project(returned, own, staged)
+    return mix(live, swap(packed, HEAD), hidden, gate[None, :])
 
 
 def solution(mesh):

time: 114 us -> 110 us (0.965)
  Pallas kernels: 19.7 us -> 15.3 us
  local copies, waits for them, and re-layouts: 3.43 us -> 5.49 us
  waiting for transfers between devices: 23.6 us -> 22 us
    pallas_call x1, Pallas kernels: 4.37 us -> 1.11 us  [project(): pl.pallas_call(project_kernel, in_specs=[pl.BlockSpec(memory_space=pltpu....]
    unnamed x18 -> x22, local copies, waits for them, and re-layouts: 3.43 us -> 5.49 us
    all_gather x1, waiting for transfers between devices: 15.6 us -> 14.1 us  [local(): lax.all_gather(jnp.concatenate([sk, sv], axis=1), ('z', 'c'), axis=0, til...]
  transfers between devices with their start and end apart: 2 -> 2, of which waited for: 2 -> 2; matrix products, arithmetic and copies ran while one was open for 0% -> 0% of each run, Pallas kernels for 7% -> 6%
where the time goes in v7:
time: 110 us
  blocking collectives  44.8 us (41%)
  waiting for transfers between devices  22 us (20%)
  Pallas kernels  15.3 us (14%)
  between operations  13.4 us (12%)
  starting transfers between devices  7.27 us (7%)
  local copies, waits for them, and re-layouts  5.49 us (5%)
  other arithmetic  1.63 us (1%)
    all_to_all x2, blocking collectives, swap(): return lax.all_to_all(x, axis, split_axis=0, concat_axis=0, tiled=True)  28.2 us
    all_gather x1, blocking collectives, local(): queries = lax.all_gather(query, 'yh', axis=0)  16.6 us
    all_gather x1, waiting for transfers between devices, local(): lax.all_gather(jnp.concatenate([sk, sv], axis=1), ('z', 'c'), axis=0, til...  14.1 us
    all_to_all x1, waiting for transfers between devices, swap(): return lax.all_to_all(x, axis, split_axis=0, concat_axis=0, tiled=True)  7.9 us
    all_to_all x1, starting transfers between devices, swap(): return lax.all_to_all(x, axis, split_axis=0, concat_axis=0, tiled=True)  7.27 us
    pallas_call x1, Pallas kernels, attend_others(): pl.pallas_call(others_kernel, grid=(STEPS,), in_specs=[pl.BlockSpec((NY,...  6.46 us
    unnamed x22, local copies, waits for them, and re-layouts  5.49 us
    pallas_call x1, Pallas kernels, attend_own(): pl.pallas_call(own_kernel, grid=(STEPS,), in_specs=[column(CAP), column(K...  4.48 us
  transfers between devices with their start and end apart: 2, of which 2 were waited for; matrix products, arithmetic and copies ran while one was open for 0% of the time, Pallas kernels for 6%

profile of v7, /device:TPU:16, one launch (start us, length us, event | category | flops | bytes accessed | tf_op | source)
XLA Modules:
  0.0 110.0 jit_solution(7086371698722921250)
XLA Ops:
  6.5 0.0 all-gather.3.cloned.1.call-start
  6.5 1.6 %pad_maximum_fusion = bf16[96,1024]{1,0:T(8,128)(2,1)} fusion(bf16[96,512]{1,0:T(8,128)(2,1)} %param.13, bf16[96,512]{1,0:T(8,128)(2,1)} %param.12), kind=kLoop, calls=%fused_computation | loop fusion | flops 393216 | bytes 393216 | tf_op jit(solution)/shard_map/concatenate | solution.py:372
  8.2 0.0 all-gather.3.cloned.1.call-update
  8.2 1.8 %shard_map.91 = bf16[8,16,1152]{2,1,0:T(8,128)(2,1)} custom-call(bf16[12,4096]{1,0:T(8,128)(2,1)} %q_ref.1, bf16[12,4096]{1,0:T(8,128)(2,1)} %k_ref.1, bf16[12,4096]{1,0:T(8,128)(2,1)} %v_ref.1), custom_call_target="tpu_custom_call" | custom-call | tf_op jit(solution)/shard_map/pallas_call | solution.py:56
  10.0 13.1 %all_to_all.15.in_ref = bf16[8,16,1152]{2,1,0:T(8,128)(2,1)S(1)} all-to-all(bf16[8,16,1152]{2,1,0:T(8,128)(2,1)} %shard_map.91), channel_id=1, replica_groups=mesh['z'=8,'yh'=4,'c'=2,'yl'=2,'x'=4] {'yl','x'}, dimensions={0} | all-to-all | bytes 589824 | tf_op jit(solution)/shard_map/all_to_all | solution.py:368
  23.2 0.0 copy-start.10
  23.2 0.7 copy-done.10
  23.8 0.7 shard_map.92
  24.5 0.0 copy-start
  24.5 0.8 copy-done
  25.3 0.0 copy-start.4
  25.3 0.6 copy-done.4
  25.9 0.0 copy-start.5
  25.9 0.6 copy-done.5
  26.6 0.0 copy-start.8
  26.6 0.6 copy-done.8
  27.2 0.6 copy-done.1
  27.8 16.6 %all-gather = bf16[384,512]{1,0:T(8,128)(2,1)} all-gather(bf16[96,512]{1,0:T(8,128)(2,1)S(1)} %get-tuple-element.13.q_ref), channel_id=2, replica_groups=mesh['z'=8,'yh'=4,'c'=2,'yl'=2,'x'=4] {'yh'}, dimensions={0}, use_global_device_ids=true | all-gather | bytes 491520 | tf_op jit(solution)/shard_map/all_gather | solution.py:374
  44.4 14.1 %all-gather.3.cloned.1.call-done.k_ref.v_ref = bf16[1536,1024]{1,0:T(8,128)(2,1)} async-done(((bf16[96,1024]{1,0:T(8,128)(2,1)}), bf16[1536,1024]{1,0:T(8,128)(2,1)}) %all-gather.3.cloned.1.call-update) | async-done | bytes 3145744 | tf_op jit(solution)/shard_map/all_gather | solution.py:372
  58.5 6.5 %shard_map.93 = bf16[4,400,128]{2,1,0:T(8,128)(2,1)} custom-call(bf16[4,96,512]{2,1,0:T(8,128)(2,1)} %bitcast.3, bf16[1536,1024]{1,0:T(8,128)(2,1)} %all-gather.3.cloned.1.call-done.k_ref.v_ref, bf16[1536,1024]{1,0:T(8,128)(2,1)} %all-gather.3.cloned.1.call-done.k_ref.v_ref, bf16[1632,128]{1,0:T(8,128)(2,1)} %copy-done), custom_call_target="tpu_custom_call" | custom-call | flops 905969664 | bytes 3145728 | tf_op jit(solution)/shard_map/pallas_call | solution.py:247
  64.9 7.3 %all-to-all-start.1 = ((bf16[4,400,128]{2,1,0:T(8,128)(2,1)}), bf16[4,400,128]{2,1,0:T(8,128)(2,1)S(1)}, u32[]{:S(2)}, u32[]{:S(2)}) async-start(bf16[4,400,128]{2,1,0:T(8,128)(2,1)} %shard_map.93), calls=%async_computation.1 | async-start | bytes 819200 | tf_op jit(solution)/shard_map/all_to_all | solution.py:368
  72.2 4.5 %shard_map.94 = (bf16[400,128]{1,0:T(8,128)(2,1)S(1)}, bf16[512,3072]{1,0:T(8,128)(2,1)S(1)}) custom-call(bf16[96,512]{1,0:T(8,128)(2,1)} %copy-done.1, bf16[1536,1024]{1,0:T(8,128)(2,1)} %all-gather.3.cloned.1.call-done.k_ref.v_ref, bf16[1536,1024]{1,0:T(8,128)(2,1)} %all-gather.3.cloned.1.call-done.k_ref.v_ref, bf16[96,512]{1,0:T(8,128)(2,1)} %copy-done.4, ...), custom_call_target="tpu_custom_call" | custom-call | flops 320864256 | bytes 3342336 | tf_op jit(solution)/shard_map/pallas_call | solution.py:263
  76.7 0.0 copy-start.2
  76.7 0.6 copy-done.2
  77.3 7.9 %all-to-all-done.1.part_ref = bf16[4,400,128]{2,1,0:T(8,128)(2,1)S(1)} async-done(((bf16[4,400,128]{2,1,0:T(8,128)(2,1)}), bf16[4,400,128]{2,1,0:T(8,128)(2,1)S(1)}, u32[]{:S(2)}, u32[]{:S(2)}) %all-to-all-start.1) | async-done | bytes 409632 | tf_op jit(solution)/shard_map/all_to_all | solution.py:368
  85.2 0.9 copy-done.3
  86.1 1.1 %shard_map.95 = bf16[8,16,2304]{2,1,0:T(8,128)(2,1)S(1)} custom-call(bf16[4,400,128]{2,1,0:T(8,128)(2,1)S(1)} %all-to-all-done.1.part_ref, bf16[400,128]{1,0:T(8,128)(2,1)S(1)} %copy-done.3, bf16[512,3072]{1,0:T(8,128)(2,1)S(1)} %get-tuple-element.18.w_ref), custom_call_target="tpu_custom_call" | custom-call | tf_op jit(solution)/shard_map/pallas_call | solution.py:332
  87.3 15.1 %all_to_all.16.in_ref = bf16[8,16,2304]{2,1,0:T(8,128)(2,1)S(1)} all-to-all(bf16[8,16,2304]{2,1,0:T(8,128)(2,1)S(1)} %shard_map.95), channel_id=1, replica_groups=mesh['z'=8,'yh'=4,'c'=2,'yl'=2,'x'=4] {'yl','x'}, dimensions={0} | all-to-all | bytes 1179648 | tf_op jit(solution)/shard_map/all_to_all | solution.py:368
  102.3 0.0 copy-done.6
  102.3 0.0 copy-done.7
  102.3 0.0 copy-done.9
  102.3 0.8 shard_map.96
  (5 shorter events, 0.0 us)
Async XLA Ops:
  6.5 51.9 %all-gather.3.cloned.1.call-start = ((), (), s32[]{:S(2)}) async-start(), calls=%async_computation.3 | async-start | bytes 3342336 | tf_op jit(solution)/shard_map/all_gather | solution.py:372
  23.2 0.7 copy-start.10
  24.5 0.8 copy-start
  25.3 0.7 copy-start.4
  25.9 0.6 copy-start.5
  26.6 0.6 copy-start.8
  27.2 0.6 copy-start.1
  64.9 20.3 %all-to-all-start.1 = ((bf16[4,400,128]{2,1,0:T(8,128)(2,1)}), bf16[4,400,128]{2,1,0:T(8,128)(2,1)S(1)}, u32[]{:S(2)}, u32[]{:S(2)}) async-start(bf16[4,400,128]{2,1,0:T(8,128)(2,1)} %shard_map.93), calls=%async_computation.1 | async-start | bytes 819200 | tf_op jit(solution)/shard_map/all_to_all | solution.py:368
  76.7 0.6 copy-start.2
  85.2 0.9 copy-start.3
  86.1 16.2 %copy-start.6 = (bf16[12,3072]{1,0:T(8,128)(2,1)S(1)}, bf16[12,3072]{1,0:T(8,128)(2,1)}, u32[]{:S(2)}) copy-start(bf16[12,3072]{1,0:T(8,128)(2,1)} %hidden_ref.1) | copy-start | bytes 221188
  86.1 16.2 %copy-start.7 = (f32[3072]{0:T(1024)S(1)}, f32[3072]{0:T(1024)}, u32[]{:S(2)}) copy-start(f32[3072]{0:T(1024)} %param.16) | copy-start | bytes 36868
  86.1 16.2 %copy-start.9 = (f32[16,128]{1,0:T(8,128)S(1)}, f32[16,128]{1,0:T(8,128)}, u32[]{:S(2)}) copy-start(f32[16,128]{1,0:T(8,128)} %copy-done.8) | copy-start | bytes 24580
Sparse Core Ops, SparseCore 0:
  9.5 48.9 all-gather.2

commit v8 on v7

--- a/solution.py
+++ b/solution.py
@@ -144,8 +144,8 @@
     return jnp.where(lane == 3 * h + 2, low, stat)
 
 
-def stale_pieces(k_ref, v_ref, bias_ref, cols):
-    chunk = KEYS // 4
+def stale_pieces(k_ref, v_ref, bias_ref, cols, parts=4):
+    chunk = KEYS // parts
     return [
         (k_ref[j:j + chunk, cols], v_ref[j:j + chunk, cols], bias_ref[j:j + chunk])
         for j in range(0, KEYS, chunk)
@@ -171,31 +171,31 @@
     pl.when(g == pl.num_programs(0) - 1)(finish)
 
 
-def others_kernel(q_ref, k_ref, v_ref, bias_ref, out_ref, stat_ref):
-    g = pl.program_id(0)
+def others_kernel(q_hbm, kv_hbm, bias_hbm, out_ref, q_ref, k_ref, v_ref, bias_ref, sems):
+    copies = [
+        pltpu.make_async_copy(kv_hbm.at[:, :GROUP], k_ref, sems.at[0]),
+        pltpu.make_async_copy(kv_hbm.at[:, GROUP:], v_ref, sems.at[1]),
+        pltpu.make_async_copy(q_hbm, q_ref, sems.at[2]),
+        pltpu.make_async_copy(bias_hbm, bias_ref, sems.at[3]),
+    ]
+    for copy in copies:
+        copy.start()
     yh = lax.axis_index("yh")
     count = NY - 1
     slots = [lax.rem(yh + k, NY) for k in range(1, NY)]
     stat = jnp.zeros((count * CAP, HD), f32)
-
-    @pl.when(g == 0)
-    def _():
-        out_ref[yh] = jnp.zeros((RETURNED, HD), bf16)
-
-    for i in range(TOGETHER):
-        cols = slice(i * HD, (i + 1) * HD)
+    out_ref[yh] = jnp.zeros((RETURNED, HD), bf16)
+    for copy in copies:
+        copy.wait()
+    for h in range(HEADS_HERE):
+        cols = slice(h * HD, (h + 1) * HD)
         query = jnp.concatenate([q_ref[slot, :, cols] for slot in slots], axis=0)
-        result, level = attend(query, stale_pieces(k_ref, v_ref, bias_ref, cols), 0, count)
-        h = g * TOGETHER + i
+        result, level = attend(query, stale_pieces(k_ref, v_ref, bias_ref, cols, 3), 0, count)
         for n, slot in enumerate(slots):
-            out_ref[slot, pl.ds(pl.multiple_of(h * CAP, 32), CAP), :] = result[n * CAP:(n + 1) * CAP]
+            out_ref[slot, h * CAP:(h + 1) * CAP, :] = result[n * CAP:(n + 1) * CAP]
         stat = add_stat(stat, level, h)
-
-    def finish():
-        for n, slot in enumerate(slots):
-            out_ref[slot, HEADS_HERE * CAP:, :] = stat_rows(stat_ref[n * CAP:(n + 1) * CAP])
-
-    collect(stat_ref, stat, finish)
+    for n, slot in enumerate(slots):
+        out_ref[slot, HEADS_HERE * CAP:, :] = stat_rows(stat[n * CAP:(n + 1) * CAP])
 
 
 def own_kernel(q_ref, k_ref, v_ref, kf_ref, vf_ref, bias_ref, w_ref, out_ref, staged_ref, stat_ref, sem):
@@ -243,20 +243,20 @@
 
 
 def attend_others(q, kv, bias):
-    rows = (NY - 1) * CAP
     return pl.pallas_call(
         others_kernel,
-        grid=(STEPS,),
-        in_specs=[
-            pl.BlockSpec((NY, CAP, TOGETHER * HD), lambda g: (0, 0, g)),
-            column(KEYS), column(KEYS, STEPS), whole(KEYS + CAP, HD),
+        in_specs=[pl.BlockSpec(memory_space=pl.ANY), pl.BlockSpec(memory_space=pltpu.HBM), pl.BlockSpec(memory_space=pl.ANY)],
+        out_specs=pl.BlockSpec(memory_space=pltpu.VMEM),
+        out_shape=jax.ShapeDtypeStruct((NY, RETURNED, HD), bf16),
+        scratch_shapes=[
+            pltpu.VMEM((NY, CAP, GROUP), bf16),
+            pltpu.VMEM((KEYS, GROUP), bf16), pltpu.VMEM((KEYS, GROUP), bf16),
+            pltpu.VMEM((KEYS + CAP, HD), bf16),
+            pltpu.SemaphoreType.DMA((4,)),
         ],
-        out_specs=whole(NY, RETURNED, HD),
-        out_shape=jax.ShapeDtypeStruct((NY, RETURNED, HD), bf16),
-        scratch_shapes=[pltpu.VMEM((rows, HD), f32)],
         compiler_params=params(60),
-        cost_estimate=cost(rows, KEYS),
-    )(q, kv, kv, bias)
+        cost_estimate=cost((NY - 1) * CAP, KEYS),
+    )(q, kv, bias)
 
 
 def attend_own(q, kv, kf, vf, bias, w):
@@ -270,7 +270,7 @@
         out_specs=(whole(RETURNED, HD), pl.BlockSpec(memory_space=pl.ANY)),
         out_shape=(pltpu.VMEM((RETURNED, HD), bf16), pltpu.VMEM((GROUP, D), bf16)),
         scratch_shapes=[pltpu.VMEM((CAP, HD), f32), pltpu.SemaphoreType.DMA],
-        compiler_params=params(56),
+        compiler_params=params(44),
         cost_estimate=cost(CAP, KEYS + CAP),
     )(q, kv, kv, kf, vf, bias, w)
 

time: 110 us -> 114 us (1.036)
  local copies, waits for them, and re-layouts: 5.49 us -> 16.8 us
  waiting for transfers between devices: 22 us -> 16.2 us
  Pallas kernels: 15.3 us -> 13.5 us
    unnamed x22 -> x38, local copies, waits for them, and re-layouts: 5.49 us -> 16.8 us
    all_to_all x1, waiting for transfers between devices: 7.9 us -> 1.89 us  [swap(): return lax.all_to_all(x, axis, split_axis=0, concat_axis=0, tiled=True)]
    pallas_call x1, Pallas kernels: 4.48 us -> 3.27 us  [attend_own(): pl.pallas_call(own_kernel, grid=(STEPS,), in_specs=[column(CAP), column(K...]
  transfers between devices with their start and end apart: 2 -> 2, of which waited for: 2 -> 2; matrix products, arithmetic and copies ran while one was open for 0% -> 0% of each run, Pallas kernels for 6% -> 5%
where the time goes in v8:
time: 114 us
  blocking collectives  44.6 us (39%)
  local copies, waits for them, and re-layouts  16.8 us (15%)
  waiting for transfers between devices  16.2 us (14%)
  Pallas kernels  13.5 us (12%)
  between operations  13.5 us (12%)
  starting transfers between devices  7.28 us (6%)
  other arithmetic  1.65 us (1%)
    all_to_all x2, blocking collectives, swap(): return lax.all_to_all(x, axis, split_axis=0, concat_axis=0, tiled=True)  28.2 us
    unnamed x38, local copies, waits for them, and re-layouts  16.8 us
    all_gather x1, blocking collectives, local(): queries = lax.all_gather(query, 'yh', axis=0)  16.4 us
    all_gather x1, waiting for transfers between devices, local(): lax.all_gather(jnp.concatenate([sk, sv], axis=1), ('z', 'c'), axis=0, til...  14.3 us
    all_to_all x1, starting transfers between devices, swap(): return lax.all_to_all(x, axis, split_axis=0, concat_axis=0, tiled=True)  7.28 us
    pallas_call x1, Pallas kernels, attend_others(): pl.pallas_call(others_kernel, in_specs=[pl.BlockSpec(memory_space=pl.ANY)...  5.88 us
    pallas_call x1, Pallas kernels, attend_own(): pl.pallas_call(own_kernel, grid=(STEPS,), in_specs=[column(CAP), column(K...  3.27 us
  transfers between devices with their start and end apart: 2, of which 2 were waited for; matrix products, arithmetic and copies ran while one was open for 0% of the time, Pallas kernels for 5%

profile of v8, /device:TPU:16, one launch (start us, length us, event | category | flops | bytes accessed | tf_op | source)
XLA Modules:
  0.0 113.6 jit_solution(1660431156467000059)
XLA Ops:
  6.5 1.6 %pad_maximum_fusion = bf16[96,1024]{1,0:T(8,128)(2,1)} fusion(bf16[96,512]{1,0:T(8,128)(2,1)} %param.13, bf16[96,512]{1,0:T(8,128)(2,1)} %param.12), kind=kLoop, calls=%fused_computation | loop fusion | flops 393216 | bytes 393216 | tf_op jit(solution)/shard_map/concatenate | solution.py:372
  8.2 0.0 all-gather.3.cloned.1.call-update
  8.2 1.9 %shard_map.91 = bf16[8,16,1152]{2,1,0:T(8,128)(2,1)} custom-call(bf16[12,4096]{1,0:T(8,128)(2,1)} %q_ref.1, bf16[12,4096]{1,0:T(8,128)(2,1)} %k_ref.1, bf16[12,4096]{1,0:T(8,128)(2,1)} %v_ref.1), custom_call_target="tpu_custom_call" | custom-call | tf_op jit(solution)/shard_map/pallas_call | solution.py:56
  10.1 13.1 %all_to_all.15.in_ref = bf16[8,16,1152]{2,1,0:T(8,128)(2,1)S(1)} all-to-all(bf16[8,16,1152]{2,1,0:T(8,128)(2,1)} %shard_map.91), channel_id=1, replica_groups=mesh['z'=8,'yh'=4,'c'=2,'yl'=2,'x'=4] {'yl','x'}, dimensions={0} | all-to-all | bytes 589824 | tf_op jit(solution)/shard_map/all_to_all | solution.py:368
  23.2 0.7 copy-done.18
  23.9 0.7 shard_map.92
  24.5 0.7 copy-done.4
  25.3 0.6 copy-done.10
  25.9 0.6 copy-done.12
  26.5 0.6 copy-done.16
  27.1 16.4 %all-gather = bf16[384,512]{1,0:T(8,128)(2,1)} all-gather(bf16[96,512]{1,0:T(8,128)(2,1)S(1)} %get-tuple-element.13.q_ref), channel_id=2, replica_groups=mesh['z'=8,'yh'=4,'c'=2,'yl'=2,'x'=4] {'yh'}, dimensions={0}, use_global_device_ids=true | all-gather | bytes 491520 | tf_op jit(solution)/shard_map/all_gather | solution.py:374
  43.5 0.6 copy-done.6
  44.1 14.3 %all-gather.3.cloned.1.call-done.kv_hbm.k_ref.v_ref = bf16[1536,1024]{1,0:T(8,128)(2,1)} async-done(((bf16[96,1024]{1,0:T(8,128)(2,1)}), bf16[1536,1024]{1,0:T(8,128)(2,1)}) %all-gather.3.cloned.1.call-update) | async-done | bytes 3145744 | tf_op jit(solution)/shard_map/all_gather | solution.py:372
  58.5 5.9 %shard_map.93 = bf16[4,400,128]{2,1,0:T(8,128)(2,1)} custom-call(bf16[4,96,512]{2,1,0:T(8,128)(2,1)} %bitcast.3, bf16[1536,1024]{1,0:T(8,128)(2,1)} %all-gather.3.cloned.1.call-done.kv_hbm.k_ref.v_ref, bf16[1632,128]{1,0:T(8,128)(2,1)} %copy-done.4), custom_call_target="tpu_custom_call" | custom-call | flops 905969664 | bytes 3145728 | tf_op jit(solution)/shard_map/pallas_call | solution.py:246
  64.4 7.3 %all-to-all-start.1 = ((bf16[4,400,128]{2,1,0:T(8,128)(2,1)}), bf16[4,400,128]{2,1,0:T(8,128)(2,1)S(1)}, u32[]{:S(2)}, u32[]{:S(2)}) async-start(bf16[4,400,128]{2,1,0:T(8,128)(2,1)} %shard_map.93), calls=%async_computation.1 | async-start | bytes 819200 | tf_op jit(solution)/shard_map/all_to_all | solution.py:368
  71.7 1.9 %copy-done.3 = bf16[512,3072]{1,0:T(8,128)(2,1)S(1)} copy-done((bf16[512,3072]{1,0:T(8,128)(2,1)S(1)}, bf16[512,3072]{1,0:T(8,128)(2,1)}, u32[]{:S(2)}) %copy-start.3) | copy-done | bytes 3145752
  73.5 1.0 copy-done.5
  74.5 0.9 copy-done.7
  75.4 0.9 copy-done.11
  76.3 0.9 copy-done.13
  77.2 3.3 %shard_map.94 = (bf16[400,128]{1,0:T(8,128)(2,1)S(1)}, bf16[512,3072]{1,0:T(8,128)(2,1)S(1)}) custom-call(bf16[96,512]{1,0:T(8,128)(2,1)S(1)} %copy-done.7, bf16[1536,1024]{1,0:T(8,128)(2,1)S(1)} %copy-done, bf16[1536,1024]{1,0:T(8,128)(2,1)S(1)} %copy-done, bf16[96,512]{1,0:T(8,128)(2,1)S(1)} %copy-done.11, bf16[96,512]{1,0:T(8,128)(2,1)S(1)} %copy-done.13, ...), custom_call_target="tpu_custom_call" | custom-call | flops 320864256 | bytes 3342336 | tf_op jit(solution)/shard_map/pallas_call | solution.py:263
  80.5 1.6 %copy-done.1 = bf16[512,3072]{1,0:T(8,128)(2,1)} copy-done((bf16[512,3072]{1,0:T(8,128)(2,1)}, bf16[512,3072]{1,0:T(8,128)(2,1)S(1)}, u32[]{:S(2)}) %copy-start.1) | copy-done | bytes 3145752
  82.1 0.6 copy-done.8
  82.8 1.9 %all-to-all-done.1.part_ref = bf16[4,400,128]{2,1,0:T(8,128)(2,1)S(1)} async-done(((bf16[4,400,128]{2,1,0:T(8,128)(2,1)}), bf16[4,400,128]{2,1,0:T(8,128)(2,1)S(1)}, u32[]{:S(2)}, u32[]{:S(2)}) %all-to-all-start.1) | async-done | bytes 409632 | tf_op jit(solution)/shard_map/all_to_all | solution.py:368
  84.7 1.9 %copy-done.2 = bf16[512,3072]{1,0:T(8,128)(2,1)S(1)} copy-done((bf16[512,3072]{1,0:T(8,128)(2,1)S(1)}, bf16[512,3072]{1,0:T(8,128)(2,1)}, u32[]{:S(2)}) %copy-start.2) | copy-done | bytes 3145752
  86.6 0.9 copy-done.9
  87.5 1.1 shard_map.95
  88.6 15.1 %all_to_all.16.in_ref = bf16[8,16,2304]{2,1,0:T(8,128)(2,1)S(1)} all-to-all(bf16[8,16,2304]{2,1,0:T(8,128)(2,1)S(1)} %shard_map.95), channel_id=1, replica_groups=mesh['z'=8,'yh'=4,'c'=2,'yl'=2,'x'=4] {'yl','x'}, dimensions={0} | all-to-all | bytes 1179648 | tf_op jit(solution)/shard_map/all_to_all | solution.py:368
  103.6 0.9 copy-done.14
  104.5 0.7 copy-done.15
  105.3 0.7 copy-done.17
  105.9 0.8 shard_map.96
  (21 shorter events, 0.0 us)
Async XLA Ops:
  6.5 51.9 %all-gather.3.cloned.1.call-start = ((), (), s32[]{:S(2)}) async-start(), calls=%async_computation.3 | async-start | bytes 3342336 | tf_op jit(solution)/shard_map/all_gather | solution.py:372
  23.2 0.7 copy-start.18
  24.5 0.8 copy-start.4
  25.3 0.6 copy-start.10
  25.9 0.6 copy-start.12
  26.5 0.6 copy-start.16
  43.5 0.6 copy-start.6
  58.5 13.2 %copy-start = (bf16[1536,1024]{1,0:T(8,128)(2,1)S(1)}, bf16[1536,1024]{1,0:T(8,128)(2,1)}, u32[]{:S(2)}) copy-start(bf16[1536,1024]{1,0:T(8,128)(2,1)} %all-gather.3.cloned.1.call-done.kv_hbm.k_ref.v_ref) | copy-start | bytes 9437188
  64.4 20.3 %all-to-all-start.1 = ((bf16[4,400,128]{2,1,0:T(8,128)(2,1)}), bf16[4,400,128]{2,1,0:T(8,128)(2,1)S(1)}, u32[]{:S(2)}, u32[]{:S(2)}) async-start(bf16[4,400,128]{2,1,0:T(8,128)(2,1)} %shard_map.93), calls=%async_computation.1 | async-start | bytes 819200 | tf_op jit(solution)/shard_map/all_to_all | solution.py:368
  71.7 1.9 %copy-start.3 = (bf16[512,3072]{1,0:T(8,128)(2,1)S(1)}, bf16[512,3072]{1,0:T(8,128)(2,1)}, u32[]{:S(2)}) copy-start(bf16[512,3072]{1,0:T(8,128)(2,1)} %w_ref.1) | copy-start | bytes 9437188
  73.5 1.0 copy-start.5
  74.5 0.9 copy-start.7
  75.4 0.9 copy-start.11
  76.3 0.9 copy-start.13
  80.5 1.6 %copy-start.1 = (bf16[512,3072]{1,0:T(8,128)(2,1)}, bf16[512,3072]{1,0:T(8,128)(2,1)S(1)}, u32[]{:S(2)}) copy-start(bf16[512,3072]{1,0:T(8,128)(2,1)S(1)} %get-tuple-element.18.w_ref) | copy-start | bytes 9437188
  82.1 0.6 copy-start.8
  84.7 1.9 %copy-start.2 = (bf16[512,3072]{1,0:T(8,128)(2,1)S(1)}, bf16[512,3072]{1,0:T(8,128)(2,1)}, u32[]{:S(2)}) copy-start(bf16[512,3072]{1,0:T(8,128)(2,1)} %copy-done.1) | copy-start | bytes 9437188
  86.6 0.9 copy-start.9
  103.6 0.9 copy-start.14
  104.5 0.7 copy-start.15
  105.2 0.7 copy-start.17
Sparse Core Ops, SparseCore 0:
  9.5 48.9 all-gather.2

commit v9 on v8

--- a/solution.py
+++ b/solution.py
@@ -270,17 +270,20 @@
         out_specs=(whole(RETURNED, HD), pl.BlockSpec(memory_space=pl.ANY)),
         out_shape=(pltpu.VMEM((RETURNED, HD), bf16), pltpu.VMEM((GROUP, D), bf16)),
         scratch_shapes=[pltpu.VMEM((CAP, HD), f32), pltpu.SemaphoreType.DMA],
-        compiler_params=params(44),
+        compiler_params=params(56),
         cost_estimate=cost(CAP, KEYS + CAP),
     )(q, kv, kv, kf, vf, bias, w)
 
 
-def project_kernel(part_ref, own_ref, w_ref, out_ref):
+def project_kernel(part_hbm, own_ref, w_ref, out_ref, part_ref, sem):
+    copy = pltpu.make_async_copy(part_hbm, part_ref, sem)
+    copy.start()
     yh = lax.axis_index("yh")
 
     def part(b, rows):
         return jnp.where(yh == b, own_ref[rows, :].astype(f32), part_ref[b, rows, :].astype(f32))
 
+    copy.wait()
     stats = [part(b, slice(HEADS_HERE * CAP, RETURNED)) for b in range(NY)]
     shares = []
     for h in range(HEADS_HERE):
@@ -331,9 +334,10 @@
 def project(parts, own, w):
     return pl.pallas_call(
         project_kernel,
-        in_specs=[pl.BlockSpec(memory_space=pltpu.VMEM)] * 3,
+        in_specs=[pl.BlockSpec(memory_space=pltpu.HBM)] + [pl.BlockSpec(memory_space=pltpu.VMEM)] * 2,
         out_specs=pl.BlockSpec(memory_space=pltpu.VMEM),
         out_shape=jax.ShapeDtypeStruct((NHEAD, 16, OUT_PACKED), bf16),
+        scratch_shapes=[pltpu.VMEM((NY, RETURNED, HD), bf16), pltpu.SemaphoreType.DMA],
         compiler_params=params(24),
     )(parts, own, w)
 

time: 114 us -> 110 us (0.965)
  local copies, waits for them, and re-layouts: 16.8 us -> 5.49 us
  waiting for transfers between devices: 16.2 us -> 22 us
  Pallas kernels: 13.5 us -> 14.8 us
    unnamed x38 -> x22, local copies, waits for them, and re-layouts: 16.8 us -> 5.49 us
    all_to_all x1, waiting for transfers between devices: 1.89 us -> 7.9 us  [swap(): return lax.all_to_all(x, axis, split_axis=0, concat_axis=0, tiled=True)]
    pallas_call x1, Pallas kernels: 3.27 us -> 4.48 us  [attend_own(): pl.pallas_call(own_kernel, grid=(STEPS,), in_specs=[column(CAP), column(K...]
  transfers between devices with their start and end apart: 2 -> 2, of which waited for: 2 -> 2; matrix products, arithmetic and copies ran while one was open for 0% -> 0% of each run, Pallas kernels for 5% -> 6%
where the time goes in v9:
time: 110 us; the launch traced here: 109 us
  blocking collectives  44.8 us (41%)
  waiting for transfers between devices  22 us (20%)
  Pallas kernels  14.8 us (13%)
  between operations  13.5 us (12%)
  starting transfers between devices  7.28 us (7%)
  local copies, waits for them, and re-layouts  5.49 us (5%)
  other arithmetic  1.63 us (1%)
    all_to_all x2, blocking collectives, swap(): return lax.all_to_all(x, axis, split_axis=0, concat_axis=0, tiled=True)  28.2 us
    all_gather x1, blocking collectives, local(): queries = lax.all_gather(query, 'yh', axis=0)  16.6 us
    all_gather x1, waiting for transfers between devices, local(): lax.all_gather(jnp.concatenate([sk, sv], axis=1), ('z', 'c'), axis=0, til...  14.1 us
    all_to_all x1, waiting for transfers between devices, swap(): return lax.all_to_all(x, axis, split_axis=0, concat_axis=0, tiled=True)  7.9 us
    all_to_all x1, starting transfers between devices, swap(): return lax.all_to_all(x, axis, split_axis=0, concat_axis=0, tiled=True)  7.28 us
    pallas_call x1, Pallas kernels, attend_others(): pl.pallas_call(others_kernel, in_specs=[pl.BlockSpec(memory_space=pl.ANY)...  5.73 us
    unnamed x22, local copies, waits for them, and re-layouts  5.49 us
    pallas_call x1, Pallas kernels, attend_own(): pl.pallas_call(own_kernel, grid=(STEPS,), in_specs=[column(CAP), column(K...  4.48 us
  transfers between devices with their start and end apart: 2, of which 2 were waited for; matrix products, arithmetic and copies ran while one was open for 0% of the time, Pallas kernels for 6%

profile of v9, /device:TPU:16, one launch (start us, length us, event | category | flops | bytes accessed | tf_op | source)
XLA Modules:
  0.0 109.5 jit_solution(16388927600545226382)
XLA Ops:
  6.5 0.0 all-gather.3.cloned.1.call-start
  6.5 1.6 %pad_maximum_fusion = bf16[96,1024]{1,0:T(8,128)(2,1)} fusion(bf16[96,512]{1,0:T(8,128)(2,1)} %param.13, bf16[96,512]{1,0:T(8,128)(2,1)} %param.12), kind=kLoop, calls=%fused_computation | loop fusion | flops 393216 | bytes 393216 | tf_op jit(solution)/shard_map/concatenate | solution.py:376
  8.2 0.0 all-gather.3.cloned.1.call-update
  8.2 1.8 %shard_map.91 = bf16[8,16,1152]{2,1,0:T(8,128)(2,1)} custom-call(bf16[12,4096]{1,0:T(8,128)(2,1)} %q_ref.1, bf16[12,4096]{1,0:T(8,128)(2,1)} %k_ref.1, bf16[12,4096]{1,0:T(8,128)(2,1)} %v_ref.1), custom_call_target="tpu_custom_call" | custom-call | tf_op jit(solution)/shard_map/pallas_call | solution.py:56
  10.0 13.1 %all_to_all.15.in_ref = bf16[8,16,1152]{2,1,0:T(8,128)(2,1)S(1)} all-to-all(bf16[8,16,1152]{2,1,0:T(8,128)(2,1)} %shard_map.91), channel_id=1, replica_groups=mesh['z'=8,'yh'=4,'c'=2,'yl'=2,'x'=4] {'yl','x'}, dimensions={0} | all-to-all | bytes 589824 | tf_op jit(solution)/shard_map/all_to_all | solution.py:372
  23.2 0.7 copy-done.10
  23.8 0.7 shard_map.92
  24.5 0.0 copy-start
  24.5 0.8 copy-done
  25.3 0.0 copy-start.4
  25.3 0.6 copy-done.4
  25.9 0.0 copy-start.5
  25.9 0.6 copy-done.5
  26.6 0.0 copy-start.8
  26.6 0.6 copy-done.8
  27.2 0.0 copy-start.1
  27.2 0.6 copy-done.1
  27.8 16.6 %all-gather = bf16[384,512]{1,0:T(8,128)(2,1)} all-gather(bf16[96,512]{1,0:T(8,128)(2,1)S(1)} %get-tuple-element.13.q_ref), channel_id=2, replica_groups=mesh['z'=8,'yh'=4,'c'=2,'yl'=2,'x'=4] {'yh'}, dimensions={0}, use_global_device_ids=true | all-gather | bytes 491520 | tf_op jit(solution)/shard_map/all_gather | solution.py:378
  44.4 14.1 %all-gather.3.cloned.1.call-done.kv_hbm.k_ref.v_ref = bf16[1536,1024]{1,0:T(8,128)(2,1)} async-done(((bf16[96,1024]{1,0:T(8,128)(2,1)}), bf16[1536,1024]{1,0:T(8,128)(2,1)}) %all-gather.3.cloned.1.call-update) | async-done | bytes 3145744 | tf_op jit(solution)/shard_map/all_gather | solution.py:376
  58.5 5.7 %shard_map.93 = bf16[4,400,128]{2,1,0:T(8,128)(2,1)} custom-call(bf16[4,96,512]{2,1,0:T(8,128)(2,1)} %bitcast.3, bf16[1536,1024]{1,0:T(8,128)(2,1)} %all-gather.3.cloned.1.call-done.kv_hbm.k_ref.v_ref, bf16[1632,128]{1,0:T(8,128)(2,1)} %copy-done), custom_call_target="tpu_custom_call" | custom-call | flops 905969664 | bytes 3145728 | tf_op jit(solution)/shard_map/pallas_call | solution.py:246
  64.2 7.3 %all-to-all-start.1 = ((bf16[4,400,128]{2,1,0:T(8,128)(2,1)}), bf16[4,400,128]{2,1,0:T(8,128)(2,1)S(1)}, u32[]{:S(2)}, u32[]{:S(2)}) async-start(bf16[4,400,128]{2,1,0:T(8,128)(2,1)} %shard_map.93), calls=%async_computation.1 | async-start | bytes 819200 | tf_op jit(solution)/shard_map/all_to_all | solution.py:372
  71.5 4.5 %shard_map.94 = (bf16[400,128]{1,0:T(8,128)(2,1)S(1)}, bf16[512,3072]{1,0:T(8,128)(2,1)S(1)}) custom-call(bf16[96,512]{1,0:T(8,128)(2,1)} %copy-done.1, bf16[1536,1024]{1,0:T(8,128)(2,1)} %all-gather.3.cloned.1.call-done.kv_hbm.k_ref.v_ref, bf16[1536,1024]{1,0:T(8,128)(2,1)} %all-gather.3.cloned.1.call-done.kv_hbm.k_ref.v_ref, bf16[96,512]{1,0:T(8,128)(2,1)} %copy-done.4, ...), custom_call_target="tpu_custom_call" | custom-call | flops 320864256 | bytes 3342336 | tf_op jit(solution)/shard_map/pallas_call | solution.py:263
  76.0 0.0 copy-start.2
  76.0 0.6 copy-done.2
  76.6 7.9 %all-to-all-done.1.part_hbm = bf16[4,400,128]{2,1,0:T(8,128)(2,1)S(1)} async-done(((bf16[4,400,128]{2,1,0:T(8,128)(2,1)}), bf16[4,400,128]{2,1,0:T(8,128)(2,1)S(1)}, u32[]{:S(2)}, u32[]{:S(2)}) %all-to-all-start.1) | async-done | bytes 409632 | tf_op jit(solution)/shard_map/all_to_all | solution.py:372
  84.5 0.9 copy-done.3
  85.4 1.3 %shard_map.95 = bf16[8,16,2304]{2,1,0:T(8,128)(2,1)S(1)} custom-call(bf16[4,400,128]{2,1,0:T(8,128)(2,1)S(1)} %all-to-all-done.1.part_hbm, bf16[400,128]{1,0:T(8,128)(2,1)S(1)} %copy-done.3, bf16[512,3072]{1,0:T(8,128)(2,1)S(1)} %get-tuple-element.18.w_ref), custom_call_target="tpu_custom_call" | custom-call | tf_op jit(solution)/shard_map/pallas_call | solution.py:335
  86.8 15.1 %all_to_all.16.in_ref = bf16[8,16,2304]{2,1,0:T(8,128)(2,1)S(1)} all-to-all(bf16[8,16,2304]{2,1,0:T(8,128)(2,1)S(1)} %shard_map.95), channel_id=1, replica_groups=mesh['z'=8,'yh'=4,'c'=2,'yl'=2,'x'=4] {'yl','x'}, dimensions={0} | all-to-all | bytes 1179648 | tf_op jit(solution)/shard_map/all_to_all | solution.py:372
  101.9 0.0 copy-done.6
  101.9 0.0 copy-done.7
  101.9 0.0 copy-done.9
  101.9 0.8 shard_map.96
  (5 shorter events, 0.0 us)
Async XLA Ops:
  6.5 51.9 %all-gather.3.cloned.1.call-start = ((), (), s32[]{:S(2)}) async-start(), calls=%async_computation.3 | async-start | bytes 3342336 | tf_op jit(solution)/shard_map/all_gather | solution.py:376
  23.2 0.7 copy-start.10
  24.5 0.8 copy-start
  25.3 0.7 copy-start.4
  25.9 0.6 copy-start.5
  26.6 0.6 copy-start.8
  27.2 0.6 copy-start.1
  64.2 20.3 %all-to-all-start.1 = ((bf16[4,400,128]{2,1,0:T(8,128)(2,1)}), bf16[4,400,128]{2,1,0:T(8,128)(2,1)S(1)}, u32[]{:S(2)}, u32[]{:S(2)}) async-start(bf16[4,400,128]{2,1,0:T(8,128)(2,1)} %shard_map.93), calls=%async_computation.1 | async-start | bytes 819200 | tf_op jit(solution)/shard_map/all_to_all | solution.py:372
  76.0 0.6 copy-start.2
  84.5 0.9 copy-start.3
  85.4 16.4 %copy-start.6 = (bf16[12,3072]{1,0:T(8,128)(2,1)S(1)}, bf16[12,3072]{1,0:T(8,128)(2,1)}, u32[]{:S(2)}) copy-start(bf16[12,3072]{1,0:T(8,128)(2,1)} %hidden_ref.1) | copy-start | bytes 221188
  85.4 16.4 %copy-start.7 = (f32[3072]{0:T(1024)S(1)}, f32[3072]{0:T(1024)}, u32[]{:S(2)}) copy-start(f32[3072]{0:T(1024)} %param.16) | copy-start | bytes 36868
  85.4 16.4 %copy-start.9 = (f32[16,128]{1,0:T(8,128)S(1)}, f32[16,128]{1,0:T(8,128)}, u32[]{:S(2)}) copy-start(f32[16,128]{1,0:T(8,128)} %copy-done.8) | copy-start | bytes 24580
Sparse Core Ops, SparseCore 0:
  9.5 48.9 all-gather.2

commit v10 on v8

--- a/solution.py
+++ b/solution.py
@@ -268,19 +268,27 @@
             pl.BlockSpec(memory_space=pltpu.HBM),
         ],
         out_specs=(whole(RETURNED, HD), pl.BlockSpec(memory_space=pl.ANY)),
-        out_shape=(pltpu.VMEM((RETURNED, HD), bf16), pltpu.VMEM((GROUP, D), bf16)),
+        out_shape=(pltpu.HBM((RETURNED, HD), bf16), pltpu.VMEM((GROUP, D), bf16)),
         scratch_shapes=[pltpu.VMEM((CAP, HD), f32), pltpu.SemaphoreType.DMA],
-        compiler_params=params(44),
+        compiler_params=params(56),
         cost_estimate=cost(CAP, KEYS + CAP),
     )(q, kv, kv, kf, vf, bias, w)
 
 
-def project_kernel(part_ref, own_ref, w_ref, out_ref):
+def project_kernel(part_hbm, own_hbm, w_ref, out_ref, part_ref, own_ref, sems):
+    copies = [
+        pltpu.make_async_copy(part_hbm, part_ref, sems.at[0]),
+        pltpu.make_async_copy(own_hbm, own_ref, sems.at[1]),
+    ]
+    for copy in copies:
+        copy.start()
     yh = lax.axis_index("yh")
 
     def part(b, rows):
         return jnp.where(yh == b, own_ref[rows, :].astype(f32), part_ref[b, rows, :].astype(f32))
 
+    for copy in copies:
+        copy.wait()
     stats = [part(b, slice(HEADS_HERE * CAP, RETURNED)) for b in range(NY)]
     shares = []
     for h in range(HEADS_HERE):
@@ -331,9 +339,13 @@
 def project(parts, own, w):
     return pl.pallas_call(
         project_kernel,
-        in_specs=[pl.BlockSpec(memory_space=pltpu.VMEM)] * 3,
+        in_specs=[pl.BlockSpec(memory_space=pltpu.HBM)] * 2 + [pl.BlockSpec(memory_space=pltpu.VMEM)],
         out_specs=pl.BlockSpec(memory_space=pltpu.VMEM),
         out_shape=jax.ShapeDtypeStruct((NHEAD, 16, OUT_PACKED), bf16),
+        scratch_shapes=[
+            pltpu.VMEM((NY, RETURNED, HD), bf16), pltpu.VMEM((RETURNED, HD), bf16),
+            pltpu.SemaphoreType.DMA((2,)),
+        ],
         compiler_params=params(24),
     )(parts, own, w)
 

time: 114 us -> 110 us (0.965)
  local copies, waits for them, and re-layouts: 16.8 us -> 4.84 us
  waiting for transfers between devices: 16.2 us -> 22.1 us
  Pallas kernels: 13.5 us -> 15.6 us
    unnamed x38 -> x20, local copies, waits for them, and re-layouts: 16.8 us -> 4.84 us
    all_to_all x1, waiting for transfers between devices: 1.89 us -> 7.92 us  [swap(): return lax.all_to_all(x, axis, split_axis=0, concat_axis=0, tiled=True)]
    pallas_call x1, Pallas kernels: 3.27 us -> 5.09 us  [attend_own(): pl.pallas_call(own_kernel, grid=(STEPS,), in_specs=[column(CAP), column(K...]
  transfers between devices with their start and end apart: 2 -> 2, of which waited for: 2 -> 2; matrix products, arithmetic and copies ran while one was open for 0% -> 0% of each run, Pallas kernels for 5% -> 7%
where the time goes in v10:
time: 110 us
  blocking collectives  44.8 us (41%)
  waiting for transfers between devices  22.1 us (20%)
  Pallas kernels  15.6 us (14%)
  between operations  13.4 us (12%)
  starting transfers between devices  7.28 us (7%)
  local copies, waits for them, and re-layouts  4.84 us (4%)
  other arithmetic  1.62 us (1%)
    all_to_all x2, blocking collectives, swap(): return lax.all_to_all(x, axis, split_axis=0, concat_axis=0, tiled=True)  28.2 us
    all_gather x1, blocking collectives, local(): queries = lax.all_gather(query, 'yh', axis=0)  16.6 us
    all_gather x1, waiting for transfers between devices, local(): lax.all_gather(jnp.concatenate([sk, sv], axis=1), ('z', 'c'), axis=0, til...  14.1 us
    all_to_all x1, waiting for transfers between devices, swap(): return lax.all_to_all(x, axis, split_axis=0, concat_axis=0, tiled=True)  7.92 us
    all_to_all x1, starting transfers between devices, swap(): return lax.all_to_all(x, axis, split_axis=0, concat_axis=0, tiled=True)  7.28 us
    pallas_call x1, Pallas kernels, attend_others(): pl.pallas_call(others_kernel, in_specs=[pl.BlockSpec(memory_space=pl.ANY)...  5.72 us
    pallas_call x1, Pallas kernels, attend_own(): pl.pallas_call(own_kernel, grid=(STEPS,), in_specs=[column(CAP), column(K...  5.09 us
    unnamed x20, local copies, waits for them, and re-layouts  4.84 us
  transfers between devices with their start and end apart: 2, of which 2 were waited for; matrix products, arithmetic and copies ran while one was open for 0% of the time, Pallas kernels for 7%

profile of v10, /device:TPU:16, one launch (start us, length us, event | category | flops | bytes accessed | tf_op | source)
XLA Modules:
  0.0 109.6 jit_solution(16004716487424851189)
XLA Ops:
  6.5 0.0 all-gather.3.cloned.1.call-start
  6.5 1.6 %pad_maximum_fusion = bf16[96,1024]{1,0:T(8,128)(2,1)} fusion(bf16[96,512]{1,0:T(8,128)(2,1)} %param.13, bf16[96,512]{1,0:T(8,128)(2,1)} %param.12), kind=kLoop, calls=%fused_computation | loop fusion | flops 393216 | bytes 393216 | tf_op jit(solution)/shard_map/concatenate | solution.py:384
  8.2 0.0 all-gather.3.cloned.1.call-update
  8.2 1.8 %shard_map.91 = bf16[8,16,1152]{2,1,0:T(8,128)(2,1)} custom-call(bf16[12,4096]{1,0:T(8,128)(2,1)} %q_ref.1, bf16[12,4096]{1,0:T(8,128)(2,1)} %k_ref.1, bf16[12,4096]{1,0:T(8,128)(2,1)} %v_ref.1), custom_call_target="tpu_custom_call" | custom-call | tf_op jit(solution)/shard_map/pallas_call | solution.py:56
  10.0 13.1 %all_to_all.15.in_ref = bf16[8,16,1152]{2,1,0:T(8,128)(2,1)S(1)} all-to-all(bf16[8,16,1152]{2,1,0:T(8,128)(2,1)} %shard_map.91), channel_id=1, replica_groups=mesh['z'=8,'yh'=4,'c'=2,'yl'=2,'x'=4] {'yl','x'}, dimensions={0} | all-to-all | bytes 589824 | tf_op jit(solution)/shard_map/all_to_all | solution.py:380
  23.2 0.0 copy-start.9
  23.2 0.7 copy-done.9
  23.8 0.7 shard_map.92
  24.5 0.0 copy-start
  24.5 0.8 copy-done
  25.3 0.6 copy-done.3
  25.9 0.0 copy-start.4
  25.9 0.6 copy-done.4
  26.5 0.0 copy-start.7
  26.5 0.6 copy-done.7
  27.1 0.0 copy-start.1
  27.1 0.6 copy-done.1
  27.8 16.6 %all-gather = bf16[384,512]{1,0:T(8,128)(2,1)} all-gather(bf16[96,512]{1,0:T(8,128)(2,1)S(1)} %get-tuple-element.13.q_ref), channel_id=2, replica_groups=mesh['z'=8,'yh'=4,'c'=2,'yl'=2,'x'=4] {'yh'}, dimensions={0}, use_global_device_ids=true | all-gather | bytes 491520 | tf_op jit(solution)/shard_map/all_gather | solution.py:386
  44.4 14.1 %all-gather.3.cloned.1.call-done.kv_hbm.k_ref.v_ref = bf16[1536,1024]{1,0:T(8,128)(2,1)} async-done(((bf16[96,1024]{1,0:T(8,128)(2,1)}), bf16[1536,1024]{1,0:T(8,128)(2,1)}) %all-gather.3.cloned.1.call-update) | async-done | bytes 3145744 | tf_op jit(solution)/shard_map/all_gather | solution.py:384
  58.5 5.7 %shard_map.93 = bf16[4,400,128]{2,1,0:T(8,128)(2,1)} custom-call(bf16[4,96,512]{2,1,0:T(8,128)(2,1)} %bitcast.3, bf16[1536,1024]{1,0:T(8,128)(2,1)} %all-gather.3.cloned.1.call-done.kv_hbm.k_ref.v_ref, bf16[1632,128]{1,0:T(8,128)(2,1)} %copy-done), custom_call_target="tpu_custom_call" | custom-call | flops 905969664 | bytes 3145728 | tf_op jit(solution)/shard_map/pallas_call | solution.py:246
  64.2 7.3 %all-to-all-start.1 = ((bf16[4,400,128]{2,1,0:T(8,128)(2,1)}), bf16[4,400,128]{2,1,0:T(8,128)(2,1)S(1)}, u32[]{:S(2)}, u32[]{:S(2)}) async-start(bf16[4,400,128]{2,1,0:T(8,128)(2,1)} %shard_map.93), calls=%async_computation.1 | async-start | bytes 819200 | tf_op jit(solution)/shard_map/all_to_all | solution.py:380
  71.5 5.1 %shard_map.94 = (bf16[400,128]{1,0:T(8,128)(2,1)}, bf16[512,3072]{1,0:T(8,128)(2,1)S(1)}) custom-call(bf16[96,512]{1,0:T(8,128)(2,1)} %copy-done.1, bf16[1536,1024]{1,0:T(8,128)(2,1)} %all-gather.3.cloned.1.call-done.kv_hbm.k_ref.v_ref, bf16[1536,1024]{1,0:T(8,128)(2,1)} %all-gather.3.cloned.1.call-done.kv_hbm.k_ref.v_ref, bf16[96,512]{1,0:T(8,128)(2,1)} %copy-done.3, ...), custom_call_target="tpu_custom_call" | custom-call | flops 320864256 | bytes 3342336 | tf_op jit(solution)/shard_map/pallas_call | solution.py:263
  76.6 7.9 %all-to-all-done.1.part_hbm = bf16[4,400,128]{2,1,0:T(8,128)(2,1)S(1)} async-done(((bf16[4,400,128]{2,1,0:T(8,128)(2,1)}), bf16[4,400,128]{2,1,0:T(8,128)(2,1)S(1)}, u32[]{:S(2)}, u32[]{:S(2)}) %all-to-all-start.1) | async-done | bytes 409632 | tf_op jit(solution)/shard_map/all_to_all | solution.py:380
  84.5 0.0 copy-start.2
  84.5 0.9 copy-done.2
  85.4 0.0 copy-start.5
  85.4 1.5 %shard_map.95 = bf16[8,16,2304]{2,1,0:T(8,128)(2,1)S(1)} custom-call(bf16[4,400,128]{2,1,0:T(8,128)(2,1)S(1)} %all-to-all-done.1.part_hbm, bf16[400,128]{1,0:T(8,128)(2,1)S(1)} %copy-done.2, bf16[512,3072]{1,0:T(8,128)(2,1)S(1)} %get-tuple-element.18.w_ref), custom_call_target="tpu_custom_call" | custom-call | tf_op jit(solution)/shard_map/pallas_call | solution.py:340
  86.9 15.1 %all_to_all.16.in_ref = bf16[8,16,2304]{2,1,0:T(8,128)(2,1)S(1)} all-to-all(bf16[8,16,2304]{2,1,0:T(8,128)(2,1)S(1)} %shard_map.95), channel_id=1, replica_groups=mesh['z'=8,'yh'=4,'c'=2,'yl'=2,'x'=4] {'yl','x'}, dimensions={0} | all-to-all | bytes 1179648 | tf_op jit(solution)/shard_map/all_to_all | solution.py:380
  102.0 0.0 copy-done.5
  102.0 0.0 copy-done.6
  102.0 0.0 copy-done.8
  102.0 0.8 shard_map.96
  (3 shorter events, 0.0 us)
Async XLA Ops:
  6.5 51.9 %all-gather.3.cloned.1.call-start = ((), (), s32[]{:S(2)}) async-start(), calls=%async_computation.3 | async-start | bytes 3342336 | tf_op jit(solution)/shard_map/all_gather | solution.py:384
  23.2 0.7 copy-start.9
  24.5 0.8 copy-start
  25.3 0.6 copy-start.3
  25.9 0.6 copy-start.4
  26.5 0.6 copy-start.7
  27.1 0.6 copy-start.1
  64.2 20.3 %all-to-all-start.1 = ((bf16[4,400,128]{2,1,0:T(8,128)(2,1)}), bf16[4,400,128]{2,1,0:T(8,128)(2,1)S(1)}, u32[]{:S(2)}, u32[]{:S(2)}) async-start(bf16[4,400,128]{2,1,0:T(8,128)(2,1)} %shard_map.93), calls=%async_computation.1 | async-start | bytes 819200 | tf_op jit(solution)/shard_map/all_to_all | solution.py:380
  84.5 0.9 copy-start.2
  85.4 16.6 %copy-start.5 = (bf16[12,3072]{1,0:T(8,128)(2,1)S(1)}, bf16[12,3072]{1,0:T(8,128)(2,1)}, u32[]{:S(2)}) copy-start(bf16[12,3072]{1,0:T(8,128)(2,1)} %hidden_ref.1) | copy-start | bytes 221188
  85.4 16.6 %copy-start.6 = (f32[3072]{0:T(1024)S(1)}, f32[3072]{0:T(1024)}, u32[]{:S(2)}) copy-start(f32[3072]{0:T(1024)} %param.16) | copy-start | bytes 36868
  85.4 16.6 %copy-start.8 = (f32[16,128]{1,0:T(8,128)S(1)}, f32[16,128]{1,0:T(8,128)}, u32[]{:S(2)}) copy-start(f32[16,128]{1,0:T(8,128)} %copy-done.7) | copy-start | bytes 24580
Sparse Core Ops, SparseCore 0:
  9.5 48.9 all-gather.2

commit v11 on v10

--- a/solution.py
+++ b/solution.py
@@ -346,7 +346,7 @@
             pltpu.VMEM((NY, RETURNED, HD), bf16), pltpu.VMEM((RETURNED, HD), bf16),
             pltpu.SemaphoreType.DMA((2,)),
         ],
-        compiler_params=params(24),
+        compiler_params=params(58),
     )(parts, own, w)
 
 

time: 110 us -> 114 us (1.036)
  Pallas kernels: 15.6 us -> 19 us
    pallas_call x1, Pallas kernels: 1.46 us -> 4.84 us  [project(): pl.pallas_call(project_kernel, in_specs=[pl.BlockSpec(memory_space=pltpu....]
    all_to_all x1, waiting for transfers between devices: 7.92 us -> 6.26 us  [swap(): return lax.all_to_all(x, axis, split_axis=0, concat_axis=0, tiled=True)]
    all_gather x1, waiting for transfers between devices: 14.1 us -> 15.6 us  [local(): lax.all_gather(jnp.concatenate([sk, sv], axis=1), ('z', 'c'), axis=0, til...]
    unnamed x20 -> x18, local copies, waits for them, and re-layouts: 4.84 us -> 5.11 us
where the time goes in v11:
time: 114 us; the launch traced here: 113 us
  blocking collectives  44.8 us (39%)
  waiting for transfers between devices  21.9 us (19%)
  Pallas kernels  19 us (17%)
  between operations  13.4 us (12%)
  starting transfers between devices  7.24 us (6%)
  local copies, waits for them, and re-layouts  5.11 us (4%)
  other arithmetic  1.62 us (1%)
    all_to_all x2, blocking collectives, swap(): return lax.all_to_all(x, axis, split_axis=0, concat_axis=0, tiled=True)  28.4 us
    all_gather x1, blocking collectives, local(): queries = lax.all_gather(query, 'yh', axis=0)  16.4 us
    all_gather x1, waiting for transfers between devices, local(): lax.all_gather(jnp.concatenate([sk, sv], axis=1), ('z', 'c'), axis=0, til...  15.6 us
    all_to_all x1, starting transfers between devices, swap(): return lax.all_to_all(x, axis, split_axis=0, concat_axis=0, tiled=True)  7.24 us
    all_to_all x1, waiting for transfers between devices, swap(): return lax.all_to_all(x, axis, split_axis=0, concat_axis=0, tiled=True)  6.26 us
    pallas_call x1, Pallas kernels, attend_others(): pl.pallas_call(others_kernel, in_specs=[pl.BlockSpec(memory_space=pl.ANY)...  5.73 us
    pallas_call x1, Pallas kernels, attend_own(): pl.pallas_call(own_kernel, grid=(STEPS,), in_specs=[column(CAP), column(K...  5.12 us
    unnamed x18, local copies, waits for them, and re-layouts  5.11 us
  transfers between devices with their start and end apart: 2, of which 2 were waited for; matrix products, arithmetic and copies ran while one was open for 0% of the time, Pallas kernels for 7%

profile of v11, /device:TPU:16, one launch (start us, length us, event | category | flops | bytes accessed | tf_op | source)
XLA Modules:
  0.0 113.0 jit_solution(10166555878165534725)
XLA Ops:
  6.5 0.0 all-gather.3.cloned.1.call-start
  6.5 1.6 %pad_maximum_fusion = bf16[96,1024]{1,0:T(8,128)(2,1)} fusion(bf16[96,512]{1,0:T(8,128)(2,1)} %param.13, bf16[96,512]{1,0:T(8,128)(2,1)} %param.12), kind=kLoop, calls=%fused_computation | loop fusion | flops 393216 | bytes 393216 | tf_op jit(solution)/shard_map/concatenate | solution.py:384
  8.2 0.0 all-gather.3.cloned.1.call-update
  8.2 1.8 %shard_map.91 = bf16[8,16,1152]{2,1,0:T(8,128)(2,1)} custom-call(bf16[12,4096]{1,0:T(8,128)(2,1)} %q_ref.1, bf16[12,4096]{1,0:T(8,128)(2,1)} %k_ref.1, bf16[12,4096]{1,0:T(8,128)(2,1)} %v_ref.1), custom_call_target="tpu_custom_call" | custom-call | tf_op jit(solution)/shard_map/pallas_call | solution.py:56
  10.0 13.1 %all_to_all.15.in_ref = bf16[8,16,1152]{2,1,0:T(8,128)(2,1)S(1)} all-to-all(bf16[8,16,1152]{2,1,0:T(8,128)(2,1)} %shard_map.91), channel_id=1, replica_groups=mesh['z'=8,'yh'=4,'c'=2,'yl'=2,'x'=4] {'yl','x'}, dimensions={0} | all-to-all | bytes 589824 | tf_op jit(solution)/shard_map/all_to_all | solution.py:380
  23.2 0.0 copy-start.7
  23.2 0.7 copy-done.7
  23.8 0.7 shard_map.92
  24.5 0.0 copy-start.1
  24.5 0.8 copy-done.1
  25.2 0.0 copy-start.3
  25.2 0.6 copy-done.3
  25.9 0.0 copy-start.4
  25.9 0.6 copy-done.4
  26.5 0.0 copy-start.2
  26.5 16.4 %all-gather = bf16[384,512]{1,0:T(8,128)(2,1)} all-gather(bf16[96,512]{1,0:T(8,128)(2,1)S(1)} %get-tuple-element.13.q_ref), channel_id=2, replica_groups=mesh['z'=8,'yh'=4,'c'=2,'yl'=2,'x'=4] {'yh'}, dimensions={0}, use_global_device_ids=true | all-gather | bytes 491520 | tf_op jit(solution)/shard_map/all_gather | solution.py:386
  42.9 15.6 %all-gather.3.cloned.1.call-done.kv_hbm.k_ref.v_ref = bf16[1536,1024]{1,0:T(8,128)(2,1)} async-done(((bf16[96,1024]{1,0:T(8,128)(2,1)}), bf16[1536,1024]{1,0:T(8,128)(2,1)}) %all-gather.3.cloned.1.call-update) | async-done | bytes 3145744 | tf_op jit(solution)/shard_map/all_gather | solution.py:384
  58.5 5.7 %shard_map.93 = bf16[4,400,128]{2,1,0:T(8,128)(2,1)} custom-call(bf16[4,96,512]{2,1,0:T(8,128)(2,1)} %bitcast.3, bf16[1536,1024]{1,0:T(8,128)(2,1)} %all-gather.3.cloned.1.call-done.kv_hbm.k_ref.v_ref, bf16[1632,128]{1,0:T(8,128)(2,1)} %copy-done.1), custom_call_target="tpu_custom_call" | custom-call | flops 905969664 | bytes 3145728 | tf_op jit(solution)/shard_map/pallas_call | solution.py:246
  64.2 7.2 %all-to-all-start.1 = ((bf16[4,400,128]{2,1,0:T(8,128)(2,1)}), bf16[4,400,128]{2,1,0:T(8,128)(2,1)S(1)}, u32[]{:S(2)}, u32[]{:S(2)}) async-start(bf16[4,400,128]{2,1,0:T(8,128)(2,1)} %shard_map.93), calls=%async_computation.1 | async-start | bytes 819200 | tf_op jit(solution)/shard_map/all_to_all | solution.py:380
  71.5 0.0 copy-done.2
  71.5 5.1 %shard_map.94 = (bf16[400,128]{1,0:T(8,128)(2,1)}, bf16[512,3072]{1,0:T(8,128)(2,1)S(1)}) custom-call(bf16[96,512]{1,0:T(8,128)(2,1)} %copy-done.2, bf16[1536,1024]{1,0:T(8,128)(2,1)} %all-gather.3.cloned.1.call-done.kv_hbm.k_ref.v_ref, bf16[1536,1024]{1,0:T(8,128)(2,1)} %all-gather.3.cloned.1.call-done.kv_hbm.k_ref.v_ref, bf16[96,512]{1,0:T(8,128)(2,1)} %copy-done.3, ...), custom_call_target="tpu_custom_call" | custom-call | flops 320864256 | bytes 3342336 | tf_op jit(solution)/shard_map/pallas_call | solution.py:263
  76.6 0.0 copy-start
  76.6 1.6 %copy-done = bf16[512,3072]{1,0:T(8,128)(2,1)} copy-done((bf16[512,3072]{1,0:T(8,128)(2,1)}, bf16[512,3072]{1,0:T(8,128)(2,1)S(1)}, u32[]{:S(2)}) %copy-start) | copy-done | bytes 3145752
  78.2 0.0 copy-start.5
  78.2 0.0 copy-start.6
  78.2 6.3 %all-to-all-done.1.part_hbm = bf16[4,400,128]{2,1,0:T(8,128)(2,1)S(1)} async-done(((bf16[4,400,128]{2,1,0:T(8,128)(2,1)}), bf16[4,400,128]{2,1,0:T(8,128)(2,1)S(1)}, u32[]{:S(2)}, u32[]{:S(2)}) %all-to-all-start.1) | async-done | bytes 409632 | tf_op jit(solution)/shard_map/all_to_all | solution.py:380
  84.5 0.8 copy-done.8
  85.3 4.8 %shard_map.95 = bf16[8,16,2304]{2,1,0:T(8,128)(2,1)} custom-call(bf16[4,400,128]{2,1,0:T(8,128)(2,1)} %copy-done.8, bf16[400,128]{1,0:T(8,128)(2,1)} %get-tuple-element.17.own_hbm, bf16[512,3072]{1,0:T(8,128)(2,1)} %copy-done), custom_call_target="tpu_custom_call" | custom-call | tf_op jit(solution)/shard_map/pallas_call | solution.py:340
  90.1 15.3 %all_to_all.16.in_ref = bf16[8,16,2304]{2,1,0:T(8,128)(2,1)S(1)} all-to-all(bf16[8,16,2304]{2,1,0:T(8,128)(2,1)} %shard_map.95), channel_id=1, replica_groups=mesh['z'=8,'yh'=4,'c'=2,'yl'=2,'x'=4] {'yl','x'}, dimensions={0} | all-to-all | bytes 1179648 | tf_op jit(solution)/shard_map/all_to_all | solution.py:380
  105.4 0.0 copy-done.5
  105.4 0.0 copy-done.6
  105.4 0.8 shard_map.96
  (1 shorter events, 0.0 us)
Async XLA Ops:
  6.5 52.0 %all-gather.3.cloned.1.call-start = ((), (), s32[]{:S(2)}) async-start(), calls=%async_computation.3 | async-start | bytes 3342336 | tf_op jit(solution)/shard_map/all_gather | solution.py:384
  23.2 0.7 copy-start.7
  24.5 0.8 copy-start.1
  25.2 0.6 copy-start.3
  25.9 0.7 copy-start.4
  26.5 44.9 %copy-start.2 = (bf16[96,512]{1,0:T(8,128)(2,1)}, bf16[96,512]{1,0:T(8,128)(2,1)S(1)}, u32[]{:S(2)}) copy-start(bf16[96,512]{1,0:T(8,128)(2,1)S(1)} %get-tuple-element.13.q_ref) | copy-start | bytes 294916
  64.2 20.3 %all-to-all-start.1 = ((bf16[4,400,128]{2,1,0:T(8,128)(2,1)}), bf16[4,400,128]{2,1,0:T(8,128)(2,1)S(1)}, u32[]{:S(2)}, u32[]{:S(2)}) async-start(bf16[4,400,128]{2,1,0:T(8,128)(2,1)} %shard_map.93), calls=%async_computation.1 | async-start | bytes 819200 | tf_op jit(solution)/shard_map/all_to_all | solution.py:380
  76.6 1.6 %copy-start = (bf16[512,3072]{1,0:T(8,128)(2,1)}, bf16[512,3072]{1,0:T(8,128)(2,1)S(1)}, u32[]{:S(2)}) copy-start(bf16[512,3072]{1,0:T(8,128)(2,1)S(1)} %get-tuple-element.18.w_ref) | copy-start | bytes 9437188
  78.2 27.2 %copy-start.5 = (bf16[12,3072]{1,0:T(8,128)(2,1)S(1)}, bf16[12,3072]{1,0:T(8,128)(2,1)}, u32[]{:S(2)}) copy-start(bf16[12,3072]{1,0:T(8,128)(2,1)} %hidden_ref.1) | copy-start | bytes 221188
  78.2 27.2 %copy-start.6 = (f32[3072]{0:T(1024)S(1)}, f32[3072]{0:T(1024)}, u32[]{:S(2)}) copy-start(f32[3072]{0:T(1024)} %param.16) | copy-start | bytes 36868
  84.5 0.8 copy-start.8
Sparse Core Ops, SparseCore 0:
  9.5 48.9 all-gather.2
